TPU v7x, 128 devices: a whole 4x4x4 slice. The times are simulated.
128 devices in a mesh: dp: 4 (over z), head: 4 (over y_hi, core), blk: 8 (over y_lo, x).
Axes of the slice: x: 4, y: 4 (y_hi: 2, y_lo: 2; y = y_hi * 2 + y_lo), z: 4, core: 2. Of those that a mesh axis runs over, the one named last changes fastest.
Arguments:
- tokens: bfloat16 [16384, 2048], P(('dp', 'head', 'blk')), may hold values from -6 to 6
- segment_ids: int32 [4, 4096], P('dp'), may hold values from 0 to 9, never falling along the last dimension, each value on 1 to 2000 neighbouring positions
- valid_mask: int32 [4, 4096], P('dp'), may hold values 0 or 1
- routes: int32 [16384, 8], P(('dp', 'head', 'blk')), may hold values from 0 to 63, all different within a row; in each aligned block of 128 rows (0 to 127, 128 to 255, ...) at most 24 rows name the same one
- attn_gain: float32 [2048], replicated, may hold values from 0.5 to 1.5
- w_query: bfloat16 [2048, 2048], P(('dp', 'blk'), 'head'), may hold values from -0.125 to 0.125
- w_key: bfloat16 [2048, 2048], P(('dp', 'blk'), 'head'), may hold values from -0.125 to 0.125
- w_value: bfloat16 [2048, 2048], P(('dp', 'blk'), 'head'), may hold values from -0.125 to 0.125
- w_out: bfloat16 [2048, 2048], P(('dp', 'blk'), 'head'), may hold values from -2 to 2
- query_gain: float32 [128], replicated, may hold values from 0.5 to 1.5
- key_gain: float32 [128], replicated, may hold values from 0.5 to 1.5
- ffn_gain: float32 [2048], replicated, may hold values from 0.5 to 1.5
- router: bfloat16 [2048, 64], replicated, may hold values from -0.0625 to 0.0625
- expert_in: bfloat16 [2048, 64, 2048], P('dp', ('head', 'blk')), may hold values from -0.125 to 0.125
- expert_out: bfloat16 [2048, 64, 1024], P('dp', ('head', 'blk')), may hold values from -1 to 1
- cotangent: bfloat16 [16384, 2048], P(('dp', 'head', 'blk')), may hold values from -6 to 6
Outputs:
- output: bfloat16 [16384, 2048], P(('dp', 'head', 'blk'))
- input_grad: float32 [16384, 2048], P(('dp', 'head', 'blk'))
- attn_gain_grad: float32 [2048], replicated
- w_query_grad: float32 [2048, 2048], P(('dp', 'blk'), 'head')
- w_key_grad: float32 [2048, 2048], P(('dp', 'blk'), 'head')
- w_value_grad: float32 [2048, 2048], P(('dp', 'blk'), 'head')
- w_out_grad: float32 [2048, 2048], P(('dp', 'blk'), 'head')
- query_gain_grad: float32 [128], replicated
- key_gain_grad: float32 [128], replicated
- ffn_gain_grad: float32 [2048], replicated
- router_grad: float32 [2048, 64], replicated
- expert_in_grad: float32 [2048, 64, 2048], P('dp', ('head', 'blk'))
- expert_out_grad: float32 [2048, 64, 1024], P('dp', ('head', 'blk'))
Inputs may be any that keep to these rules, and one draw needn't show every extreme that they name: `routes`: each row names 8 different experts. In each aligned block of 128 rows (the rows of one device) no expert is named by more than 24 rows, a bound that some block reaches. `segment_ids`: segment numbers never fall along a sequence; a document has at most 2000 tokens, and one has exactly that many.
All inputs are finite; a program needn't handle non-finite values. No bound on the sum of `valid_mask` on one device may be relied on, other than what follows from the above.
Results may differ from a plain program's by a relative error of at most 0.033.
Values may be sent and summed in bfloat16 or wider, within the bound.
A program may use at most 256 MiB of HBM per device.

v0:
```python
import math

import jax
import jax.numpy as jnp
from jax import lax
from jax.sharding import PartitionSpec as P

HEADS = 16
HD = 128
FF = 1024
TOPK = 8
EXP_DEV = 2


epsilon = 1e-06
rope_base = 50000.0
masked_score = -1e30
highest = lax.Precision.HIGHEST


def rms_rows(values):
    return lax.rsqrt(jnp.mean(values * values, axis=-1, keepdims=True) + epsilon)


def rms_back(values, inverse, grad_scaled):
    inner_mean = jnp.mean(grad_scaled * values, axis=-1, keepdims=True)
    return inverse * grad_scaled - values * inverse * inverse * inverse * inner_mean


def rotary(values, positions, turning):
    half_dim = values.shape[-1] // 2
    frequency = rope_base ** (-jnp.arange(half_dim, dtype=jnp.float32) / half_dim)
    angles = positions.astype(jnp.float32)[:, None] * frequency[None, :]
    cosine = jnp.cos(angles)[:, None, :]
    sine_part = turning * jnp.sin(angles)[:, None, :]
    first_half = values[..., :half_dim]
    second = values[..., half_dim:]
    return jnp.concatenate(
        [first_half * cosine - second * sine_part, second * cosine + first_half * sine_part],
        axis=-1,
    )


def gather_rows(values):
    return lax.all_gather(values, "head", axis=0, tiled=True)


def sum_rows(values):
    return lax.psum_scatter(
        values.astype(jnp.bfloat16), "head", scatter_dimension=0, tiled=True
    ).astype(jnp.float32)


def to_experts(buffer):
    return lax.all_to_all(buffer, ("head", "blk"), split_axis=1, concat_axis=1, tiled=True)


def from_experts(buffer):
    return lax.all_to_all(buffer, ("head", "blk"), split_axis=1, concat_axis=1, tiled=True)


def on_device(
    tokens,
    segment_ids,
    valid_mask,
    routes,
    attn_gain,
    w_query,
    w_key,
    w_value,
    w_out,
    query_gain,
    key_gain,
    ffn_gain,
    router,
    expert_in,
    expert_out,
    cotangent,
):
    head_count = lax.axis_size("head")
    block_count = lax.axis_size("blk")
    block_pos = lax.axis_index("blk")
    tok_local = tokens.shape[0]
    model_width = tokens.shape[1]
    local_heads = HEADS // head_count
    head_width = local_heads * HD
    query_count = tok_local * head_count
    seq_len = query_count * block_count
    group_count = head_count * block_count
    experts_all = EXP_DEV * group_count
    capacity = 3 * tok_local * TOPK // (2 * experts_all)
    score_scale = HD ** (-0.5)
    f32 = jnp.float32
    bf16 = jnp.bfloat16
    full_query, full_key, full_value, full_out = (
        lax.all_gather(w_query, ("dp", "blk"), axis=0, tiled=True),
        lax.all_gather(w_key, ("dp", "blk"), axis=0, tiled=True),
        lax.all_gather(w_value, ("dp", "blk"), axis=0, tiled=True),
        lax.all_gather(w_out, ("dp", "blk"), axis=0, tiled=True),
    )
    full_in, full_back = (
        lax.all_gather(expert_in, "dp", axis=0, tiled=True),
        lax.all_gather(expert_out, "dp", axis=0, tiled=True),
    )
    token_grid = jnp.arange(seq_len, dtype=jnp.int32).reshape(head_count, block_count, tok_local)
    seg_grid = segment_ids[0].reshape(head_count, block_count, tok_local)
    valid_grid = valid_mask[0].reshape(head_count, block_count, tok_local)
    query_ids = lax.dynamic_index_in_dim(token_grid, block_pos, 1, keepdims=False).reshape(-1)
    query_seg = lax.dynamic_index_in_dim(seg_grid, block_pos, 1, keepdims=False).reshape(-1)
    cycle_ids = jnp.transpose(token_grid, (1, 0, 2)).reshape(-1)
    cycle_seg = jnp.transpose(seg_grid, (1, 0, 2)).reshape(-1)
    cycle_valid = jnp.transpose(valid_grid, (1, 0, 2)).reshape(-1)
    inputs = tokens.astype(f32)
    first_inv = rms_rows(inputs)
    normed = (inputs * first_inv * attn_gain).astype(bf16)
    normed_all = gather_rows(normed)
    query_proj = jnp.dot(normed_all, full_query, preferred_element_type=f32).reshape(
        query_count, local_heads, HD
    )
    key_proj = jnp.dot(normed_all, full_key, preferred_element_type=f32).reshape(
        query_count, local_heads, HD
    )
    value_heads = (
        jnp.dot(normed_all, full_value, preferred_element_type=f32)
        .astype(bf16)
        .reshape(query_count, local_heads, HD)
    )
    query_inv = rms_rows(query_proj)
    query_unit = query_proj * query_inv
    query_heads = rotary(query_unit * query_gain, query_ids, 1.0).astype(bf16)
    key_inv = rms_rows(key_proj)
    key_unit = key_proj * key_inv
    key_heads = rotary(key_unit * key_gain, query_ids, 1.0).astype(bf16)

    def masked_scores(key_rows, first_row, block_size):
        raw = (
            jnp.einsum("qhd,khd->hqk", query_heads, key_rows, preferred_element_type=f32)
            * score_scale
        )
        key_seg = lax.dynamic_slice_in_dim(cycle_seg, first_row, block_size)
        key_valid = lax.dynamic_slice_in_dim(cycle_valid, first_row, block_size)
        key_ids = lax.dynamic_slice_in_dim(cycle_ids, first_row, block_size)
        allowed = (query_seg[:, None] == key_seg[None, :]) & (
            (key_valid[None, :] > 0) | (query_ids[:, None] == key_ids[None, :])
        )
        return jnp.where(allowed[None], raw, masked_score)

    start_state = (
        jnp.full((local_heads, query_count), masked_score, f32),
        jnp.zeros((local_heads, query_count), f32),
        jnp.zeros((query_count, local_heads, HD), f32),
    )
    key_piece = lax.all_gather(key_heads, "blk", axis=0, tiled=True)
    value_piece = lax.all_gather(value_heads, "blk", axis=0, tiled=True)
    row_span = key_piece.shape[0]
    block_size = math.gcd(512, row_span)

    def one_block(online, block_idx):
        offset = block_idx * block_size
        key_rows = lax.dynamic_slice_in_dim(key_piece, offset, block_size, 0)
        value_rows = lax.dynamic_slice_in_dim(value_piece, offset, block_size, 0)
        scores = masked_scores(key_rows, offset, block_size)
        row_peak, row_total, accum = online
        new_peak = jnp.maximum(row_peak, jnp.max(scores, axis=-1))
        factor = jnp.exp(row_peak - new_peak)
        weights = jnp.exp(scores - new_peak[..., None])
        row_total = row_total * factor + jnp.sum(weights, axis=-1)
        update = jnp.einsum(
            "hqk,khd->qhd", weights.astype(bf16), value_rows, preferred_element_type=f32
        )
        accum = accum * jnp.transpose(factor)[..., None] + update
        return ((new_peak, row_total, accum), None)

    online, _ = lax.scan(
        one_block, start_state, jnp.arange(row_span // block_size, dtype=jnp.int32)
    )
    row_peak, row_total, accum = online
    attended = accum / jnp.transpose(row_total)[..., None]
    log_total = row_peak + jnp.log(row_total)
    attended_b = attended.astype(bf16).reshape(query_count, head_width)
    branch = sum_rows(jnp.einsum("qc,mc->qm", attended_b, full_out, preferred_element_type=f32))
    middle = inputs + branch
    second_inv = rms_rows(middle)
    normed_ffn = (middle * second_inv * ffn_gain).astype(bf16)
    logits = jnp.dot(normed_ffn, router, preferred_element_type=f32)
    probabilities = jax.nn.softmax(logits, axis=-1)
    expert_ids = jnp.arange(experts_all, dtype=jnp.int32)
    chosen_hot = (routes[..., None] == expert_ids).astype(jnp.int32)
    flat_hot = chosen_hot.reshape(tok_local * TOPK, experts_all)
    slot_ids = jnp.sum(
        (jnp.cumsum(flat_hot, axis=0, dtype=jnp.int32) - flat_hot) * flat_hot,
        axis=-1,
        dtype=jnp.int32,
    ).reshape(tok_local, TOPK)
    hot_float = chosen_hot.astype(f32)
    chosen = jnp.sum(probabilities[:, None, :] * hot_float, axis=-1)
    gate_total = jnp.sum(chosen, axis=-1, keepdims=True)
    gate_weights = chosen / gate_total
    places = routes % EXP_DEV * (group_count * capacity) + routes // EXP_DEV * capacity + slot_ids
    flat_places = places.reshape(-1)
    empty_rows = jnp.zeros((experts_all * capacity, model_width), bf16)
    send_rows = empty_rows.at[flat_places].set(
        jnp.broadcast_to(normed_ffn[:, None, :], (tok_local, TOPK, model_width)).reshape(
            -1, model_width
        )
    )
    arrived = to_experts(send_rows.reshape(EXP_DEV, group_count, capacity, model_width))
    expert_rows = arrived.reshape(EXP_DEV, group_count * capacity, model_width)
    gate_up = jnp.einsum("erd,def->erf", expert_rows, full_in, preferred_element_type=f32)
    gate_part = gate_up[..., :FF]
    up_part = gate_up[..., FF:]
    sigmoid_gate = jax.nn.sigmoid(gate_part)
    silu_gate = jax.nn.silu(gate_part)
    hidden_b = (silu_gate * up_part).astype(bf16)
    expert_result = jnp.einsum(
        "erf,def->erd", hidden_b, full_back, preferred_element_type=f32
    ).astype(bf16)
    returned = from_experts(expert_result.reshape(EXP_DEV, group_count, capacity, model_width))
    picked = returned.reshape(experts_all * capacity, model_width)[places]
    picked_float = picked.astype(f32)
    mixture = jnp.sum(gate_weights[..., None] * picked_float, axis=1)
    output = (middle + mixture).astype(bf16)
    grad_out = cotangent.astype(f32)
    grad_picked = (gate_weights[..., None] * grad_out[:, None, :]).astype(bf16)
    grad_gates = jnp.sum(grad_out[:, None, :] * picked_float, axis=-1)
    send_grads = empty_rows.at[flat_places].set(grad_picked.reshape(-1, model_width))
    arrived_grads = to_experts(
        send_grads.reshape(EXP_DEV, group_count, capacity, model_width)
    ).reshape(EXP_DEV, group_count * capacity, model_width)
    grad_hidden = jnp.einsum("erd,def->erf", arrived_grads, full_back, preferred_element_type=f32)
    grad_gate = grad_hidden * up_part * sigmoid_gate * (1.0 + gate_part * (1.0 - sigmoid_gate))
    grad_up = grad_hidden * silu_gate
    grad_gate_up = jnp.concatenate([grad_gate, grad_up], axis=-1).astype(bf16)
    grad_rows = jnp.einsum(
        "erf,def->erd", grad_gate_up, full_in, preferred_element_type=f32
    ).astype(bf16)
    back_rows = from_experts(grad_rows.reshape(EXP_DEV, group_count, capacity, model_width))
    grad_routes = back_rows.reshape(experts_all * capacity, model_width)[places]
    term_in = jnp.einsum("erc,erf->cef", expert_rows, grad_gate_up, preferred_element_type=f32)
    term_back = jnp.einsum("erc,erf->cef", arrived_grads, hidden_b, preferred_element_type=f32)
    expert_grads = lax.psum_scatter(
        jnp.concatenate([term_in, term_back], axis=-1).astype(jnp.bfloat16),
        "dp",
        scatter_dimension=0,
        tiled=True,
    ).astype(jnp.float32)
    expert_in_grad = expert_grads[..., : 2 * FF]
    expert_out_grad = expert_grads[..., 2 * FF :]
    mean_grad = jnp.sum(grad_gates * gate_weights, axis=-1, keepdims=True)
    grad_chosen = (grad_gates - mean_grad) / gate_total
    grad_probs = jnp.sum(grad_chosen[..., None] * hot_float, axis=1)
    grad_logits = probabilities * (
        grad_probs - jnp.sum(probabilities * grad_probs, axis=-1, keepdims=True)
    )
    router_term = jnp.dot(normed_ffn.astype(f32).T, grad_logits, precision=highest)
    grad_ffn = jnp.sum(grad_routes.astype(f32), axis=1) + jnp.dot(
        grad_logits, router.astype(f32).T, precision=highest
    )
    ffn_gain_term = jnp.sum(grad_ffn * middle * second_inv, axis=0)
    grad_middle = grad_out + rms_back(middle, second_inv, grad_ffn * ffn_gain)
    grad_branch = grad_middle.astype(bf16)
    branch_all = gather_rows(grad_branch)
    grad_att_b = (
        jnp.dot(branch_all, full_out, preferred_element_type=f32)
        .astype(bf16)
        .reshape(query_count, local_heads, HD)
    )
    row_delta = jnp.transpose(jnp.sum(grad_att_b.astype(f32) * attended, axis=-1))
    keys_all, values_all = (
        lax.all_gather(key_heads, "blk", axis=0, tiled=True),
        lax.all_gather(value_heads, "blk", axis=0, tiled=True),
    )
    back_size = math.gcd(512, seq_len)

    def back_block(grad_query, block_idx):
        offset = block_idx * back_size
        key_rows = lax.dynamic_slice_in_dim(keys_all, offset, back_size, 0)
        value_rows = lax.dynamic_slice_in_dim(values_all, offset, back_size, 0)
        scores = masked_scores(key_rows, offset, back_size)
        probs_block = jnp.exp(scores - log_total[..., None])
        grad_probs_block = jnp.einsum(
            "qhd,khd->hqk", grad_att_b, value_rows, preferred_element_type=f32
        )
        grad_scores = (probs_block * (grad_probs_block - row_delta[..., None])).astype(bf16)
        grad_query = grad_query + jnp.einsum(
            "hqk,khd->qhd", grad_scores, key_rows, preferred_element_type=f32
        )
        grad_key_rows = jnp.einsum(
            "hqk,qhd->khd", grad_scores, query_heads, preferred_element_type=f32
        )
        grad_value_rows = jnp.einsum(
            "hqk,qhd->khd", probs_block.astype(bf16), grad_att_b, preferred_element_type=f32
        )
        return (grad_query, (grad_key_rows, grad_value_rows))

    grad_query_sum, key_parts = lax.scan(
        back_block,
        jnp.zeros((query_count, local_heads, HD), f32),
        jnp.arange(seq_len // back_size, dtype=jnp.int32),
    )
    key_terms = key_parts[0].reshape(seq_len, local_heads, HD)
    value_terms = key_parts[1].reshape(seq_len, local_heads, HD)
    grad_keys, grad_values = (
        lax.psum_scatter(
            key_terms.astype(jnp.bfloat16), "blk", scatter_dimension=0, tiled=True
        ).astype(jnp.float32),
        lax.psum_scatter(
            value_terms.astype(jnp.bfloat16), "blk", scatter_dimension=0, tiled=True
        ).astype(jnp.float32),
    )
    grad_query_b = (grad_query_sum * score_scale).astype(bf16)
    grad_key_b = (grad_keys * score_scale).astype(bf16)
    grad_value_flat = grad_values.astype(bf16).reshape(query_count, head_width)
    grad_query_unit = rotary(grad_query_b.astype(f32), query_ids, -1.0)
    query_gain_term = jnp.sum(grad_query_unit * query_unit, axis=(0, 1))
    grad_query_flat = (
        rms_back(query_proj, query_inv, grad_query_unit * query_gain)
        .astype(bf16)
        .reshape(query_count, head_width)
    )
    grad_key_unit = rotary(grad_key_b.astype(f32), query_ids, -1.0)
    key_gain_term = jnp.sum(grad_key_unit * key_unit, axis=(0, 1))
    grad_key_flat = (
        rms_back(key_proj, key_inv, grad_key_unit * key_gain)
        .astype(bf16)
        .reshape(query_count, head_width)
    )
    normed_part_sum = jnp.einsum(
        "qc,dc->qd", grad_query_flat, full_query, preferred_element_type=f32
    )
    normed_part_sum = normed_part_sum + jnp.einsum(
        "qc,dc->qd", grad_key_flat, full_key, preferred_element_type=f32
    )
    normed_part_sum = normed_part_sum + jnp.einsum(
        "qc,dc->qd", grad_value_flat, full_value, preferred_element_type=f32
    )
    grad_normed = sum_rows(normed_part_sum)
    attn_gain_term = jnp.sum(grad_normed * inputs * first_inv, axis=0)
    input_grad = grad_middle + rms_back(inputs, first_inv, grad_normed * attn_gain)
    attn_grads = lax.psum_scatter(
        jnp.concatenate(
            [
                jnp.einsum("qc,qf->cf", normed_all, grad_query_flat, preferred_element_type=f32),
                jnp.einsum("qc,qf->cf", normed_all, grad_key_flat, preferred_element_type=f32),
                jnp.einsum("qc,qf->cf", normed_all, grad_value_flat, preferred_element_type=f32),
                jnp.einsum("qc,qf->cf", branch_all, attended_b, preferred_element_type=f32),
            ],
            axis=1,
        ).astype(jnp.bfloat16),
        ("dp", "blk"),
        scatter_dimension=0,
        tiled=True,
    ).astype(jnp.float32)
    summed = lax.psum(
        (attn_gain_term, ffn_gain_term, query_gain_term, key_gain_term, router_term),
        ("dp", "head", "blk"),
    )
    return (
        output,
        input_grad,
        summed[0],
        attn_grads[:, :head_width],
        attn_grads[:, head_width : 2 * head_width],
        attn_grads[:, 2 * head_width : 3 * head_width],
        attn_grads[:, 3 * head_width :],
        summed[2],
        summed[3],
        summed[1],
        summed[4],
        expert_in_grad,
        expert_out_grad,
    )


def solution(mesh):
    placed = (
        P(("dp", "head", "blk"), None),
        P("dp", None),
        P("dp", None),
        P(("dp", "head", "blk"), None),
        P(),
        P(("dp", "blk"), "head"),
        P(("dp", "blk"), "head"),
        P(("dp", "blk"), "head"),
        P(("dp", "blk"), "head"),
        P(),
        P(),
        P(),
        P(),
        P("dp", ("head", "blk"), None),
        P("dp", ("head", "blk"), None),
        P(("dp", "head", "blk"), None),
    )
    return jax.shard_map(
        on_device,
        mesh=mesh,
        in_specs=placed,
        out_specs=(
            P(("dp", "head", "blk"), None),
            P(("dp", "head", "blk"), None),
            P(),
            P(("dp", "blk"), "head"),
            P(("dp", "blk"), "head"),
            P(("dp", "blk"), "head"),
            P(("dp", "blk"), "head"),
            P(),
            P(),
            P(),
            P(),
            P("dp", ("head", "blk"), None),
            P("dp", ("head", "blk"), None),
        ),
        check_vma=False,
    )
```

profile of v0, /device:TPU:0, one launch (start us, length us, event | category | flops | bytes accessed | tf_op | source)
XLA Modules:
  0.0 1989.0 jit_solution(15340407097306516658)
XLA Ops:
  14.0 27.2 %all-gather.11.cloned.1.call-done = bf16[512,2048]{1,0:T(8,128)(2,1)} async-done(((bf16[128,2048]{1,0:T(8,128)(2,1)}), bf16[512,2048]{1,0:T(8,128)(2,1)}) %all-gather.11.cloned.1.call-update) | async-done | bytes 2097168 | tf_op jit(solution)/shard_map/all_gather | solution.py:45
  41.2 154.4 %all-gather.19.cloned.1.call-done = bf16[2048,512]{1,0:T(8,128)(2,1)} async-done(((bf16[64,512]{1,0:T(8,128)(2,1)}), bf16[2048,512]{1,0:T(8,128)(2,1)}) %all-gather.19.cloned.1.call-update) | async-done | bytes 2097168 | tf_op jit(solution)/shard_map/all_gather | solution.py:98
  202.0 148.2 %all-gather.13.cloned.1.call-done = bf16[2048,512]{1,0:T(8,128)(2,1)} async-done(((bf16[64,512]{1,0:T(8,128)(2,1)}), bf16[2048,512]{1,0:T(8,128)(2,1)}) %all-gather.13.cloned.1.call-update) | async-done | bytes 2097168 | tf_op jit(solution)/shard_map/all_gather | solution.py:97
  354.2 150.7 %all-gather.17.cloned.1.call-done = bf16[2048,512]{1,0:T(8,128)(2,1)} async-done(((bf16[64,512]{1,0:T(8,128)(2,1)}), bf16[2048,512]{1,0:T(8,128)(2,1)}) %all-gather.17.cloned.1.call-update) | async-done | bytes 2097168 | tf_op jit(solution)/shard_map/all_gather | solution.py:96
  515.6 43.7 %all-gather.21.cloned.1.call-done = bf16[4096,4,128]{2,0,1:T(8,128)(2,1)} async-done(((bf16[512,4,128]{2,0,1:T(8,128)(2,1)}), bf16[4096,4,128]{2,0,1:T(8,128)(2,1)}) %all-gather.21.cloned.1.call-update) | async-done | bytes 4194320 | tf_op jit(solution)/shard_map/all_gather | solution.py:154
  559.3 53.5 %all-gather.15.cloned.1.call-done = bf16[4096,4,128]{2,0,1:T(8,128)(2,1)} async-done(((bf16[512,4,128]{2,0,1:T(8,128)(2,1)}), bf16[4096,4,128]{2,0,1:T(8,128)(2,1)}) %all-gather.15.cloned.1.call-update) | async-done | bytes 4194320 | tf_op jit(solution)/shard_map/all_gather | solution.py:153
  612.7 58.2 %while.30 = (s32[]{:T(128)}, f32[4,512]{1,0:T(4,128)S(1)}, f32[4,512]{1,0:T(4,128)S(1)}, f32[512,4,128]{0,2,1:T(8,128)S(1)}, s32[4,128]{1,0:T(4,128)S(1)}, /*ind...) while((s32[]{:T(128)}, f32[4,512]{1,0:T(4,128)S(1)}, ...), condition=%wide.region_6.7_spmd.clone, body=%wide.region_3.6_spmd.clone.sunk | while | flops 550253056 | bytes 17452288 | solution.py:174
  671.8 94.8 %all-gather.23.cloned.1.call-done = bf16[2048,512]{1,0:T(8,128)(2,1)} async-done(((bf16[64,512]{1,0:T(8,128)(2,1)}), bf16[2048,512]{1,0:T(8,128)(2,1)}) %all-gather.23.cloned.1.call-update) | async-done | bytes 2097168 | tf_op jit(solution)/shard_map/all_gather | solution.py:99
  778.2 18.0 reduce-window.6
  857.7 58.5 %all-to-all-done.2 = bf16[2,32,24,2048]{3,2,0,1:T(8,128)(2,1)} async-done(((bf16[2,32,24,2048]{3,2,0,1:T(8,128)(2,1)}), bf16[2,32,24,2048]{3,2,0,1:T(8,128)(2,1)}, u32[]{:S(2)}, u32[]{:S(2)}) %all-to-all-start.2) | async-done | bytes 6291488 | tf_op jit(solution)/shard_map/all_to_all | solution.py:55
  927.9 72.9 %all-to-all-done = bf16[2,32,24,2048]{3,2,0,1:T(8,128)(2,1)} async-done(((bf16[2,32,24,2048]{3,2,0,1:T(8,128)(2,1)}), bf16[2,32,24,2048]{3,2,0,1:T(8,128)(2,1)}, u32[]{:S(2)}, u32[]{:S(2)}) %all-to-all-start) | async-done | bytes 6291488 | tf_op jit(solution)/shard_map/all_to_all | solution.py:55
  1007.3 21.2 %fusion.112 = f32[2,768,2048]{2,1,0:T(8,128)} fusion(bf16[2,768,2048]{2,1,0:T(8,128)(2,1)} %bitcast.304, bf16[2048,2,2048]{2,0,1:T(8,128)(2,1)} %all-gather.25.cloned.1.call-done), kind=kOutput, calls=%fused_computation.233 | convolution fusion | flops 12884901888 | bytes 35651584 | tf_op jit(solution)/shard_map/erd,def->erf/dot_general | solution.py:209
  1065.5 19.4 convolution_convert_fusion.1
  1091.5 53.5 %all-to-all-done.1 = bf16[2,32,24,2048]{3,2,0,1:T(8,128)(2,1)} async-done(((bf16[2,32,24,2048]{3,2,0,1:T(8,128)(2,1)}), bf16[2,32,24,2048]{3,2,0,1:T(8,128)(2,1)}, u32[]{:S(2)}, u32[]{:S(2)}) %all-to-all-start.1) | async-done | bytes 6291488 | tf_op jit(solution)/shard_map/all_to_all | solution.py:59
  1175.6 54.0 %all-to-all-done.3 = bf16[2,32,24,2048]{3,2,0,1:T(8,128)(2,1)} async-done(((bf16[2,32,24,2048]{3,2,0,1:T(8,128)(2,1)}), bf16[2,32,24,2048]{3,2,0,1:T(8,128)(2,1)}, u32[]{:S(2)}, u32[]{:S(2)}) %all-to-all-start.3) | async-done | bytes 6291488 | tf_op jit(solution)/shard_map/all_to_all | solution.py:59
  1258.0 25.6 %all-gather.29.cloned.1.call-done = bf16[512,2048]{1,0:T(8,128)(2,1)} async-done(((bf16[128,2048]{1,0:T(8,128)(2,1)}), bf16[512,2048]{1,0:T(8,128)(2,1)}) %all-gather.29.cloned.1.call-update) | async-done | bytes 2097168 | tf_op jit(solution)/shard_map/all_gather | solution.py:45
  1290.3 107.1 %while.31 = (s32[]{:T(128)}, f32[512,4,128]{0,2,1:T(8,128)S(1)}, bf16[8,512,4,128]{3,1,0,2:T(8,128)(2,1)}, bf16[8,512,4,128]{3,1,0,2:T(8,128)(2,1)}, s32[8]{0:T(...) while((s32[]{:T(128)}, f32[512,4,128]{0,2,1:T(8,128)S(1)}, ...), condition=%wide.region_27.28_spmd.clone, body=%wide.region_26.27_spmd.clone.sunk | while | flops 1354236416 | bytes 29666620 | solution.py:296
  1400.9 49.1 %reduce-scatter.11.cloned.1.call-done = bf16[512,4,128]{2,0,1:T(8,128)(2,1)} async-done(((bf16[4096,4,128]{2,0,1:T(8,128)(2,1)}), bf16[512,4,128]{2,0,1:T(8,128)(2,1)}) %reduce-scatter.11.cloned.1.call-update) | async-done | bytes 524304 | tf_op jit(solution)/shard_map/reduce_scatter | solution.py:304
  1467.4 37.6 %reduce-scatter.13.cloned.1.call-done = bf16[512,4,128]{2,0,1:T(8,128)(2,1)} async-done(((bf16[4096,4,128]{2,0,1:T(8,128)(2,1)}), bf16[512,4,128]{2,0,1:T(8,128)(2,1)}) %reduce-scatter.13.cloned.1.call-update) | async-done | bytes 524304 | tf_op jit(solution)/shard_map/reduce_scatter | solution.py:307
  1549.8 20.6 %convert_bitcast_fusion = bf16[2048,2,2048]{0,2,1:T(8,128)(2,1)} fusion(bf16[2,768,2048]{2,1,0:T(8,128)(2,1)} %bitcast.305, bf16[2,768,1024]{2,1,0:T(8,128)(2,1)} %get-tuple-element.640, bf16[2,768,1024]{2,1,0:T(8,128)(2,1)} %get-tuple-element.639), kind=kOutput, calls=%fused_computation.60 | convolution fusion | flops 12905873408 | bytes 29360128 | tf_op jit(solution)/shard_map/erc,erf->cef/dot_general | solution.py:239
  1570.4 27.4 %pad_maximum_fusion = bf16[2048,2,3072]{0,2,1:T(8,128)(2,1)} fusion(bf16[2048,2,1024]{0,2,1:T(8,128)(2,1)} %convert_bitcast_fusion.1, bf16[2048,2,2048]{0,2,1:T(8,128)(2,1)} %convert_bitcast_fusion), kind=kLoop, calls=%fused_computation.59 | loop fusion | flops 50331648 | bytes 50331648 | tf_op jit(solution)/shard_map/concatenate | solution.py:242
  1604.9 70.1 %all-reduce = (f32[2048]{0:T(1024)}, f32[128]{0:T(128)}, f32[128]{0:T(128)}, f32[2048]{0:T(1024)}) all-reduce(f32[2048]{0:T(1024)S(1)} %get-tuple-element.563, f32[128]{0:T(128)S(1)} %bitcast_reduce_fusion.1, f32[128]{0:T(128)S(1)} %bitcast_reduce_fusion, ...), channel_id=1, replica_groups=mesh['dp'=4,'head'=4,'blk'=8] {'dp','head','blk'}, use_global_device_ids=true, to_apply=%region_35.36 | all-reduce | flops 4352 | bytes 34816 | tf_op jit(solution)/shard_map/psum | solution.py:354
  1675.0 58.7 %reduce-scatter.19.cloned.1.call-done = bf16[64,2048]{1,0:T(8,128)(2,1)} async-done(((bf16[2048,2048]{1,0:T(8,128)(2,1)}), bf16[64,2048]{1,0:T(8,128)(2,1)}) %reduce-scatter.19.cloned.1.call-update) | async-done | bytes 262160
  1738.1 209.8 %reduce-scatter.17.cloned.1.call-done = bf16[512,2,3072]{0,2,1:T(8,128)(2,1)} async-done(((bf16[2048,2,3072]{0,2,1:T(8,128)(2,1)}), bf16[512,2,3072]{0,2,1:T(8,128)(2,1)}) %reduce-scatter.17.cloned.1.call-update) | async-done | bytes 6291472 | tf_op jit(solution)/shard_map/reduce_scatter | solution.py:241
  (498 shorter events, 491.6 us)
Async XLA Ops:
  8.0 803.7 %copy-start = (bf16[2048,64]{0,1:T(8,128)(2,1)S(1)}, bf16[2048,64]{0,1:T(8,128)(2,1)}, u32[]{:S(2)}) copy-start(bf16[2048,64]{0,1:T(8,128)(2,1)} %param.32) | copy-start | bytes 786436
  8.0 33.1 %all-gather.11.cloned.1.call-start = ((), (), s32[]{:S(2)}) async-start(), calls=%async_computation.10 | async-start | bytes 2621440 | tf_op jit(solution)/shard_map/all_gather | solution.py:45
  11.9 183.6 %all-gather.19.cloned.1.call-start = ((), (), s32[]{:S(2)}) async-start(), calls=%async_computation.14 | async-start | bytes 2162688 | tf_op jit(solution)/shard_map/all_gather | solution.py:98
  12.7 337.6 %all-gather.13.cloned.1.call-start = ((), (), s32[]{:S(2)}) async-start(), calls=%async_computation.11 | async-start | bytes 2162688 | tf_op jit(solution)/shard_map/all_gather | solution.py:97
  13.4 491.5 %all-gather.17.cloned.1.call-start = ((), (), s32[]{:S(2)}) async-start(), calls=%async_computation.13 | async-start | bytes 2162688 | tf_op jit(solution)/shard_map/all_gather | solution.py:96
  14.0 545.3 %all-gather.21.cloned.1.call-start = ((), (), s32[]{:S(2)}) async-start(), calls=%async_computation.15 | async-start | bytes 4718592 | tf_op jit(solution)/shard_map/all_gather | solution.py:154
  200.1 412.6 %all-gather.15.cloned.1.call-start = ((), (), s32[]{:S(2)}) async-start(), calls=%async_computation.12 | async-start | bytes 4718592 | tf_op jit(solution)/shard_map/all_gather | solution.py:153
  354.1 154.7 %copy-start.7 = (f32[512,4,128]{2,0,1:T(8,128)}, f32[512,4,128]{2,0,1:T(8,128)S(1)}, u32[]{:S(2)}) copy-start(f32[512,4,128]{2,0,1:T(8,128)S(1)} %copy.284) | copy-start | bytes 3145732
  354.2 154.7 %copy-start.63 = (f32[128]{0:T(128)S(1)}, f32[128]{0:T(128)}, u32[]{:S(2)}) copy-start(f32[128]{0:T(128)} %param.29) | copy-start | bytes 1540
  513.0 253.5 %all-gather.23.cloned.1.call-start = ((), (), s32[]{:S(2)}) async-start(), calls=%async_computation.16 | async-start | bytes 2162688 | tf_op jit(solution)/shard_map/all_gather | solution.py:99
  513.7 295.3 %reduce-scatter.9.cloned.1.call-start = ((), (), s32[]{:S(2)}) async-start(), calls=%async_computation.17 | async-start | bytes 2621440 | tf_op jit(solution)/shard_map/reduce_scatter | solution.py:49
  770.8 236.5 %all-gather.25.cloned.1.call-start = ((), (), s32[]{:S(2)}) async-start(), calls=%async_computation.18 | async-start | bytes 20971520 | tf_op jit(solution)/shard_map/all_gather | solution.py:102
  831.2 85.0 %all-to-all-start.2 = ((bf16[2,32,24,2048]{3,2,0,1:T(8,128)(2,1)}), bf16[2,32,24,2048]{3,2,0,1:T(8,128)(2,1)}, u32[]{:S(2)}, u32[]{:S(2)}) async-start(bf16[2,32,24,2048]{3,2,0,1:T(8,128)(2,1)} %copy.304), calls=%async_computation.3 | async-start | bytes 12582912 | tf_op jit(solution)/shard_map/all_to_all | solution.py:55
  836.6 191.9 %all-gather.27.cloned.1.call-start = ((), (), s32[]{:S(2)}) async-start(), calls=%async_computation.19 | async-start | bytes 10485760 | tf_op jit(solution)/shard_map/all_gather | solution.py:103
  916.1 84.7 %all-to-all-start = ((bf16[2,32,24,2048]{3,2,0,1:T(8,128)(2,1)}), bf16[2,32,24,2048]{3,2,0,1:T(8,128)(2,1)}, u32[]{:S(2)}, u32[]{:S(2)}) async-start(bf16[2,32,24,2048]{3,2,0,1:T(8,128)(2,1)} %copy.297), calls=%async_computation.1 | async-start | bytes 12582912 | tf_op jit(solution)/shard_map/all_to_all | solution.py:55
  1060.6 84.5 %all-to-all-start.1 = ((bf16[2,32,24,2048]{3,2,0,1:T(8,128)(2,1)}), bf16[2,32,24,2048]{3,2,0,1:T(8,128)(2,1)}, u32[]{:S(2)}, u32[]{:S(2)}) async-start(bf16[2,32,24,2048]{3,2,0,1:T(8,128)(2,1)} %copy.301), calls=%async_computation.2 | async-start | bytes 12582912 | tf_op jit(solution)/shard_map/all_to_all | solution.py:59
  1145.1 84.5 %all-to-all-start.3 = ((bf16[2,32,24,2048]{3,2,0,1:T(8,128)(2,1)}), bf16[2,32,24,2048]{3,2,0,1:T(8,128)(2,1)}, u32[]{:S(2)}, u32[]{:S(2)}) async-start(bf16[2,32,24,2048]{3,2,0,1:T(8,128)(2,1)} %copy.306), calls=%async_computation.4 | async-start | bytes 12582912 | tf_op jit(solution)/shard_map/all_to_all | solution.py:59
  1150.0 133.6 %all-gather.29.cloned.1.call-start = ((), (), s32[]{:S(2)}) async-start(), calls=%async_computation.20 | async-start | bytes 2621440 | tf_op jit(solution)/shard_map/all_gather | solution.py:45
  1257.9 192.1 %reduce-scatter.11.cloned.1.call-start = ((), (), s32[]{:S(2)}) async-start(), calls=%async_computation.21 | async-start | bytes 4718592 | tf_op jit(solution)/shard_map/reduce_scatter | solution.py:304
  1397.4 107.6 %reduce-scatter.13.cloned.1.call-start = ((), (), s32[]{:S(2)}) async-start(), calls=%async_computation.22 | async-start | bytes 4718592 | tf_op jit(solution)/shard_map/reduce_scatter | solution.py:307
  1398.1 201.9 %reduce-scatter.15.cloned.1.call-start = ((), (), s32[]{:S(2)}) async-start(), calls=%async_computation.23 | async-start | bytes 2621440 | tf_op jit(solution)/shard_map/reduce_scatter | solution.py:49
  1513.8 219.8 %reduce-scatter.19.cloned.1.call-start = ((), (), s32[]{:S(2)}) async-start(), calls=%async_computation.26 | async-start | bytes 8650752
  1537.4 410.5 %reduce-scatter.17.cloned.1.call-start = ((), (), s32[]{:S(2)}) async-start(), calls=%async_computation.25 | async-start | bytes 31457280 | tf_op jit(solution)/shard_map/reduce_scatter | solution.py:241
  1597.8 381.6 %all-reduce.3.cloned.1.call-start = ((), (), s32[]{:S(2)}) async-start(), calls=%async_computation.24 | async-start | bytes 1048576 | tf_op jit(solution)/shard_map/psum | solution.py:354
  (75 other events, 1338.7 us)
Sparse Core Ops, SparseCore 0:
  12.0 29.0 all-gather.10
  42.8 152.6 all-gather.18
  197.2 153.0 all-gather.12
  351.8 153.0 all-gather.16
  506.9 52.3 all-gather.20
  561.3 51.3 all-gather.14
  614.4 152.1 all-gather.22
  770.9 38.1 reduce-scatter.8
  1258.1 25.5 all-gather.28
  1397.5 52.4 reduce-scatter.10
  1453.1 51.8 reduce-scatter.12
  1513.9 37.1 reduce-scatter.14
  1553.6 180.0 reduce-scatter.18
  1736.1 211.7 reduce-scatter.16
Sparse Core Ops, SparseCore 1:
  777.3 153.6 all-gather.24
  932.6 84.1 all-gather.26
  1603.6 184.1 all-reduce.2
where the time goes:
time: 2000 us; the launch traced here: 1990 us
  waiting for transfers between devices  1310 us (66%)
  matrix products  250 us (12%)
  local copies, waits for them, and re-layouts  186 us (9%)
  other arithmetic  124 us (6%)
  blocking collectives  70.1 us (4%)
  starting transfers between devices  22.2 us (1%)
    reduce_scatter x1, waiting for transfers between devices, on_device(): lax.psum_scatter(jnp.concatenate([term_in, term_back], axis=-1).astype(jn...  210 us
    all_gather x1, waiting for transfers between devices, on_device(): lax.all_gather(w_value, ('dp', 'blk'), axis=0, tiled=True)  154 us
    all_gather x1, waiting for transfers between devices, on_device(): lax.all_gather(w_query, ('dp', 'blk'), axis=0, tiled=True)  151 us
    all_gather x1, waiting for transfers between devices, on_device(): lax.all_gather(w_key, ('dp', 'blk'), axis=0, tiled=True)  148 us
    all_to_all x2, waiting for transfers between devices, to_experts(): lax.all_to_all(buffer, ('head', 'blk'), split_axis=1, concat_axis=1, tile...  131 us
    all_to_all x2, waiting for transfers between devices, from_experts(): lax.all_to_all(buffer, ('head', 'blk'), split_axis=1, concat_axis=1, tile...  107 us
    all_gather x1, waiting for transfers between devices, on_device(): lax.all_gather(w_out, ('dp', 'blk'), axis=0, tiled=True)  94.8 us
    psum x1, blocking collectives, on_device(): lax.psum((attn_gain_term, ffn_gain_term, query_gain_term, key_gain_term,...  70.1 us
  transfers between devices with their start and end apart: 21, of which 17 were waited for; matrix products, arithmetic and copies ran while one was open for 19% of the time, Pallas kernels for 0%

commit v1 on v0

v1 whole, which is shorter than its diff:
```python
import functools
import math

import jax
import jax.numpy as jnp
from jax import lax
from jax.experimental import pallas as pl
from jax.experimental.pallas import tpu as pltpu
from jax.sharding import PartitionSpec as P

HEADS = 16
HD = 128
FF = 1024
TOPK = 8
EXP_DEV = 2
CAP = 24
EXPERTS = 64

epsilon = 1e-06
rope_base = 50000.0
highest = lax.Precision.HIGHEST
f32 = jnp.float32
bf16 = jnp.bfloat16
i32 = jnp.int32
MESH = pl.DeviceIdType.MESH
ANY = pl.BlockSpec(memory_space=pl.ANY)
VMEM = pl.BlockSpec(memory_space=pltpu.VMEM)
SMEM = pl.BlockSpec(memory_space=pltpu.SMEM)
DMA = pltpu.SemaphoreType.DMA


def rms_rows(values):
    return lax.rsqrt(jnp.mean(values * values, axis=-1, keepdims=True) + epsilon)


def rms_back(values, inverse, grad_scaled):
    inner_mean = jnp.mean(grad_scaled * values, axis=-1, keepdims=True)
    return inverse * grad_scaled - values * inverse * inverse * inverse * inner_mean


def wrap4(value):
    return lax.rem(value + 4, 4)


class Place:
    def __init__(self):
        head, blk = lax.axis_index("head"), lax.axis_index("blk")
        self.dp = lax.axis_index("dp")
        self.yh, self.co = head // 2, lax.rem(head, 2)
        self.yl, self.x = blk // 4, lax.rem(blk, 4)
        self.head = head
        self.zr, self.zl, self.zo = (wrap4(self.dp + s) for s in (1, -1, 2))
        self.xr, self.xl, self.xo = (wrap4(self.x + s) for s in (1, -1, 2))
        y = self.yh * 2 + self.yl
        self.yr, self.ylf, self.yo = (wrap4(y + s) for s in (1, -1, 2))
        self.ZR, self.ZL = {"dp": self.zr}, {"dp": self.zl}
        self.XR, self.XL, self.XO = (self.to_x(v) for v in (self.xr, self.xl, self.xo))
        self.Y = {"blk": (1 - self.yl) * 4 + self.x}
        self.C = {"head": self.yh * 2 + (1 - self.co)}
        self.H = {"head": (1 - self.yh) * 2 + self.co}
        self.YR, self.YL = self.to_y(self.yr), self.to_y(self.ylf)

    def to_x(self, x):
        return {"blk": self.yl * 4 + x}

    def to_y(self, y):
        return {"head": (y // 2) * 2 + self.co, "blk": lax.rem(y, 2) * 4 + self.x}


def greet(devices):
    barrier = pltpu.get_barrier_semaphore()
    for device in devices:
        pl.semaphore_signal(barrier, inc=1, device_id=device, device_id_type=MESH)
    pl.semaphore_wait(barrier, len(devices))


class Wire:
    def __init__(self, send_sem, recv_sem):
        self.send_sem, self.recv_sem, self.started = send_sem, recv_sem, []

    def send(self, src, dst, device):
        at = len(self.started)
        copy = pltpu.make_async_remote_copy(
            src_ref=src,
            dst_ref=dst,
            send_sem=self.send_sem.at[at],
            recv_sem=self.recv_sem.at[at],
            device_id=device,
            device_id_type=MESH,
        )
        copy.start()
        self.started.append(copy)
        return copy

    def drain(self):
        for copy in self.started:
            copy.wait_send()


def local(src, dst, sem):
    copy = pltpu.make_async_copy(src, dst, sem)
    copy.start()
    return copy


def remote_call(body, name, cid, sends, locals_, ins, outs, out_shape, scratch=(), vmem=None):
    return pl.pallas_call(
        body,
        name=name,
        out_shape=out_shape,
        in_specs=ins,
        out_specs=outs,
        scratch_shapes=[DMA((sends,)), DMA((sends,)), DMA((max(locals_, 1),)), *scratch],
        compiler_params=pltpu.CompilerParams(
            collective_id=cid, has_side_effects=True, vmem_limit_bytes=vmem
        ),
    )


def shaped(shape, dtype=bf16):
    return jax.ShapeDtypeStruct(shape, dtype)


def weights_kernel(w, wo, n, g, go, m, ss, rs, ls):
    p = Place()
    dp, yl, x = p.dp, p.yl, p.x
    own = [
        local(w, g.at[:, dp, yl, x], ls.at[0]),
        local(n, m.at[p.head], ls.at[1]),
        local(wo, go.at[dp], ls.at[2]),
    ]
    greet([p.ZR, p.ZL, p.XR, p.XL, p.Y, p.C, p.H])
    wire = Wire(ss, rs)
    n_c = wire.send(n, m.at[p.head], p.C)
    z1 = wire.send(w, g.at[:, dp, yl, x], p.ZR)
    z2 = wire.send(w, g.at[:, dp, yl, x], p.ZL)
    n_h = wire.send(n, m.at[p.head], p.H)
    o1 = wire.send(wo, go.at[dp], p.ZR)
    o2 = wire.send(wo, go.at[dp], p.ZL)
    z1.wait_recv()
    z3 = wire.send(g.at[0:2, p.zl, yl, x], g.at[0:2, p.zl, yl, x], p.ZR)
    z2.wait_recv()
    z4 = wire.send(g.at[2, p.zr, yl, x], g.at[2, p.zr, yl, x], p.ZL)
    own[0].wait()
    z3.wait_recv()
    z4.wait_recv()
    b1 = wire.send(g.at[2, :, yl, x], g.at[2, :, yl, x], p.XR)
    b2 = wire.send(g.at[2, :, yl, x], g.at[2, :, yl, x], p.XL)
    a1 = wire.send(g.at[0:2, :, yl, x], g.at[0:2, :, yl, x], p.Y)
    c1 = wire.send(g.at[2, :, yl, x], g.at[2, :, yl, x], p.Y)
    o1.wait_recv()
    o3 = wire.send(go.at[p.zl, 0:32], go.at[p.zl, 0:32], p.ZR)
    o2.wait_recv()
    o4 = wire.send(go.at[p.zr, 32:64], go.at[p.zr, 32:64], p.ZL)
    n_h.wait_recv()
    other = (1 - p.yh) * 2 + p.co
    n_f = wire.send(m.at[other], m.at[other], p.C)
    b1.wait_recv()
    b3 = wire.send(g.at[2, 0:2, yl, p.xl], g.at[2, 0:2, yl, p.xl], p.XR)
    c2 = wire.send(g.at[2, :, yl, p.xl], g.at[2, :, yl, p.xl], p.Y)
    b2.wait_recv()
    b4 = wire.send(g.at[2, 2:4, yl, p.xr], g.at[2, 2:4, yl, p.xr], p.XL)
    c3 = wire.send(g.at[2, :, yl, p.xr], g.at[2, :, yl, p.xr], p.Y)
    a1.wait_recv()
    a2 = wire.send(g.at[0:2, :, :, x], g.at[0:2, :, :, x], p.XR)
    a3 = wire.send(g.at[0:2, :, :, x], g.at[0:2, :, :, x], p.XL)
    b3.wait_recv()
    b4.wait_recv()
    c4 = wire.send(g.at[2, :, yl, p.xo], g.at[2, :, yl, p.xo], p.Y)
    a2.wait_recv()
    a4 = wire.send(g.at[0, :, :, p.xl], g.at[0, :, :, p.xl], p.XR)
    a3.wait_recv()
    a5 = wire.send(g.at[1, :, :, p.xr], g.at[1, :, :, p.xr], p.XL)
    for copy in (n_c, n_f, o3, o4, c1, c2, c3, c4, a4, a5):
        copy.wait_recv()
    own[1].wait()
    own[2].wait()
    wire.drain()


def gather_weights(w, wo, n):
    return remote_call(
        weights_kernel,
        "gather_weights",
        1,
        24,
        3,
        [ANY] * 3,
        [ANY] * 3,
        (shaped((3, 4, 2, 4, 64, 512)), shaped((4, 64, 512)), shaped((4, 128, 2048))),
    )(w, wo, n)


def rows_kernel(n, m, ss, rs, ls):
    p = Place()
    own = local(n, m.at[p.head], ls.at[0])
    greet([p.C, p.H])
    wire = Wire(ss, rs)
    n_h = wire.send(n, m.at[p.head], p.H)
    n_c = wire.send(n, m.at[p.head], p.C)
    n_h.wait_recv()
    other = (1 - p.yh) * 2 + p.co
    n_f = wire.send(m.at[other], m.at[other], p.C)
    n_c.wait_recv()
    n_f.wait_recv()
    own.wait()
    wire.drain()


def gather_rows(n):
    return remote_call(
        rows_kernel, "gather_rows", 2, 3, 1, [ANY], [ANY], (shaped((4, 128, 2048)),)
    )(n)[0]


def sum_kernel(part, out, ss, rs, ls, got_c, got_h, half):
    p = Place()
    greet([p.C, p.H])
    wire = Wire(ss, rs)
    far = wire.send(part.at[1 - p.yh, 1 - p.co], got_c.at[0], p.C)
    near = wire.send(part.at[p.yh, 1 - p.co], got_c.at[1], p.C)
    far.wait_recv()

    def add_far(i, carry):
        rows = pl.ds(pl.multiple_of(i * 16, 16), 16)
        half[rows] = (
            part[1 - p.yh, p.co, rows].astype(f32) + got_c[0, rows].astype(f32)
        ).astype(bf16)
        return carry

    lax.fori_loop(0, 8, add_far, 0)
    over = wire.send(half, got_h, p.H)
    near.wait_recv()
    over.wait_recv()

    def add_near(i, carry):
        rows = pl.ds(pl.multiple_of(i * 16, 16), 16)
        out[rows] = (
            part[p.yh, p.co, rows].astype(f32)
            + got_c[1, rows].astype(f32)
            + got_h[rows].astype(f32)
        )
        return carry

    lax.fori_loop(0, 8, add_near, 0)
    wire.drain()


def sum_rows(part, cid):
    return remote_call(
        sum_kernel,
        "sum_rows",
        cid,
        3,
        1,
        [VMEM],
        [VMEM],
        (shaped((128, 2048), f32),),
        scratch=[
            pltpu.VMEM((2, 128, 2048), bf16),
            pltpu.VMEM((128, 2048), bf16),
            pltpu.VMEM((128, 2048), bf16),
        ],
        vmem=16 << 20,
    )(part.reshape(2, 2, 128, 2048))[0]


def heads_kernel(q, k, v, go, qd, kd, vd, gd, ss, rs, ls):
    p = Place()
    yl, x = p.yl, p.x
    own = [
        local(q.at[x], qd.at[:, x], ls.at[0]),
        local(k.at[x], kd.at[:, yl, x], ls.at[1]),
        local(v.at[x], vd.at[:, yl, x], ls.at[2]),
        local(go, gd.at[:, yl, x], ls.at[3]),
    ]
    greet([p.Y, p.XR, p.XL, p.XO])
    wire = Wire(ss, rs)
    done = [
        wire.send(k.at[x], kd.at[:, yl, x], p.Y),
        wire.send(v.at[x], vd.at[:, yl, x], p.Y),
    ]
    w1 = wire.send(go, gd.at[:, yl, x], p.Y)
    moved = []
    for there, came, device in ((p.xo, p.xo, p.XO), (p.xr, p.xl, p.XR), (p.xl, p.xr, p.XL)):
        ks = wire.send(k.at[there], kd.at[:, yl, x], device)
        vs = wire.send(v.at[there], vd.at[:, yl, x], device)
        moved.append((came, ks, vs))
    for there, device in ((p.xo, p.XO), (p.xr, p.XR), (p.xl, p.XL)):
        done.append(wire.send(q.at[there], qd.at[:, x], device))
    for came, ks, vs in moved[1:] + moved[:1]:
        ks.wait_recv()
        done.append(wire.send(kd.at[:, yl, came], kd.at[:, yl, came], p.Y))
        vs.wait_recv()
        done.append(wire.send(vd.at[:, yl, came], vd.at[:, yl, came], p.Y))
    own[3].wait()
    w1.wait_recv()
    w2 = wire.send(gd.at[:, :, x], gd.at[:, :, x], p.XR)
    w3 = wire.send(gd.at[:, :, x], gd.at[:, :, x], p.XL)
    w2.wait_recv()
    done.append(wire.send(gd.at[0:2, :, p.xl], gd.at[0:2, :, p.xl], p.XR))
    w3.wait_recv()
    done.append(wire.send(gd.at[2:4, :, p.xr], gd.at[2:4, :, p.xr], p.XL))
    for copy in done:
        copy.wait_recv()
    for copy in own[:3]:
        copy.wait()
    wire.drain()


def heads_over_x(q, k, v, go):
    return remote_call(
        heads_kernel,
        "heads_over_x",
        3,
        22,
        4,
        [ANY] * 4,
        [ANY] * 4,
        (
            shaped((4, 4, 128, 128)),
            shaped((4, 2, 4, 128, 128)),
            shaped((4, 2, 4, 128, 128)),
            shaped((4, 2, 4, 64, 512)),
        ),
    )(q, k, v, go)


def back_x_kernel(o, att, ss, rs, ls):
    p = Place()
    own = local(o.at[:, p.x], att.at[p.x], ls.at[0])
    greet([p.XR, p.XL, p.XO])
    wire = Wire(ss, rs)
    for there, device in ((p.xo, p.XO), (p.xr, p.XR), (p.xl, p.XL)):
        wire.send(o.at[:, there], att.at[p.x], device)
    for copy in wire.started:
        copy.wait_recv()
    own.wait()
    wire.drain()


def back_over_x(o):
    return remote_call(
        back_x_kernel, "back_over_x", 4, 3, 1, [ANY], [ANY], (shaped((4, 4, 128, 128)),)
    )(o)[0]


def go_x_kernel(o, d, ss, rs, ls):
    p = Place()
    own = local(o.at[p.x], d.at[:, p.x], ls.at[0])
    greet([p.XR, p.XL, p.XO])
    wire = Wire(ss, rs)
    for there, device in ((p.xo, p.XO), (p.xr, p.XR), (p.xl, p.XL)):
        wire.send(o.at[there], d.at[:, p.x], device)
    for copy in wire.started:
        copy.wait_recv()
    own.wait()
    wire.drain()


def go_over_x(o):
    return remote_call(
        go_x_kernel, "go_over_x", 5, 3, 1, [ANY], [ANY], (shaped((4, 4, 128, 128)),)
    )(o)[0]


def grads_x_kernel(dq, dk, dv, qd, kd, vd, ss, rs, ls, gk, gv, sk, sv):
    p = Place()
    x, yl = p.x, p.yl
    own = local(dq.at[:, x], qd.at[x], ls.at[0])
    greet([p.Y, p.XR, p.XL, p.XO])
    wire = Wire(ss, rs)
    order = ((p.xo, p.XO), (p.xr, p.XR), (p.xl, p.XL), (x, None))
    pairs = []
    for i, (there, device) in enumerate(order):
        pairs.append(
            (
                wire.send(dk.at[:, 1 - yl, there], gk.at[i], p.Y),
                wire.send(dv.at[:, 1 - yl, there], gv.at[i], p.Y),
            )
        )
    last = []
    for there, device in order[:3]:
        last.append(wire.send(dq.at[:, there], qd.at[x], device))
    for i, (there, device) in enumerate(order):
        for grads, got, summed, out, arrived in (
            (dk, gk, sk, kd, pairs[i][0]),
            (dv, gv, sv, vd, pairs[i][1]),
        ):
            arrived.wait_recv()
            for run in range(4):
                total = grads[run, yl, there].astype(f32) + got[i, run].astype(f32)
                if device is None:
                    out[x, run] = total.astype(bf16)
                else:
                    summed[i, run] = total.astype(bf16)
            if device is not None:
                last.append(wire.send(summed.at[i], out.at[x], device))
    for copy in last:
        copy.wait_recv()
    own.wait()
    wire.drain()


def grads_over_x(dq, dk, dv):
    return remote_call(
        grads_x_kernel,
        "grads_over_x",
        6,
        17,
        1,
        [ANY, VMEM, VMEM],
        [ANY, VMEM, VMEM],
        (shaped((4, 4, 128, 128)),) * 3,
        scratch=[
            pltpu.VMEM((4, 4, 128, 128), bf16),
            pltpu.VMEM((4, 4, 128, 128), bf16),
            pltpu.VMEM((3, 4, 128, 128), bf16),
            pltpu.VMEM((3, 4, 128, 128), bf16),
        ],
        vmem=16 << 20,
    )(dq, dk, dv)


QB = 256
KB = 512
SCALE = HD**-0.5
SCALE2 = SCALE * math.log2(math.e)


def attend_kernel(lim, q, k, v, qseg, qpos, kseg, o_low, o, linv, vext):
    rows = k.shape[0]
    ones = (lax.broadcasted_iota(i32, (KB, HD), 1) == 0).astype(bf16)

    def fill(i, carry):
        at = pl.ds(pl.multiple_of(i * KB, KB), KB)
        vext[at, :HD] = v[at]
        vext[at, HD:] = ones
        return carry

    lax.fori_loop(0, rows // KB, fill, 0)

    def one_query(b, carry):
        at = pl.ds(pl.multiple_of(b * QB, QB), QB)
        query, seg, pos = q[at], qseg[at], qpos[at]

        def one_key(j, acc):
            keys = pl.ds(pl.multiple_of(j * KB, KB), KB)
            score = lax.dot_general(
                query, k[keys], (((1,), (1,)), ((), ())), preferred_element_type=f32
            )
            key_pos = j * KB + lax.broadcasted_iota(i32, (1, KB), 1)
            allowed = (seg == kseg[:, keys]) | (pos == key_pos)
            weight = jnp.where(allowed, jnp.exp2(score * SCALE2), 0.0).astype(bf16)
            return acc + jnp.dot(weight, vext[keys], preferred_element_type=f32)

        acc = lax.fori_loop(lim[0, b], lim[1, b], one_key, jnp.zeros((QB, 2 * HD), f32))
        inverse = 1.0 / acc[:, HD : HD + 1]
        result = acc[:, :HD] * inverse
        o[at] = result
        o_low[at] = result.astype(bf16)
        linv[at] = jnp.broadcast_to(inverse, (QB, HD))
        return carry

    lax.fori_loop(0, q.shape[0] // QB, one_query, 0)


def attend(lim, q, k, v, qseg, qpos, kseg):
    n = q.shape[0]
    return pl.pallas_call(
        attend_kernel,
        name="attend",
        out_shape=(shaped((n, HD)), shaped((n, HD), f32), shaped((n, HD), f32)),
        in_specs=[SMEM] + [VMEM] * 6,
        out_specs=[VMEM] * 3,
        scratch_shapes=[pltpu.VMEM((k.shape[0], 2 * HD), bf16)],
        compiler_params=pltpu.CompilerParams(vmem_limit_bytes=32 << 20),
    )(lim, q, k, v, qseg[:, None], qpos[:, None], kseg[None])


def attend_back_kernel(
    lim, q, k, v, g, qseg, qpos, kseg, linv, delta, dq, dk, dv, kt, dk_acc, dv_acc
):
    rows = k.shape[0]

    def fill(i, carry):
        at = pl.ds(pl.multiple_of(i * KB, KB), KB)
        kt[:, at] = k[at].astype(f32).T.astype(bf16)
        dk_acc[at] = jnp.zeros((KB, HD), f32)
        dv_acc[at] = jnp.zeros((KB, HD), f32)
        return carry

    lax.fori_loop(0, rows // KB, fill, 0)
    across = (((1,), (1,)), ((), ()))

    def one_query(b, carry):
        at = pl.ds(pl.multiple_of(b * QB, QB), QB)
        query, grad = q[at], g[at]
        seg, pos, inverse, shift = qseg[:, at], qpos[:, at], linv[:, at], delta[:, at]

        def one_key(j, acc):
            keys = pl.ds(pl.multiple_of(j * KB, KB), KB)
            key = k[keys]
            score = lax.dot_general(key, query, across, preferred_element_type=f32)
            key_pos = j * KB + lax.broadcasted_iota(i32, (KB, 1), 0)
            allowed = (kseg[keys] == seg) | (key_pos == pos)
            prob = jnp.where(allowed, jnp.exp2(score * SCALE2), 0.0) * inverse
            grad_prob = lax.dot_general(v[keys], grad, across, preferred_element_type=f32)
            grad_score = (prob * (grad_prob - shift)).astype(bf16)
            dv_acc[keys] += jnp.dot(prob.astype(bf16), grad, preferred_element_type=f32)
            dk_acc[keys] += jnp.dot(grad_score, query, preferred_element_type=f32)
            return acc + jnp.dot(kt[:, keys], grad_score, preferred_element_type=f32)

        acc = lax.fori_loop(lim[0, b], lim[1, b], one_key, jnp.zeros((HD, QB), f32))
        dq[at] = (acc * SCALE).T.astype(bf16)
        return carry

    lax.fori_loop(0, q.shape[0] // QB, one_query, 0)

    def finish(i, carry):
        at = pl.ds(pl.multiple_of(i * KB, KB), KB)
        dk[at] = (dk_acc[at] * SCALE).astype(bf16)
        dv[at] = dv_acc[at].astype(bf16)
        return carry

    lax.fori_loop(0, rows // KB, finish, 0)


def attend_back(lim, q, k, v, g, qseg, qpos, kseg, linv, delta):
    n, rows = q.shape[0], k.shape[0]
    return pl.pallas_call(
        attend_back_kernel,
        name="attend_back",
        out_shape=(shaped((n, HD)), shaped((rows, HD)), shaped((rows, HD))),
        in_specs=[SMEM] + [VMEM] * 9,
        out_specs=[VMEM] * 3,
        scratch_shapes=[
            pltpu.VMEM((HD, rows), bf16),
            pltpu.VMEM((rows, HD), f32),
            pltpu.VMEM((rows, HD), f32),
        ],
        compiler_params=pltpu.CompilerParams(vmem_limit_bytes=40 << 20),
    )(lim, q, k, v, g, qseg[None], qpos[None], kseg[:, None], linv[None], delta[None])


def spread_kernel(src, dst, ss, rs, ls):
    p = Place()
    yh, co, yl, x = p.yh, p.co, p.yl, p.x
    own = local(src, dst.at[yh, co, yl, x], ls.at[0])
    greet([p.XR, p.XL, p.YR, p.YL, p.C])
    wire = Wire(ss, rs)
    A, A1, A2 = pl.ds(0, 64), pl.ds(0, 32), pl.ds(32, 32)
    B, B1, B2 = pl.ds(64, 64), pl.ds(64, 32), pl.ds(96, 32)

    def at_y(y, rows):
        return dst.at[y // 2, co, lax.rem(y, 2), :, rows]

    def at_x(xx, rows):
        return dst.at[:, co, :, xx, rows]

    def both(ref, device):
        return wire.send(ref, ref, device)

    y = yh * 2 + yl
    me = dst.at[yh, co, yl]
    a1 = wire.send(src.at[A], me.at[x, A], p.XR)
    b1 = wire.send(src.at[B], me.at[x, B], p.YR)
    a2 = wire.send(src.at[A], me.at[x, A], p.XL)
    b2 = wire.send(src.at[B], me.at[x, B], p.YL)
    a1.wait_recv()
    a3 = both(me.at[p.xl, A1], p.XR)
    a2.wait_recv()
    a4 = both(me.at[p.xr, A2], p.XL)
    yr, ylf, yo = p.yr, p.ylf, p.yo

    def block(yy, rows):
        return dst.at[yy // 2, co, lax.rem(yy, 2), x, rows]

    b1.wait_recv()
    b3 = both(block(ylf, B1), p.YR)
    b2.wait_recv()
    b4 = both(block(yr, B2), p.YL)
    own.wait()
    a3.wait_recv()
    a4.wait_recv()
    a5 = both(at_y(y, A), p.YR)
    a6 = both(at_y(y, A), p.YL)
    b3.wait_recv()
    b4.wait_recv()
    b5 = both(at_x(x, B), p.XR)
    b6 = both(at_x(x, B), p.XL)
    last = [both(at_y(y, A), p.C), both(at_x(x, B), p.C)]
    a5.wait_recv()
    a7 = both(at_y(ylf, A1), p.YR)
    b5.wait_recv()
    b7 = both(at_x(p.xl, B1), p.XR)
    a6.wait_recv()
    a8 = both(at_y(yr, A2), p.YL)
    b6.wait_recv()
    b8 = both(at_x(p.xr, B2), p.XL)
    last += [both(at_y(ylf, A), p.C), both(at_x(p.xl, B), p.C)]
    last += [both(at_y(yr, A), p.C), both(at_x(p.xr, B), p.C)]
    a7.wait_recv()
    last.append(both(at_y(yo, A1), p.C))
    b7.wait_recv()
    last.append(both(at_x(p.xo, B1), p.C))
    a8.wait_recv()
    last.append(both(at_y(yo, A2), p.C))
    b8.wait_recv()
    last.append(both(at_x(p.xo, B2), p.C))
    for copy in last:
        copy.wait_recv()
    wire.drain()


def spread(src):
    width = src.shape[1]
    return remote_call(
        spread_kernel,
        "spread",
        7,
        26,
        1,
        [ANY],
        [ANY],
        (shaped((2, 2, 2, 4, 128, width)),),
    )(src)[0].reshape(32, 128, width)


def pick_kernel(sel, src, rows_out, grads_out):
    width = rows_out.shape[-1]
    tokens = jnp.concatenate([src[0, :, :width], src[1, :, :width]], axis=0)
    cot = jnp.concatenate([src[0, :, width : 2 * width], src[1, :, width : 2 * width]], axis=0)
    info = jnp.concatenate([src[0, :, 2 * width :], src[1, :, 2 * width :]], axis=0)
    table = lax.dot_general(
        sel[...], info, (((1,), (1,)), ((), ())), preferred_element_type=f32
    )
    row = lax.broadcasted_iota(i32, (2 * CAP, 256), 0)
    block = lax.broadcasted_iota(i32, (2 * CAP, 256), 1) // 128
    want = row - block * CAP
    for e in range(EXP_DEV):
        slot = jnp.broadcast_to(table[e : e + 1], (2 * CAP, 256)).astype(i32)
        hit = (slot == want) & (want >= 0) & (want < CAP)
        one = hit.astype(bf16)
        gate = jnp.sum(jnp.where(hit, table[2 + e : 3 + e], 0.0), axis=1, keepdims=True)
        rows_out[e, 0] = jnp.dot(one, tokens, preferred_element_type=f32).astype(bf16)
        grads_out[e, 0] = (jnp.dot(one, cot, preferred_element_type=f32) * gate).astype(bf16)


def pick_rows(sel, src, width):
    blocks, _, full = src.shape
    pairs = blocks // 2
    out = shaped((EXP_DEV, pairs, 2 * CAP, width))
    spec = pl.BlockSpec((EXP_DEV, 1, 2 * CAP, width), lambda i: (0, i, 0, 0))
    return pl.pallas_call(
        pick_kernel,
        name="pick_rows",
        grid=(pairs,),
        out_shape=(out, out),
        in_specs=[
            pl.BlockSpec((8, 128), lambda i: (0, 0)),
            pl.BlockSpec((2, 128, full), lambda i: (i, 0, 0)),
        ],
        out_specs=[spec, spec],
        compiler_params=pltpu.CompilerParams(vmem_limit_bytes=40 << 20),
    )(sel, src)


def fold_kernel(p0, p1, p2, p3, out, ss, rs, ls, ra, rb, rc, rd, re, rf, rg, acc_x, acc_y):
    p = Place()
    dp, yl, x = p.dp, p.yl, p.x
    greet([p.ZR, p.ZL, p.XR, p.XL, p.Y])
    wire = Wire(ss, rs)

    def added(dst, *srcs):
        total = srcs[0][...].astype(f32)
        for src in srcs[1:]:
            total = total + src[...].astype(f32)
        dst[...] = total.astype(dst.dtype)

    def loop(count, body):
        def step(i, carry):
            body(i)
            return carry

        lax.fori_loop(0, count, step, 0)

    firsts = []
    for i, part in ((2, p2), (3, p3)):
        firsts.append(wire.send(part.at[:, 1 - yl], rb.at[i - 2], p.Y))
    starts = []
    for i, part in ((0, p0), (1, p1)):
        starts.append(
            (
                wire.send(part.at[0:2, :, p.xo], ra.at[i, 0], p.XR),
                wire.send(part.at[2:4, :, p.xo], ra.at[i, 1], p.XL),
            )
        )
    seconds = []
    for i, part in ((0, p0), (1, p1)):
        one, two = starts[i]
        one.wait_recv()
        loop(2, lambda d: added(part.at[d, :, p.xr], part.at[d, :, p.xr], ra.at[i, 0, d]))
        s1 = wire.send(part.at[:, :, p.xr], rc.at[i, 0], p.XR)
        two.wait_recv()
        loop(2, lambda d: added(part.at[d + 2, :, p.xl], part.at[d + 2, :, p.xl], ra.at[i, 1, d]))
        s2 = wire.send(part.at[:, :, p.xl], rc.at[i, 1], p.XL)
        seconds.append((s1, s2))
    mids = []
    for i, part in ((2, p2), (3, p3)):
        firsts[i - 2].wait_recv()
        loop(4, lambda d: added(acc_y.at[i - 2, d], part.at[d, yl], rb.at[i - 2, d]))
        acc = acc_y.at[i - 2]
        mids.append(
            (
                wire.send(acc.at[0:2, p.xo], rd.at[i - 2, 0], p.XR),
                wire.send(acc.at[2:4, p.xo], rd.at[i - 2, 1], p.XL),
            )
        )
    yends = []
    for i, part in ((0, p0), (1, p1)):
        for s in seconds[i]:
            s.wait_recv()
        acc = acc_x.at[i]
        loop(4, lambda d: added(acc.at[d], part.at[d, :, x], rc.at[i, 0, d], rc.at[i, 1, d]))
        yends.append(wire.send(acc.at[:, 1 - yl], re.at[i], p.Y))
    xends = []
    for i in (2, 3):
        acc = acc_y.at[i - 2]
        one, two = mids[i - 2]
        one.wait_recv()
        loop(2, lambda d: added(acc.at[d, p.xr], acc.at[d, p.xr], rd.at[i - 2, 0, d]))
        s1 = wire.send(acc.at[:, p.xr], rf.at[i - 2, 0], p.XR)
        two.wait_recv()
        loop(2, lambda d: added(acc.at[d + 2, p.xl], acc.at[d + 2, p.xl], rd.at[i - 2, 1, d]))
        s2 = wire.send(acc.at[:, p.xl], rf.at[i - 2, 1], p.XL)
        xends.append((s1, s2))
    parts = []
    zs = []

    def z_first(i, acc):
        parts.append(acc)
        zs.append(
            (
                wire.send(acc.at[p.zo, 0:32], rg.at[i, 0, 0:32], p.ZR),
                wire.send(acc.at[p.zo, 32:64], rg.at[i, 1, 0:32], p.ZL),
            )
        )

    for i in (0, 1):
        yends[i].wait_recv()
        acc = acc_x.at[i]
        loop(4, lambda d: added(acc.at[d, yl], acc.at[d, yl], re.at[i, d]))
        z_first(i, acc.at[:, yl])
    for i in (2, 3):
        for s in xends[i - 2]:
            s.wait_recv()
        acc = acc_y.at[i - 2]
        loop(
            4, lambda d: added(acc.at[d, x], acc.at[d, x], rf.at[i - 2, 0, d], rf.at[i - 2, 1, d])
        )
        z_first(i, acc.at[:, x])
    ends = []
    for i in range(4):
        one, two = zs[i]
        acc = parts[i]
        one.wait_recv()
        added(acc.at[p.zr, 0:32], acc.at[p.zr, 0:32], rg.at[i, 0, 0:32])
        s1 = wire.send(acc.at[p.zr], rg.at[i, 2], p.ZR)
        two.wait_recv()
        added(acc.at[p.zl, 32:64], acc.at[p.zl, 32:64], rg.at[i, 1, 0:32])
        s2 = wire.send(acc.at[p.zl], rg.at[i, 3], p.ZL)
        ends.append((s1, s2))
    for i in range(4):
        for s in ends[i]:
            s.wait_recv()
        added(out.at[i], parts[i].at[dp], rg.at[i, 2], rg.at[i, 3])
    wire.drain()


def fold_grads(grads):
    return remote_call(
        fold_kernel,
        "fold_grads",
        8,
        36,
        1,
        [VMEM] * 4,
        [VMEM],
        (shaped((4, 64, 512), f32),),
        scratch=[
            pltpu.VMEM((2, 2, 2, 2, 64, 512), bf16),
            pltpu.VMEM((2, 4, 4, 64, 512), bf16),
            pltpu.VMEM((2, 2, 4, 2, 64, 512), bf16),
            pltpu.VMEM((2, 2, 2, 64, 512), bf16),
            pltpu.VMEM((2, 4, 64, 512), bf16),
            pltpu.VMEM((2, 2, 4, 64, 512), bf16),
            pltpu.VMEM((4, 4, 64, 512), bf16),
            pltpu.VMEM((2, 4, 2, 64, 512), bf16),
            pltpu.VMEM((2, 4, 4, 64, 512), bf16),
        ],
        vmem=48 << 20,
    )(*[g.reshape(4, 2, 4, 64, 512) for g in grads])[0]


def on_device(
    tokens,
    segment_ids,
    valid_mask,
    routes,
    attn_gain,
    w_query,
    w_key,
    w_value,
    w_out,
    query_gain,
    key_gain,
    ffn_gain,
    router,
    expert_in,
    expert_out,
    cotangent,
):
    blk = lax.axis_index("blk")
    device = lax.axis_index("head") * 8 + blk
    yl = blk // 4
    tok, width = tokens.shape
    full_in = lax.all_gather(expert_in, "dp", axis=0, tiled=True)
    full_back = lax.all_gather(expert_out, "dp", axis=0, tiled=True)

    segment, valid = segment_ids[0], valid_mask[0]
    seq_len = segment.shape[0]
    place = jnp.arange(seq_len, dtype=i32)
    query_ids = (jnp.arange(4)[:, None] * 1024 + blk * 128 + jnp.arange(128)[None]).reshape(-1)
    frequency = rope_base ** (-jnp.arange(64, dtype=f32) / 64)
    angles = query_ids.astype(f32)[:, None] * frequency[None]
    cosine, sine = jnp.cos(angles)[None], jnp.sin(angles)[None]
    half_ids = (jnp.arange(4)[:, None] * 1024 + yl * 512 + jnp.arange(512)[None]).reshape(-1)
    half_seg = lax.dynamic_index_in_dim(segment.reshape(4, 2, 512), yl, 1, keepdims=False).reshape(-1)
    key_seg = jnp.where(valid > 0, segment, -1)
    ends = half_seg.reshape(-1, QB)
    lower = jnp.sum(segment[None] < ends[:, :1], axis=1, dtype=i32) // KB
    upper = (jnp.sum(segment[None] <= ends[:, -1:], axis=1, dtype=i32) + KB - 1) // KB
    limits = jnp.stack([lower, upper])

    def rotary(values, turning):
        a, b = values[..., :64], values[..., 64:]
        turned = turning * sine
        return jnp.concatenate([a * cosine - b * turned, b * cosine + a * turned], axis=-1)

    inputs = tokens.astype(f32)
    first_inv = rms_rows(inputs)
    normed = (inputs * first_inv * attn_gain).astype(bf16)
    w_three = jnp.stack([w_query, w_key, w_value])
    gathered, out_part, normed_all = gather_weights(w_three, w_out, normed)
    full_query, full_key, full_value = (gathered[i].reshape(2048, 512) for i in range(3))
    normed_all = normed_all.reshape(512, width)

    def by_head(flat):
        return jnp.transpose(flat.reshape(512, 4, HD), (1, 0, 2))

    def flat_of(heads):
        return jnp.transpose(heads.reshape(4, 512, HD), (1, 0, 2)).reshape(512, 512)

    query_proj = by_head(jnp.dot(normed_all, full_query, preferred_element_type=f32))
    key_proj = by_head(jnp.dot(normed_all, full_key, preferred_element_type=f32))
    value_heads = by_head(jnp.dot(normed_all, full_value, preferred_element_type=f32).astype(bf16))
    query_inv = rms_rows(query_proj)
    query_unit = query_proj * query_inv
    query_heads = rotary(query_unit * query_gain, 1.0).astype(bf16)
    key_inv = rms_rows(key_proj)
    key_unit = key_proj * key_inv
    key_heads = rotary(key_unit * key_gain, 1.0).astype(bf16)

    runs = (4, 4, 128, HD)
    q, k, v, full_out = heads_over_x(
        query_heads.reshape(runs), key_heads.reshape(runs), value_heads.reshape(runs), out_part
    )
    q, k, v = q.reshape(2048, HD), k.reshape(4096, HD), v.reshape(4096, HD)
    full_out = full_out.reshape(2048, 512)
    att_low, att, inverse = attend(limits, q, k, v, half_seg, half_ids, key_seg)
    attended = back_over_x(att_low.reshape(runs))
    attended_flat = flat_of(attended)
    branch_part = jnp.einsum("qc,mc->qm", attended_flat, full_out, preferred_element_type=f32)
    middle = inputs + sum_rows(branch_part.astype(bf16), 9)
    second_inv = rms_rows(middle)
    normed_ffn = (middle * second_inv * ffn_gain).astype(bf16)
    logits = jnp.dot(normed_ffn, router, preferred_element_type=f32)
    probabilities = jax.nn.softmax(logits, axis=-1)

    expert_ids = jnp.arange(EXPERTS, dtype=i32)
    hot = jnp.sum((routes[..., None] == expert_ids).astype(f32), axis=1)
    before = (jnp.arange(tok)[:, None] > jnp.arange(tok)[None]).astype(bf16)
    slots = jnp.dot(before, hot.astype(bf16), preferred_element_type=f32)
    slot_code = jnp.where(hot > 0, slots, -1.0)
    chosen = probabilities * hot
    gate_total = jnp.sum(chosen, axis=-1, keepdims=True)
    gates = chosen / gate_total

    sent = jnp.concatenate(
        [normed_ffn, cotangent, slot_code.astype(bf16), gates.astype(bf16)], axis=1
    )
    everyone = spread(sent)
    lane = jnp.arange(128)[None]
    sel_row = jnp.arange(8)[:, None]
    sel = (
        (sel_row < 4) & (lane == (sel_row // 2) * EXPERTS + device * EXP_DEV + sel_row % 2)
    ).astype(bf16)
    expert_rows, arrived_grads = pick_rows(sel, everyone, width)
    expert_rows = expert_rows.reshape(EXP_DEV, -1, width)
    arrived_grads = arrived_grads.reshape(EXP_DEV, -1, width)

    gate_up = jnp.einsum("erd,def->erf", expert_rows, full_in, preferred_element_type=f32)
    gate_part, up_part = gate_up[..., :FF], gate_up[..., FF:]
    sigmoid_gate = jax.nn.sigmoid(gate_part)
    silu_gate = gate_part * sigmoid_gate
    hidden = (silu_gate * up_part).astype(bf16)
    expert_result = jnp.einsum(
        "erf,def->erd", hidden, full_back, preferred_element_type=f32
    ).astype(bf16)

    def home(rows):
        rows = rows.reshape(EXP_DEV, 32, CAP, width)
        moved = lax.all_to_all(rows, ("head", "blk"), split_axis=1, concat_axis=1, tiled=True)
        return moved.reshape(EXP_DEV * 32 * CAP, width)

    returned = home(expert_result)
    term_back = jnp.einsum("erc,erf->ecf", arrived_grads, hidden, preferred_element_type=f32)
    grad_hidden = jnp.einsum("erd,def->erf", arrived_grads, full_back, preferred_element_type=f32)
    grad_gate = grad_hidden * up_part * sigmoid_gate * (1.0 + gate_part * (1.0 - sigmoid_gate))
    grad_up = grad_hidden * silu_gate
    grad_gate_up = jnp.concatenate([grad_gate, grad_up], axis=-1).astype(bf16)
    grad_rows = jnp.einsum(
        "erf,def->erd", grad_gate_up, full_in, preferred_element_type=f32
    ).astype(bf16)
    back_rows = home(grad_rows)
    term_in = jnp.einsum("erc,erf->ecf", expert_rows, grad_gate_up, preferred_element_type=f32)

    def fold_dp(term):
        return lax.psum_scatter(term.astype(bf16), "dp", scatter_dimension=1, tiled=True)

    expert_out_grad = jnp.transpose(fold_dp(term_back), (1, 0, 2)).astype(f32)
    expert_in_grad = jnp.transpose(fold_dp(term_in), (1, 0, 2)).astype(f32)

    code = jnp.transpose(slot_code.reshape(tok, 32, EXP_DEV), (0, 2, 1))
    home_hot = code[..., None] == jnp.arange(CAP, dtype=f32)
    home_gate = jnp.transpose(gates.reshape(tok, 32, EXP_DEV), (0, 2, 1))[..., None]
    flat_hot = home_hot.reshape(tok, -1)
    mixture = jnp.dot(
        jnp.where(home_hot, home_gate, 0.0).astype(bf16).reshape(tok, -1),
        returned,
        preferred_element_type=f32,
    )
    output = (middle + mixture).astype(bf16)
    grad_out = cotangent.astype(f32)
    dots = jnp.einsum("td,rd->tr", cotangent, returned, preferred_element_type=f32)
    grad_gates = jnp.sum(jnp.where(flat_hot, dots, 0.0).reshape(tok, EXP_DEV, 32, CAP), axis=-1)
    grad_gates = jnp.transpose(grad_gates, (0, 2, 1)).reshape(tok, EXPERTS)
    mean_grad = jnp.sum(grad_gates * gates, axis=-1, keepdims=True)
    grad_probs = (grad_gates - mean_grad) / gate_total * hot
    grad_logits = probabilities * (
        grad_probs - jnp.sum(probabilities * grad_probs, axis=-1, keepdims=True)
    )
    router_term = jnp.dot(normed_ffn.astype(f32).T, grad_logits, precision=highest)
    grad_ffn = jnp.dot(
        flat_hot.astype(bf16), back_rows, preferred_element_type=f32
    ) + jnp.dot(grad_logits, router.astype(f32).T, precision=highest)
    ffn_gain_term = jnp.sum(grad_ffn * middle * second_inv, axis=0)
    grad_middle = grad_out + rms_back(middle, second_inv, grad_ffn * ffn_gain)
    grad_branch = grad_middle.astype(bf16)
    branch_all = gather_rows(grad_branch).reshape(512, width)
    grad_att = by_head(
        jnp.dot(branch_all, full_out, preferred_element_type=f32).astype(bf16)
    )
    grad_att = go_over_x(grad_att.reshape(runs)).reshape(2048, HD)
    delta = jnp.sum(grad_att.astype(f32) * att, axis=-1)
    dq, dk, dv = attend_back(
        limits, q, k, v, grad_att, half_seg, half_ids, key_seg, inverse[:, 0], delta
    )
    cut = (4, 2, 4, 128, HD)
    grad_query, grad_key, grad_value = grads_over_x(
        dq.reshape(runs), dk.reshape(cut), dv.reshape(cut)
    )
    heads_shape = (4, 512, HD)
    grad_query_unit = rotary(grad_query.reshape(heads_shape).astype(f32), -1.0)
    query_gain_term = jnp.sum(grad_query_unit * query_unit, axis=(0, 1))
    grad_query_flat = flat_of(
        rms_back(query_proj, query_inv, grad_query_unit * query_gain).astype(bf16)
    )
    grad_key_unit = rotary(grad_key.reshape(heads_shape).astype(f32), -1.0)
    key_gain_term = jnp.sum(grad_key_unit * key_unit, axis=(0, 1))
    grad_key_flat = flat_of(rms_back(key_proj, key_inv, grad_key_unit * key_gain).astype(bf16))
    grad_value_flat = flat_of(grad_value)
    normed_part = jnp.einsum("qc,dc->qd", grad_query_flat, full_query, preferred_element_type=f32)
    normed_part += jnp.einsum("qc,dc->qd", grad_key_flat, full_key, preferred_element_type=f32)
    normed_part += jnp.einsum("qc,dc->qd", grad_value_flat, full_value, preferred_element_type=f32)
    grad_normed = sum_rows(normed_part.astype(bf16), 10)
    attn_gain_term = jnp.sum(grad_normed * inputs * first_inv, axis=0)
    input_grad = grad_middle + rms_back(inputs, first_inv, grad_normed * attn_gain)

    def weight_grad(rows, grads):
        return jnp.einsum("qc,qf->cf", rows, grads, preferred_element_type=f32).astype(bf16)

    attn_grads = fold_grads(
        [
            weight_grad(normed_all, grad_query_flat),
            weight_grad(normed_all, grad_key_flat),
            weight_grad(normed_all, grad_value_flat),
            weight_grad(branch_all, attended_flat),
        ]
    )
    summed = lax.psum(
        (attn_gain_term, ffn_gain_term, query_gain_term, key_gain_term, router_term),
        ("dp", "head", "blk"),
    )
    return (
        output,
        input_grad,
        summed[0],
        attn_grads[0],
        attn_grads[1],
        attn_grads[2],
        attn_grads[3],
        summed[2],
        summed[3],
        summed[1],
        summed[4],
        expert_in_grad,
        expert_out_grad,
    )


def solution(mesh):
    placed = (
        P(("dp", "head", "blk"), None),
        P("dp", None),
        P("dp", None),
        P(("dp", "head", "blk"), None),
        P(),
        P(("dp", "blk"), "head"),
        P(("dp", "blk"), "head"),
        P(("dp", "blk"), "head"),
        P(("dp", "blk"), "head"),
        P(),
        P(),
        P(),
        P(),
        P("dp", ("head", "blk"), None),
        P("dp", ("head", "blk"), None),
        P(("dp", "head", "blk"), None),
    )
    return jax.shard_map(
        on_device,
        mesh=mesh,
        in_specs=placed,
        out_specs=(
            P(("dp", "head", "blk"), None),
            P(("dp", "head", "blk"), None),
            P(),
            P(("dp", "blk"), "head"),
            P(("dp", "blk"), "head"),
            P(("dp", "blk"), "head"),
            P(("dp", "blk"), "head"),
            P(),
            P(),
            P(),
            P(),
            P("dp", ("head", "blk"), None),
            P("dp", ("head", "blk"), None),
        ),
        check_vma=False,
    )
```

time: 2000 us -> 997 us (0.50)
  waiting for transfers between devices: 1310 us -> 171 us
  Pallas kernels: 0 us -> 453 us
  matrix products: 250 us -> 151 us
  other arithmetic: 124 us -> 31.5 us
  local copies, waits for them, and re-layouts: 186 us -> 94.2 us
    all_gather x10 -> x2, waiting for transfers between devices: 698 us -> 0.01 us  [the longest x1 0.01 us: on_device(): full_in = lax.all_gather(expert_in, 'dp', axis=0, tiled=True)]
    pallas_call x0 -> x13, Pallas kernels: none -> 453 us  [the longest x1 117 us: spread(): remote_call(spread_kernel, 'spread', 7, 26, 1, [ANY], [ANY], (shaped((2,...]
    reduce_scatter x5 -> x2, waiting for transfers between devices: 308 us -> 0.01 us  [fold_dp(): lax.psum_scatter(term.astype(bf16), 'dp', scatter_dimension=1, tiled=True)]
    all_to_all x4 -> x2, waiting for transfers between devices: 239 us -> 121 us  [home(): lax.all_to_all(rows, ('head', 'blk'), split_axis=1, concat_axis=1, tiled=...]
    dot_general x64 -> x12, matrix products: 167 us -> 71.3 us  [the longest x1 20.7 us: on_device(): jnp.einsum('erc,erf->ecf', expert_rows, grad_gate_up, preferred_element_t...]
    unnamed x18 -> x5, waiting for transfers between devices: 62.1 us -> 0.08 us
    psum x1, waiting for transfers between devices: 0.01 us -> 49.2 us  [on_device(): lax.psum((attn_gain_term, ffn_gain_term, query_gain_term, key_gain_term,...]
    concatenate x4 -> x2, other arithmetic: 33.9 us -> 4.45 us  [rotary(): jnp.concatenate([a * cosine - b * turned, b * cosine + a * turned], axis=-1)]
  transfers between devices with their start and end apart: 21 -> 7, of which waited for: 17 -> 3; matrix products, arithmetic and copies ran while one was open for 19% -> 22% of each run, Pallas kernels for 0% -> 46%
where the time goes in v1:
time: 997 us; the launch traced here: 989 us
  Pallas kernels  453 us (45%)
  waiting for transfers between devices  171 us (17%)
  matrix products  151 us (15%)
  local copies, waits for them, and re-layouts  94.2 us (9%)
  blocking collectives  63.1 us (6%)
  other arithmetic  31.5 us (3%)
  between operations  15.4 us (2%)
  starting transfers between devices  10.6 us (1%)
    all_to_all x2, waiting for transfers between devices, home(): lax.all_to_all(rows, ('head', 'blk'), split_axis=1, concat_axis=1, tiled=...  121 us
    pallas_call x1, Pallas kernels, spread(): remote_call(spread_kernel, 'spread', 7, 26, 1, [ANY], [ANY], (shaped((2,...  117 us
    pallas_call x1, Pallas kernels, fold_grads(): remote_call(fold_kernel, 'fold_grads', 8, 36, 1, [VMEM] * 4, [VMEM], (sha...  83.7 us
    pallas_call x1, Pallas kernels, gather_weights(): remote_call(weights_kernel, 'gather_weights', 1, 24, 3, [ANY] * 3, [ANY]...  68.5 us
    psum x1, blocking collectives, on_device(): lax.psum((attn_gain_term, ffn_gain_term, query_gain_term, key_gain_term,...  63.1 us
    unnamed x197, local copies, waits for them, and re-layouts  51.2 us
    psum x1, waiting for transfers between devices, on_device(): lax.psum((attn_gain_term, ffn_gain_term, query_gain_term, key_gain_term,...  49.2 us
    pallas_call x1, Pallas kernels, heads_over_x(): remote_call(heads_kernel, 'heads_over_x', 3, 22, 4, [ANY] * 4, [ANY] * 4,...  38.4 us
  transfers between devices with their start and end apart: 7, of which 3 were waited for; matrix products, arithmetic and copies ran while one was open for 22% of the time, Pallas kernels for 46%

profile of v1, /device:TPU:0, one launch (start us, length us, event | category | flops | bytes accessed | tf_op | source)
XLA Modules:
  0.0 989.4 jit_solution(13751890771453331059)
XLA Ops:
  20.9 68.5 %gather_weights.1 = (bf16[3,4,2,4,64,512]{5,4,3,2,1,0:T(8,128)(2,1)}, bf16[4,64,512]{2,1,0:T(8,128)(2,1)}, bf16[4,128,2048]{2,1,0:T(8,128)(2,1)}) custom-call(bf16[3,64,512]{2,1,0:T(8,128)(2,1)} %pad_maximum_fusion.7.w, bf16[64,512]{1,0:T(8,128)(2,1)} %wo.1, bf16[128,2048]{1,0:T(8,128)(2,1)} %fusion.20.n), custom_call_target="tpu_custom_call" | custom-call | tf_op jit(solution)/shard_map/gather_weights/pallas_call | solution.py:182
  122.0 38.4 %heads_over_x.1 = (bf16[4,4,128,128]{3,2,1,0:T(8,128)(2,1)}, bf16[4,2,4,128,128]{4,3,2,1,0:T(8,128)(2,1)}, bf16[4,2,4,128,128]{4,3,2,1,0:T(8,128)(2,1)}, bf16[4,2,4,64,512]{4,3,2,1,0:T(8,128)(2,1)}) custom-call(bf16[4,4,128,128]{3,2,1,0:T(8,128)(2,1)} %pad_maximum_fusion.5.q, bf16[4,4,128,128]{3,2,1,0:T(8,128)(2,1)} %pad_maximum_fusion.6.k, ...), custom_call_target="tpu_custom_call" | custom-call | tf_op jit(solution)/shard_map/heads_over_x/pallas_call | solution.py:312
  164.4 12.3 %attend.1 = (bf16[2048,128]{1,0:T(8,128)(2,1)S(1)}, f32[2048,128]{1,0:T(8,128)S(1)}, f32[2048,128]{1,0:T(8,128)S(1)}) custom-call(s32[2,8]{1,0:T(2,128)S(1)} %pad_add_fusion.lim, bf16[2048,128]{1,0:T(8,128)(2,1)S(1)} %bitcast.202, bf16[4096,128]{1,0:T(8,128)(2,1)S(1)} %bitcast.195, bf16[4096,128]{1,0:T(8,128)(2,1)S(1)} %bitcast.197, ...), custom_call_target="tpu_custom_call" | custom-call | tf_op jit(solution)/shard_map/attend/pallas_call | solution.py:470
  178.4 8.3 back_over_x.1
  191.3 16.7 %sum_rows.2 = f32[128,2048]{1,0:T(8,128)S(1)} custom-call(bf16[2,2,128,2048]{3,2,1,0:T(8,128)(2,1)S(1)} %bitcast.201), custom_call_target="tpu_custom_call" | custom-call | tf_op jit(solution)/shard_map/sum_rows/pallas_call | solution.py:250
  215.6 116.8 %spread.1 = bf16[2,2,2,4,128,4224]{5,4,3,2,1,0:T(8,128)(2,1)} custom-call(bf16[128,4224]{1,0:T(8,128)(2,1)} %concatenate.37.src), custom_call_target="tpu_custom_call" | custom-call | tf_op jit(solution)/shard_map/spread/pallas_call | solution.py:618
  332.5 23.1 %pick_rows.1 = (bf16[2,16,48,2048]{3,2,1,0:T(8,128)(2,1)S(1)}, bf16[2,16,48,2048]{3,2,1,0:T(8,128)(2,1)S(1)}) custom-call(bf16[8,128]{1,0:T(8,128)(2,1)S(1)} %fusion.38.sel, bf16[32,128,4224]{2,1,0:T(8,128)(2,1)} %bitcast.221), custom_call_target="tpu_custom_call" | custom-call | tf_op jit(solution)/shard_map/pick_rows/pallas_call | solution.py:655
  361.1 21.3 %fusion.60 = f32[2,768,2048]{2,1,0:T(8,128)} fusion(bf16[2,768,2048]{2,1,0:T(8,128)(2,1)} %bitcast.215, bf16[2048,2,2048]{2,0,1:T(8,128)(2,1)} %all-gather.3.cloned.1.call-done), kind=kOutput, calls=%fused_computation.166 | convolution fusion | flops 12884901888 | bytes 35651584 | tf_op jit(solution)/shard_map/erd,def->erf/dot_general | solution.py:913
  382.4 18.7 %multiply_convert_fusion.1 = (bf16[2,768,1024]{2,1,0:T(8,128)(2,1)}, bf16[2,768,1024]{2,1,0:T(8,128)(2,1)}, bf16[2,768,1024]{2,1,0:T(8,128)(2,1)}) fusion(f32[2,768,2048]{2,1,0:T(8,128)} %fusion.60, bf16[2,768,2048]{2,1,0:T(8,128)(2,1)} %bitcast.217, bf16[2048,2,1024]{2,0,1:T(8,128)(2,1)} %all-gather.5.cloned.1.call-done), kind=kOutput, calls=%fused_computation.8 | convolution fusion | flops 6466043904 | bytes 36700160 | tf_op jit(solution)/shard_map/erd,def->erf/dot_general | solution.py:929
  401.1 10.9 %convolution_convert_fusion.1 = bf16[2,2048,1024]{2,1,0:T(8,128)(2,1)} fusion(bf16[2,768,2048]{2,1,0:T(8,128)(2,1)S(1)} %bitcast.220, bf16[2,768,1024]{2,1,0:T(8,128)(2,1)} %get-tuple-element.155), kind=kOutput, calls=%fused_computation.12 | convolution fusion | flops 6446645248 | bytes 17825792 | tf_op jit(solution)/shard_map/erc,erf->ecf/dot_general | solution.py:928
  412.1 20.7 %convolution_convert_fusion = bf16[2,2048,2048]{2,1,0:T(8,128)(2,1)} fusion(bf16[2,768,2048]{2,1,0:T(8,128)(2,1)} %bitcast.216, bf16[2,768,1024]{2,1,0:T(8,128)(2,1)} %get-tuple-element.154, bf16[2,768,1024]{2,1,0:T(8,128)(2,1)} %get-tuple-element.153), kind=kOutput, calls=%fused_computation | convolution fusion | flops 12905873408 | bytes 29360128 | tf_op jit(solution)/shard_map/erc,erf->ecf/dot_general | solution.py:937
  432.8 10.9 %convolution_convert_fusion.2 = bf16[2,768,2048]{2,1,0:T(8,128)(2,1)S(1)} fusion(bf16[2,768,1024]{2,1,0:T(8,128)(2,1)} %get-tuple-element.155, bf16[2048,2,1024]{2,0,1:T(8,128)(2,1)} %all-gather.5.cloned.1.call-done), kind=kOutput, calls=%fused_computation.13 | convolution fusion | flops 6445596672 | bytes 17825792 | tf_op jit(solution)/shard_map/erf,def->erd/dot_general | solution.py:918
  452.2 19.9 %convolution_convert_fusion.3 = bf16[2,768,2048]{2,1,0:T(8,128)(2,1)} fusion(bf16[2048,2,2048]{2,0,1:T(8,128)(2,1)} %all-gather.3.cloned.1.call-done, bf16[2,768,1024]{2,1,0:T(8,128)(2,1)} %get-tuple-element.154, bf16[2,768,1024]{2,1,0:T(8,128)(2,1)} %get-tuple-element.153), kind=kOutput, calls=%fused_computation.14 | convolution fusion | flops 12900630528 | bytes 29360128 | tf_op jit(solution)/shard_map/erf,def->erd/dot_general | solution.py:933
  478.8 53.0 %all-to-all-done = bf16[2,32,24,2048]{3,2,0,1:T(8,128)(2,1)} async-done(((bf16[2,32,24,2048]{3,2,0,1:T(8,128)(2,1)}), bf16[2,32,24,2048]{3,2,0,1:T(8,128)(2,1)}, u32[]{:S(2)}, u32[]{:S(2)}) %all-to-all-start) | async-done | bytes 6291488 | tf_op jit(solution)/shard_map/all_to_all | solution.py:924
  547.9 68.3 %all-to-all-done.1 = bf16[2,32,24,2048]{3,2,0,1:T(8,128)(2,1)} async-done(((bf16[2,32,24,2048]{3,2,0,1:T(8,128)(2,1)}), bf16[2,32,24,2048]{3,2,0,1:T(8,128)(2,1)}, u32[]{:S(2)}, u32[]{:S(2)}) %all-to-all-start.1) | async-done | bytes 6291488 | tf_op jit(solution)/shard_map/all_to_all | solution.py:924
  626.1 17.0 %gather_rows.1 = bf16[4,128,2048]{2,1,0:T(8,128)(2,1)} custom-call(bf16[128,2048]{1,0:T(8,128)(2,1)} %fusion.50.n), custom_call_target="tpu_custom_call" | custom-call | tf_op jit(solution)/shard_map/gather_rows/pallas_call | solution.py:211
  649.7 10.1 %go_over_x.1 = bf16[4,4,128,128]{3,2,1,0:T(8,128)(2,1)} custom-call(bf16[4,4,128,128]{3,2,1,0:T(8,128)(2,1)} %bitcast.249), custom_call_target="tpu_custom_call" | custom-call | tf_op jit(solution)/shard_map/go_over_x/pallas_call | solution.py:362
  664.8 15.8 %attend_back.1 = (bf16[2048,128]{1,0:T(8,128)(2,1)S(1)}, bf16[4096,128]{1,0:T(8,128)(2,1)S(1)}, bf16[4096,128]{1,0:T(8,128)(2,1)S(1)}) custom-call(s32[2,8]{1,0:T(2,128)S(1)} %copy-done.15, bf16[2048,128]{1,0:T(8,128)(2,1)S(1)} %bitcast.203, bf16[4096,128]{1,0:T(8,128)(2,1)S(1)} %bitcast.196, bf16[4096,128]{1,0:T(8,128)(2,1)S(1)} %bitcast.198, ...), custom_call_target="tpu_custom_call" | custom-call | tf_op jit(solution)/shard_map/attend_back/pallas_call | solution.py:531
  680.7 26.1 %grads_over_x.1 = (bf16[4,4,128,128]{3,2,1,0:T(8,128)(2,1)S(1)}, bf16[4,4,128,128]{3,2,1,0:T(8,128)(2,1)S(1)}, bf16[4,4,128,128]{3,2,1,0:T(8,128)(2,1)S(1)}) custom-call(bf16[4,4,128,128]{3,2,1,0:T(8,128)(2,1)S(1)} %bitcast.206, bf16[4,2,4,128,128]{4,3,2,1,0:T(8,128)(2,1)S(1)} %bitcast.204, bf16[4,2,4,128,128]{4,3,2,1,0:T(8,128)(2,1)S(1)} %bitcast.205), custom_call_target="tpu_custom_call" | custom-call | tf_op jit(solution)/shard_map/grads_over_x/pallas_call | solution.py:406
  725.1 16.5 %sum_rows.3 = f32[128,2048]{1,0:T(8,128)S(1)} custom-call(bf16[2,2,128,2048]{3,2,1,0:T(8,128)(2,1)S(1)} %bitcast.191), custom_call_target="tpu_custom_call" | custom-call | tf_op jit(solution)/shard_map/sum_rows/pallas_call | solution.py:250
  749.6 83.7 %fold_grads.1 = f32[4,64,512]{2,1,0:T(8,128)S(1)} custom-call(bf16[4,2,4,64,512]{4,3,2,1,0:T(8,128)(2,1)S(1)} %bitcast.199, bf16[4,2,4,64,512]{4,3,2,1,0:T(8,128)(2,1)S(1)} %bitcast.200, bf16[4,2,4,64,512]{4,3,2,1,0:T(8,128)(2,1)} %bitcast.235, bf16[4,2,4,64,512]{4,3,2,1,0:T(8,128)(2,1)} %bitcast.236), custom_call_target="tpu_custom_call" | custom-call | tf_op jit(solution)/shard_map/fold_grads/pallas_call | solution.py:782
  839.3 63.1 %all-reduce = (f32[2048]{0:T(1024)}, f32[128]{0:T(128)}, f32[128]{0:T(128)}, f32[2048]{0:T(1024)}) all-reduce(f32[2048]{0:T(1024)S(1)} %get-tuple-element.133, f32[128]{0:T(128)} %get-tuple-element.131, f32[128]{0:T(128)} %get-tuple-element.129, ...), channel_id=1, replica_groups=mesh['dp'=4,'head'=4,'blk'=8] {'dp','head','blk'}, use_global_device_ids=true, to_apply=%region_19.20 | all-reduce | flops 4352 | bytes 34816 | tf_op jit(solution)/shard_map/psum | solution.py:1012
  920.5 11.1 %copy.253 = f32[512,2,2048]{2,1,0:T(2,128)} copy(f32[512,2,2048]{2,0,1:T(8,128)S(1)} %convert_bitcast_fusion) | data formatting | bytes 16777216
  931.5 49.2 %all-reduce.3.cloned.1.call-done = f32[2048,64]{0,1:T(8,128)} async-done(((f32[2048,64]{0,1:T(8,128)}), f32[2048,64]{0,1:T(8,128)}) %all-reduce.3.cloned.1.call-update) | async-done | bytes 524304 | tf_op jit(solution)/shard_map/psum | solution.py:1012
  (317 shorter events, 173.4 us)
Async XLA Ops:
  7.2 202.6 %copy-start = (bf16[2048,64]{0,1:T(8,128)(2,1)S(1)}, bf16[2048,64]{0,1:T(8,128)(2,1)}, u32[]{:S(2)}) copy-start(bf16[2048,64]{0,1:T(8,128)(2,1)} %param.28) | copy-start | bytes 786436
  7.2 353.9 %all-gather.3.cloned.1.call-start = ((), (), s32[]{:S(2)}) async-start(), calls=%async_computation.4 | async-start | bytes 20971520 | tf_op jit(solution)/shard_map/all_gather | solution.py:828
  13.5 369.0 %all-gather.5.cloned.1.call-start = ((), (), s32[]{:S(2)}) async-start(), calls=%async_computation.5 | async-start | bytes 10485760 | tf_op jit(solution)/shard_map/all_gather | solution.py:829
  16.9 893.0 %reduce-scatter.5.cloned.1.call-start = ((), (), s32[]{:S(2)}) async-start(), calls=%async_computation.8 | async-start | bytes 10485760 | tf_op jit(solution)/shard_map/reduce_scatter | solution.py:940
  18.9 97.8 %copy-start.12 = (s32[4,1,512]{2,1,0:T(1,128)}, s32[4,1,512]{2,1,0:T(1,128)S(1)}, u32[]{:S(2)}) copy-start(s32[4,1,512]{2,1,0:T(1,128)S(1)} %get-tuple-element.152) | copy-start | bytes 24580
  208.2 124.2 %copy-start.45 = (f32[128,64]{1,0:T(8,128)}, f32[128,64]{1,0:T(8,128)S(1)}, u32[]{:S(2)}) copy-start(f32[128,64]{1,0:T(8,128)S(1)} %copy.223) | copy-start | bytes 98308
  209.5 122.9 %copy-start.18 = (f32[128,2048]{1,0:T(8,128)}, f32[128,2048]{1,0:T(8,128)S(1)}, u32[]{:S(2)}) copy-start(f32[128,2048]{1,0:T(8,128)S(1)} %get-tuple-element.150) | copy-start | bytes 3145732
  209.7 122.7 %copy-start.32 = (bf16[128,2048]{1,0:T(8,128)(2,1)}, bf16[128,2048]{1,0:T(8,128)(2,1)S(1)}, u32[]{:S(2)}) copy-start(bf16[128,2048]{1,0:T(8,128)(2,1)S(1)} %multiply_convert_fusion.3) | copy-start | bytes 1572868
  210.4 122.0 %copy-start.37 = (f32[128,64]{1,0:T(8,128)}, f32[128,64]{1,0:T(8,128)S(1)}, u32[]{:S(2)}) copy-start(f32[128,64]{1,0:T(8,128)S(1)} %copy.227) | copy-start | bytes 98308
  210.8 121.6 %copy-start.79 = (f32[128]{0:T(128)}, f32[128]{0:T(128)S(1)}, u32[]{:S(2)}) copy-start(f32[128]{0:T(128)S(1)} %get-tuple-element.147) | copy-start | bytes 1540
  412.1 505.2 %reduce-scatter.3.cloned.1.call-start = ((), (), s32[]{:S(2)}) async-start(), calls=%async_computation.7 | async-start | bytes 20971520 | tf_op jit(solution)/shard_map/reduce_scatter | solution.py:940
  446.9 84.8 %all-to-all-start = ((bf16[2,32,24,2048]{3,2,0,1:T(8,128)(2,1)}), bf16[2,32,24,2048]{3,2,0,1:T(8,128)(2,1)}, u32[]{:S(2)}, u32[]{:S(2)}) async-start(bf16[2,32,24,2048]{3,2,0,1:T(8,128)(2,1)} %copy.234), calls=%async_computation | async-start | bytes 12582912 | tf_op jit(solution)/shard_map/all_to_all | solution.py:924
  531.7 84.5 %all-to-all-start.1 = ((bf16[2,32,24,2048]{3,2,0,1:T(8,128)(2,1)}), bf16[2,32,24,2048]{3,2,0,1:T(8,128)(2,1)}, u32[]{:S(2)}, u32[]{:S(2)}) async-start(bf16[2,32,24,2048]{3,2,0,1:T(8,128)(2,1)} %copy.236), calls=%async_computation.1 | async-start | bytes 12582912 | tf_op jit(solution)/shard_map/all_to_all | solution.py:924
  536.6 444.1 %all-reduce.3.cloned.1.call-start = ((), (), s32[]{:S(2)}) async-start(), calls=%async_computation.6 | async-start | bytes 1048576 | tf_op jit(solution)/shard_map/psum | solution.py:1012
  749.5 83.8 %copy-start.25 = (bf16[128,2048]{1,0:T(8,128)(2,1)S(1)}, bf16[128,2048]{1,0:T(8,128)(2,1)}, u32[]{:S(2)}) copy-start(bf16[128,2048]{1,0:T(8,128)(2,1)} %param.16) | copy-start | bytes 1572868
  749.5 83.8 %copy-start.61 = (f32[2048]{0:T(1024)S(1)}, f32[2048]{0:T(1024)}, u32[]{:S(2)}) copy-start(f32[2048]{0:T(1024)} %param.20) | copy-start | bytes 24580
  749.5 83.8 %copy-start.78 = (f32[128]{0:T(128)S(1)}, f32[128]{0:T(128)}, u32[]{:S(2)}) copy-start(f32[128]{0:T(128)} %copy-done.77) | copy-start | bytes 1540
  749.5 85.4 %copy-start.33 = (bf16[128,2048]{1,0:T(8,128)(2,1)S(1)}, bf16[128,2048]{1,0:T(8,128)(2,1)}, u32[]{:S(2)}) copy-start(bf16[128,2048]{1,0:T(8,128)(2,1)} %copy-done.32) | copy-start | bytes 1572868
  749.5 85.4 %copy-start.48 = (f32[128,64]{1,0:T(8,128)S(1)}, f32[128,64]{1,0:T(8,128)}, u32[]{:S(2)}) copy-start(f32[128,64]{1,0:T(8,128)} %get-tuple-element.144) | copy-start | bytes 98308
  749.5 85.4 %copy-start.71 = (f32[128]{0:T(128)S(1)}, f32[128]{0:T(128)}, u32[]{:S(2)}) copy-start(f32[128]{0:T(128)} %copy-done.69) | copy-start | bytes 1540
  749.6 85.4 %copy-start.76 = (f32[128]{0:T(128)S(1)}, f32[128]{0:T(128)}, u32[]{:S(2)}) copy-start(f32[128]{0:T(128)} %copy-done.75) | copy-start | bytes 1540
  749.6 86.7 %copy-start.20 = (f32[128,2048]{1,0:T(8,128)S(1)}, f32[128,2048]{1,0:T(8,128)}, u32[]{:S(2)}) copy-start(f32[128,2048]{1,0:T(8,128)} %copy-done.18) | copy-start | bytes 3145732
  749.6 86.7 %copy-start.36 = (bf16[128,2048]{1,0:T(8,128)(2,1)S(1)}, bf16[128,2048]{1,0:T(8,128)(2,1)}, u32[]{:S(2)}) copy-start(bf16[128,2048]{1,0:T(8,128)(2,1)} %param.31) | copy-start | bytes 1572868
  749.6 86.7 %copy-start.74 = (f32[128]{0:T(128)S(1)}, f32[128]{0:T(128)}, u32[]{:S(2)}) copy-start(f32[128]{0:T(128)} %copy-done.72) | copy-start | bytes 1540
  (74 other events, 936.4 us)
Sparse Core Ops, SparseCore 0:
  13.5 159.5 all-gather.2
  174.8 82.2 all-gather.4
  412.2 79.6 reduce-scatter.4
  494.2 147.7 reduce-scatter.2
  839.4 141.2 all-reduce.2

commit v2 on v1

--- a/solution.py
+++ b/solution.py
@@ -18,7 +18,6 @@
 
 epsilon = 1e-06
 rope_base = 50000.0
-highest = lax.Precision.HIGHEST
 f32 = jnp.float32
 bf16 = jnp.bfloat16
 i32 = jnp.int32
@@ -53,7 +52,7 @@
         self.xr, self.xl, self.xo = (wrap4(self.x + s) for s in (1, -1, 2))
         y = self.yh * 2 + self.yl
         self.yr, self.ylf, self.yo = (wrap4(y + s) for s in (1, -1, 2))
-        self.ZR, self.ZL = {"dp": self.zr}, {"dp": self.zl}
+        self.ZR, self.ZL, self.ZO = {"dp": self.zr}, {"dp": self.zl}, {"dp": self.zo}
         self.XR, self.XL, self.XO = (self.to_x(v) for v in (self.xr, self.xl, self.xo))
         self.Y = {"blk": (1 - self.yl) * 4 + self.x}
         self.C = {"head": self.yh * 2 + (1 - self.co)}
@@ -613,12 +612,12 @@
     wire.drain()
 
 
-def spread(src):
+def spread(src, cid):
     width = src.shape[1]
     return remote_call(
         spread_kernel,
         "spread",
-        7,
+        cid,
         26,
         1,
         [ANY],
@@ -627,50 +626,225 @@
     )(src)[0].reshape(32, 128, width)
 
 
-def pick_kernel(sel, src, rows_out, grads_out):
-    width = rows_out.shape[-1]
-    tokens = jnp.concatenate([src[0, :, :width], src[1, :, :width]], axis=0)
-    cot = jnp.concatenate([src[0, :, width : 2 * width], src[1, :, width : 2 * width]], axis=0)
-    info = jnp.concatenate([src[0, :, 2 * width :], src[1, :, 2 * width :]], axis=0)
+def slot_hits(table, count, rows_down):
+    shape = (count * 2 * CAP, 256) if rows_down else (256, count * 2 * CAP)
+    line = lax.broadcasted_iota(i32, shape, 0 if rows_down else 1)
+    block = lax.broadcasted_iota(i32, shape, 1 if rows_down else 0) // 128
+    expert = line // (2 * CAP)
+    want = line - expert * (2 * CAP) - block * CAP
+
+    def spread_out(first):
+        value = jnp.zeros(shape, f32)
+        for e in range(count):
+            c = first + e
+            at = table[c : c + 1] if rows_down else table[:, c : c + 1]
+            value = jnp.where(expert == e, at, value)
+        return value
+
+    hit = (spread_out(0).astype(i32) == want) & (want >= 0) & (want < CAP)
+    return hit, spread_out(count)
+
+
+def pick_kernel(gated, sel, info, src, rows_out, *gates_out):
+    tokens = jnp.concatenate([src[0], src[1]], axis=0)
+    both = jnp.concatenate([info[0], info[1]], axis=0)
     table = lax.dot_general(
-        sel[...], info, (((1,), (1,)), ((), ())), preferred_element_type=f32
-    )
-    row = lax.broadcasted_iota(i32, (2 * CAP, 256), 0)
-    block = lax.broadcasted_iota(i32, (2 * CAP, 256), 1) // 128
-    want = row - block * CAP
+        sel[...], both, (((1,), (1,)), ((), ())), preferred_element_type=f32
+    )
+    hit, gate = slot_hits(table, EXP_DEV, True)
+    rows = jnp.dot(hit.astype(bf16), tokens, preferred_element_type=f32).astype(bf16)
     for e in range(EXP_DEV):
-        slot = jnp.broadcast_to(table[e : e + 1], (2 * CAP, 256)).astype(i32)
-        hit = (slot == want) & (want >= 0) & (want < CAP)
-        one = hit.astype(bf16)
-        gate = jnp.sum(jnp.where(hit, table[2 + e : 3 + e], 0.0), axis=1, keepdims=True)
-        rows_out[e, 0] = jnp.dot(one, tokens, preferred_element_type=f32).astype(bf16)
-        grads_out[e, 0] = (jnp.dot(one, cot, preferred_element_type=f32) * gate).astype(bf16)
-
-
-def pick_rows(sel, src, width):
-    blocks, _, full = src.shape
-    pairs = blocks // 2
-    out = shaped((EXP_DEV, pairs, 2 * CAP, width))
-    spec = pl.BlockSpec((EXP_DEV, 1, 2 * CAP, width), lambda i: (0, i, 0, 0))
+        rows_out[e, 0] = rows[e * 2 * CAP : (e + 1) * 2 * CAP]
+    if gated:
+        total = jnp.sum(jnp.where(hit, gate, 0.0), axis=1, keepdims=True)
+        total = jnp.broadcast_to(total, (EXP_DEV * 2 * CAP, 128))
+        for e in range(EXP_DEV):
+            gates_out[0][e, 0] = total[e * 2 * CAP : (e + 1) * 2 * CAP]
+
+
+def pick_rows(sel, info, src, width, gated):
+    pairs = src.shape[0] // 2
+
+    def spec(lanes):
+        return pl.BlockSpec((EXP_DEV, 1, 2 * CAP, lanes), lambda i: (0, i, 0, 0))
+
+    shapes = [shaped((EXP_DEV, pairs, 2 * CAP, width)), shaped((EXP_DEV, pairs, 2 * CAP, 128), f32)]
+    specs = [spec(width), spec(128)]
     return pl.pallas_call(
-        pick_kernel,
+        functools.partial(pick_kernel, gated),
         name="pick_rows",
         grid=(pairs,),
-        out_shape=(out, out),
+        out_shape=shapes[: 1 + gated],
         in_specs=[
             pl.BlockSpec((8, 128), lambda i: (0, 0)),
-            pl.BlockSpec((2, 128, full), lambda i: (i, 0, 0)),
+            pl.BlockSpec((2, 128, 128), lambda i: (i, 0, 0)),
+            pl.BlockSpec((2, 128, width), lambda i: (i, 0, 0)),
         ],
-        out_specs=[spec, spec],
+        out_specs=specs[: 1 + gated],
         compiler_params=pltpu.CompilerParams(vmem_limit_bytes=40 << 20),
-    )(sel, src)
-
-
-def fold_kernel(p0, p1, p2, p3, out, ss, rs, ls, ra, rb, rc, rd, re, rf, rg, acc_x, acc_y):
+    )(sel, info, src)
+
+
+HOME_SENDS = 18
+
+
+def home_scratch():
+    return [
+        pltpu.VMEM((2, 4, 8 * CAP, 2048), bf16),
+        pltpu.VMEM((2, 2, 4, 128, 2048), bf16),
+        pltpu.VMEM((2, 2, 64, 2048), bf16),
+        pltpu.VMEM((2, 2, 64, 2048), bf16),
+        pltpu.VMEM((2, 4, 64, 2048), bf16),
+        pltpu.VMEM((2, 2, 2, 64, 2048), bf16),
+        pltpu.VMEM((2, 2, 32, 2048), bf16),
+        pltpu.VMEM((2, 2, 64, 2048), bf16),
+    ]
+
+
+def home_steps(p, wire, sems, gated, sel, info, rows, out, cat, q, a1, b1, a2, b2, c1, c2):
+    yh, co, yl, x = p.yh, p.co, p.yl, p.x
+    ys = [(yy // 2, lax.rem(yy, 2)) for yy in (p.yr, p.ylf, p.yo)]
+    (rh, rl), (lh, ll), (oh, ol) = ys
+    own, first = [], []
+    for e in range(EXP_DEV):
+        lines = pl.ds(e * 2 * CAP, 2 * CAP)
+        there = pl.ds((2 + e) * 2 * CAP, 2 * CAP)
+        first.append(wire.send(rows.at[e, :, 1 - co], cat.at[:, :, there], p.C))
+        own.append(local(rows.at[e, :, co], cat.at[:, :, lines], sems.at[e]))
+    yield
+    for copy in own:
+        copy.wait()
+    for copy in first:
+        copy.wait_recv()
+
+    def place(i, carry):
+        h, pair = i // 4, lax.rem(i, 4)
+        block = h * 16 + co * 8 + pair * 2
+        both = jnp.concatenate([info[block], info[block + 1]], axis=0)
+        table = lax.dot_general(
+            both, sel[...], (((1,), (1,)), ((), ())), preferred_element_type=f32
+        )
+        hit, gate = slot_hits(table, 4, False)
+        value = jnp.where(hit, gate if gated else 1.0, 0.0).astype(bf16)
+        for c in range(0, 2048, 512):
+            total = jnp.dot(
+                value, cat[h, pair, :, c : c + 512], preferred_element_type=f32
+            ).astype(bf16)
+            at = lax.rem(pair, 2) * 2
+            q[h, pair // 2, at, :, c : c + 512] = total[:128]
+            q[h, pair // 2, at + 1, :, c : c + 512] = total[128:]
+        return carry
+
+    lax.fori_loop(0, 8, place, 0)
+    A, B = pl.ds(0, 64), pl.ds(64, 64)
+    s1 = [
+        wire.send(q.at[oh, ol, 0:2, A], a1.at[0], p.YR),
+        wire.send(q.at[0, :, p.xo, B], b1.at[0], p.XR),
+        wire.send(q.at[oh, ol, 2:4, A], a1.at[1], p.YL),
+        wire.send(q.at[1, :, p.xo, B], b1.at[1], p.XL),
+    ]
+    yield
+
+    def add(dst, *srcs):
+        total = srcs[0][...].astype(f32)
+        for src in srcs[1:]:
+            total = total + src[...].astype(f32)
+        dst[...] = total.astype(dst.dtype)
+
+    def loop(count, body):
+        def step(i, carry):
+            body(i)
+            return carry
+
+        lax.fori_loop(0, count, step, 0)
+
+    def plus(dst, src):
+        add(dst, dst, src)
+
+    s2 = []
+    s1[0].wait_recv()
+    loop(2, lambda i: plus(q.at[rh, rl, i, A], a1.at[0, i]))
+    s2.append(wire.send(q.at[rh, rl, :, A], a2.at[0], p.YR))
+    s1[1].wait_recv()
+    loop(2, lambda i: plus(q.at[0, i, p.xr, B], b1.at[0, i]))
+    s2.append(wire.send(q.at[:, :, p.xr, B], b2.at[0], p.XR))
+    s1[2].wait_recv()
+    loop(2, lambda i: plus(q.at[lh, ll, 2 + i, A], a1.at[1, i]))
+    s2.append(wire.send(q.at[lh, ll, :, A], a2.at[1], p.YL))
+    s1[3].wait_recv()
+    loop(2, lambda i: plus(q.at[1, i, p.xl, B], b1.at[1, i]))
+    s2.append(wire.send(q.at[:, :, p.xl, B], b2.at[1], p.XL))
+    yield
+    for copy in s2:
+        copy.wait_recv()
+    loop(4, lambda i: add(q.at[yh, yl, i, A], q.at[yh, yl, i, A], a2.at[0, i], a2.at[1, i]))
+    s3 = [
+        wire.send(q.at[yh, yl, p.xo, 0:32], c1.at[0, 0], p.XR),
+        wire.send(q.at[yh, yl, p.xo, 32:64], c1.at[0, 1], p.XL),
+    ]
+    for h in range(2):
+        loop(2, lambda i: add(q.at[h, i, x, B], q.at[h, i, x, B], b2.at[0, h, i], b2.at[1, h, i]))
+    s3 += [
+        wire.send(q.at[oh, ol, x, 64:96], c1.at[1, 0], p.YR),
+        wire.send(q.at[oh, ol, x, 96:128], c1.at[1, 1], p.YL),
+    ]
+    yield
+    s4 = []
+    s3[0].wait_recv()
+    plus(q.at[yh, yl, p.xr, 0:32], c1.at[0, 0])
+    s4.append(wire.send(q.at[yh, yl, p.xr, A], c2.at[0, 0], p.XR))
+    s3[1].wait_recv()
+    plus(q.at[yh, yl, p.xl, 32:64], c1.at[0, 1])
+    s4.append(wire.send(q.at[yh, yl, p.xl, A], c2.at[0, 1], p.XL))
+    s3[2].wait_recv()
+    plus(q.at[rh, rl, x, 64:96], c1.at[1, 0])
+    s4.append(wire.send(q.at[rh, rl, x, B], c2.at[1, 0], p.YR))
+    s3[3].wait_recv()
+    plus(q.at[lh, ll, x, 96:128], c1.at[1, 1])
+    s4.append(wire.send(q.at[lh, ll, x, B], c2.at[1, 1], p.YL))
+    yield
+    for copy in s4:
+        copy.wait_recv()
+    add(out.at[0:64], q.at[yh, yl, x, A], c2.at[0, 0], c2.at[0, 1])
+    add(out.at[64:128], q.at[yh, yl, x, B], c2.at[1, 0], c2.at[1, 1])
+    wire.drain()
+    yield
+
+
+def home_kernel(gated, sel, info, rows, out, ss, rs, ls, *scratch):
+    p = Place()
+    greet([p.XR, p.XL, p.YR, p.YL, p.C])
+    for _ in home_steps(p, Wire(ss, rs), ls, gated, sel, info, rows, out, *scratch):
+        pass
+
+
+def rows_home(sel, info, rows, gated, cid):
+    return remote_call(
+        functools.partial(home_kernel, gated),
+        "rows_home",
+        cid,
+        HOME_SENDS,
+        2,
+        [VMEM, VMEM, ANY],
+        [VMEM],
+        (shaped((128, 2048), f32),),
+        scratch=home_scratch(),
+        vmem=48 << 20,
+    )(sel, info, rows.reshape(EXP_DEV, 2, 2, 4, 2 * CAP, 2048))[0]
+
+
+def fold_kernel(
+    p0, p1, p2, p3, small, out, whole, ss, rs, ls,
+    ra, rb, rc, rd, re, rf, rg, acc_x, acc_y, sz, az, sx, ax, sy, ay, sc, ac, sh,
+):
     p = Place()
     dp, yl, x = p.dp, p.yl, p.x
-    greet([p.ZR, p.ZL, p.XR, p.XL, p.Y])
+    greet([p.ZR, p.ZL, p.ZO, p.XR, p.XL, p.XO, p.Y, p.C, p.H])
     wire = Wire(ss, rs)
+    zs_out = [
+        wire.send(small.at[there], sz.at[i], device)
+        for i, (there, device) in enumerate(((p.zo, p.ZO), (p.zr, p.ZR), (p.zl, p.ZL)))
+    ]
 
     def added(dst, *srcs):
         total = srcs[0][...].astype(f32)
@@ -706,6 +880,14 @@
         loop(2, lambda d: added(part.at[d + 2, :, p.xl], part.at[d + 2, :, p.xl], ra.at[i, 1, d]))
         s2 = wire.send(part.at[:, :, p.xl], rc.at[i, 1], p.XL)
         seconds.append((s1, s2))
+    for copy in zs_out:
+        copy.wait_recv()
+    for half in range(2):
+        az[half] = small[dp, half] + sz[0, half] + sz[1, half] + sz[2, half]
+    xs_out = [
+        wire.send(az.at[:, there], sx.at[i], device)
+        for i, (there, device) in enumerate(((p.xo, p.XO), (p.xr, p.XR), (p.xl, p.XL)))
+    ]
     mids = []
     for i, part in ((2, p2), (3, p3)):
         firsts[i - 2].wait_recv()
@@ -717,6 +899,10 @@
                 wire.send(acc.at[2:4, p.xo], rd.at[i - 2, 1], p.XL),
             )
         )
+    for copy in xs_out:
+        copy.wait_recv()
+    ax[...] = az[:, x] + sx[0] + sx[1] + sx[2]
+    y_out = wire.send(ax.at[1 - yl], sy, p.Y)
     yends = []
     for i, part in ((0, p0), (1, p1)):
         for s in seconds[i]:
@@ -724,6 +910,9 @@
         acc = acc_x.at[i]
         loop(4, lambda d: added(acc.at[d], part.at[d, :, x], rc.at[i, 0, d], rc.at[i, 1, d]))
         yends.append(wire.send(acc.at[:, 1 - yl], re.at[i], p.Y))
+    y_out.wait_recv()
+    ay[...] = ax[yl] + sy[...]
+    c_out = wire.send(ay, sc, p.C)
     xends = []
     for i in (2, 3):
         acc = acc_y.at[i - 2]
@@ -747,11 +936,17 @@
             )
         )
 
+    c_out.wait_recv()
+    ac[...] = ay[...] + sc[...]
+    h_out = wire.send(ac, sh, p.H)
     for i in (0, 1):
         yends[i].wait_recv()
         acc = acc_x.at[i]
         loop(4, lambda d: added(acc.at[d, yl], acc.at[d, yl], re.at[i, d]))
         z_first(i, acc.at[:, yl])
+    h_out.wait_recv()
+    whole[dp, yl, x] = ac[...] + sh[...]
+    y_all = wire.send(whole.at[dp, yl, x], whole.at[dp, yl, x], p.Y)
     for i in (2, 3):
         for s in xends[i - 2]:
             s.wait_recv()
@@ -760,6 +955,10 @@
             4, lambda d: added(acc.at[d, x], acc.at[d, x], rf.at[i - 2, 0, d], rf.at[i - 2, 1, d])
         )
         z_first(i, acc.at[:, x])
+    y_all.wait_recv()
+    x_all = [
+        wire.send(whole.at[dp, :, x], whole.at[dp, :, x], device) for device in (p.XO, p.XR, p.XL)
+    ]
     ends = []
     for i in range(4):
         one, two = zs[i]
@@ -771,23 +970,28 @@
         added(acc.at[p.zl, 32:64], acc.at[p.zl, 32:64], rg.at[i, 1, 0:32])
         s2 = wire.send(acc.at[p.zl], rg.at[i, 3], p.ZL)
         ends.append((s1, s2))
+    for copy in x_all:
+        copy.wait_recv()
+    z_all = [wire.send(whole.at[dp], whole.at[dp], device) for device in (p.ZO, p.ZR, p.ZL)]
     for i in range(4):
         for s in ends[i]:
             s.wait_recv()
         added(out.at[i], parts[i].at[dp], rg.at[i, 2], rg.at[i, 3])
+    for copy in z_all:
+        copy.wait_recv()
     wire.drain()
 
 
-def fold_grads(grads):
+def fold_grads(grads, small):
     return remote_call(
         fold_kernel,
         "fold_grads",
         8,
-        36,
+        52,
         1,
-        [VMEM] * 4,
-        [VMEM],
-        (shaped((4, 64, 512), f32),),
+        [VMEM] * 5,
+        [VMEM] * 2,
+        (shaped((4, 64, 512), f32), shaped((4, 2, 4, 40, 128), f32)),
         scratch=[
             pltpu.VMEM((2, 2, 2, 2, 64, 512), bf16),
             pltpu.VMEM((2, 4, 4, 64, 512), bf16),
@@ -798,9 +1002,18 @@
             pltpu.VMEM((4, 4, 64, 512), bf16),
             pltpu.VMEM((2, 4, 2, 64, 512), bf16),
             pltpu.VMEM((2, 4, 4, 64, 512), bf16),
+            pltpu.VMEM((3, 2, 4, 40, 128), f32),
+            pltpu.VMEM((2, 4, 40, 128), f32),
+            pltpu.VMEM((3, 2, 40, 128), f32),
+            pltpu.VMEM((2, 40, 128), f32),
+            pltpu.VMEM((40, 128), f32),
+            pltpu.VMEM((40, 128), f32),
+            pltpu.VMEM((40, 128), f32),
+            pltpu.VMEM((40, 128), f32),
+            pltpu.VMEM((40, 128), f32),
         ],
         vmem=48 << 20,
-    )(*[g.reshape(4, 2, 4, 64, 512) for g in grads])[0]
+    )(*[g.reshape(4, 2, 4, 64, 512) for g in grads], small.reshape(4, 2, 4, 40, 128))
 
 
 def on_device(
@@ -897,43 +1110,53 @@
     gate_total = jnp.sum(chosen, axis=-1, keepdims=True)
     gates = chosen / gate_total
 
-    sent = jnp.concatenate(
-        [normed_ffn, cotangent, slot_code.astype(bf16), gates.astype(bf16)], axis=1
-    )
-    everyone = spread(sent)
+    code = jnp.transpose(slot_code.reshape(tok, 32, EXP_DEV), (0, 2, 1))
+    home_hot = code[..., None] == jnp.arange(CAP, dtype=f32)
+    def to_peers(rows):
+        return lax.all_to_all(rows, ("head", "blk"), split_axis=1, concat_axis=1, tiled=True)
+
+    sent = jnp.concatenate([normed_ffn, slot_code.astype(bf16), gates.astype(bf16)], axis=1)
+    everyone = spread(sent, 7)
+    all_cot = spread(cotangent, 11)
     lane = jnp.arange(128)[None]
     sel_row = jnp.arange(8)[:, None]
-    sel = (
-        (sel_row < 4) & (lane == (sel_row // 2) * EXPERTS + device * EXP_DEV + sel_row % 2)
-    ).astype(bf16)
-    expert_rows, arrived_grads = pick_rows(sel, everyone, width)
+    info = everyone[:, :, width:]
+    column = (sel_row // 2) * EXPERTS + device * EXP_DEV + sel_row % 2
+    sel = ((sel_row < 4) & (lane == column)).astype(bf16)
+    nearby = (device ^ 8) * EXP_DEV
+    column = sel_row % 2 + jnp.where(sel_row // 2 % 2 == 0, device * EXP_DEV, nearby)
+    sel_chip = (lane == column + (sel_row // 4) * EXPERTS).astype(bf16)
+    expert_rows, row_gates = pick_rows(sel, info, everyone, width, True)
     expert_rows = expert_rows.reshape(EXP_DEV, -1, width)
-    arrived_grads = arrived_grads.reshape(EXP_DEV, -1, width)
+    row_gates = row_gates.reshape(EXP_DEV, -1, 128)[..., :1]
+    (arrived_cot,) = pick_rows(sel, info, all_cot, width, False)
+    arrived_cot = arrived_cot.reshape(EXP_DEV, -1, width)
 
     gate_up = jnp.einsum("erd,def->erf", expert_rows, full_in, preferred_element_type=f32)
     gate_part, up_part = gate_up[..., :FF], gate_up[..., FF:]
     sigmoid_gate = jax.nn.sigmoid(gate_part)
     silu_gate = gate_part * sigmoid_gate
-    hidden = (silu_gate * up_part).astype(bf16)
+    hidden_full = silu_gate * up_part
+    hidden = hidden_full.astype(bf16)
+    scaled_hidden = (hidden_full * row_gates).astype(bf16)
     expert_result = jnp.einsum(
         "erf,def->erd", hidden, full_back, preferred_element_type=f32
     ).astype(bf16)
-
-    def home(rows):
-        rows = rows.reshape(EXP_DEV, 32, CAP, width)
-        moved = lax.all_to_all(rows, ("head", "blk"), split_axis=1, concat_axis=1, tiled=True)
-        return moved.reshape(EXP_DEV * 32 * CAP, width)
-
-    returned = home(expert_result)
-    term_back = jnp.einsum("erc,erf->ecf", arrived_grads, hidden, preferred_element_type=f32)
-    grad_hidden = jnp.einsum("erd,def->erf", arrived_grads, full_back, preferred_element_type=f32)
+    row_dots = jnp.sum(expert_result.astype(f32) * arrived_cot.astype(f32), axis=-1)
+
+    grad_hidden = row_gates * jnp.einsum(
+        "erd,def->erf", arrived_cot, full_back, preferred_element_type=f32
+    )
     grad_gate = grad_hidden * up_part * sigmoid_gate * (1.0 + gate_part * (1.0 - sigmoid_gate))
     grad_up = grad_hidden * silu_gate
     grad_gate_up = jnp.concatenate([grad_gate, grad_up], axis=-1).astype(bf16)
     grad_rows = jnp.einsum(
         "erf,def->erd", grad_gate_up, full_in, preferred_element_type=f32
     ).astype(bf16)
-    back_rows = home(grad_rows)
+    mixture = rows_home(sel_chip, info, expert_result, True, 12)
+    grad_home = rows_home(sel_chip, info, grad_rows, False, 13)
+    back_dots = to_peers(row_dots.reshape(EXP_DEV, 32, CAP))
+    term_back = jnp.einsum("erc,erf->ecf", arrived_cot, scaled_hidden, preferred_element_type=f32)
     term_in = jnp.einsum("erc,erf->ecf", expert_rows, grad_gate_up, preferred_element_type=f32)
 
     def fold_dp(term):
@@ -942,29 +1165,22 @@
     expert_out_grad = jnp.transpose(fold_dp(term_back), (1, 0, 2)).astype(f32)
     expert_in_grad = jnp.transpose(fold_dp(term_in), (1, 0, 2)).astype(f32)
 
-    code = jnp.transpose(slot_code.reshape(tok, 32, EXP_DEV), (0, 2, 1))
-    home_hot = code[..., None] == jnp.arange(CAP, dtype=f32)
-    home_gate = jnp.transpose(gates.reshape(tok, 32, EXP_DEV), (0, 2, 1))[..., None]
-    flat_hot = home_hot.reshape(tok, -1)
-    mixture = jnp.dot(
-        jnp.where(home_hot, home_gate, 0.0).astype(bf16).reshape(tok, -1),
-        returned,
-        preferred_element_type=f32,
-    )
     output = (middle + mixture).astype(bf16)
     grad_out = cotangent.astype(f32)
-    dots = jnp.einsum("td,rd->tr", cotangent, returned, preferred_element_type=f32)
-    grad_gates = jnp.sum(jnp.where(flat_hot, dots, 0.0).reshape(tok, EXP_DEV, 32, CAP), axis=-1)
+    grad_gates = jnp.sum(jnp.where(home_hot, back_dots, 0.0), axis=-1)
     grad_gates = jnp.transpose(grad_gates, (0, 2, 1)).reshape(tok, EXPERTS)
     mean_grad = jnp.sum(grad_gates * gates, axis=-1, keepdims=True)
     grad_probs = (grad_gates - mean_grad) / gate_total * hot
     grad_logits = probabilities * (
         grad_probs - jnp.sum(probabilities * grad_probs, axis=-1, keepdims=True)
     )
-    router_term = jnp.dot(normed_ffn.astype(f32).T, grad_logits, precision=highest)
-    grad_ffn = jnp.dot(
-        flat_hot.astype(bf16), back_rows, preferred_element_type=f32
-    ) + jnp.dot(grad_logits, router.astype(f32).T, precision=highest)
+    high = grad_logits.astype(bf16)
+    halves = jnp.concatenate([high, (grad_logits - high.astype(f32)).astype(bf16)], axis=1)
+    router_term = jnp.einsum("td,te->de", normed_ffn, halves, preferred_element_type=f32)
+    router_term = router_term[:, :EXPERTS] + router_term[:, EXPERTS:]
+    grad_ffn = grad_home + jnp.einsum(
+        "te,de->td", halves, jnp.concatenate([router, router], axis=1), preferred_element_type=f32
+    )
     ffn_gain_term = jnp.sum(grad_ffn * middle * second_inv, axis=0)
     grad_middle = grad_out + rms_back(middle, second_inv, grad_ffn * ffn_gain)
     grad_branch = grad_middle.astype(bf16)
@@ -1001,30 +1217,33 @@
     def weight_grad(rows, grads):
         return jnp.einsum("qc,qf->cf", rows, grads, preferred_element_type=f32).astype(bf16)
 
-    attn_grads = fold_grads(
+    gains = jnp.concatenate([attn_gain_term, ffn_gain_term, query_gain_term, key_gain_term])
+    gains = jnp.pad(gains, (0, 32 * 8 * 128 - gains.shape[0])).reshape(32, 8, 128)
+    small = jnp.concatenate([router_term.reshape(32, 32, 128), gains], axis=1)
+    attn_grads, summed = fold_grads(
         [
             weight_grad(normed_all, grad_query_flat),
             weight_grad(normed_all, grad_key_flat),
             weight_grad(normed_all, grad_value_flat),
             weight_grad(branch_all, attended_flat),
-        ]
-    )
-    summed = lax.psum(
-        (attn_gain_term, ffn_gain_term, query_gain_term, key_gain_term, router_term),
-        ("dp", "head", "blk"),
-    )
+        ],
+        small,
+    )
+    summed = summed.reshape(32, 40, 128)
+    router_grad = summed[:, :32].reshape(router.shape)
+    gains = summed[:, 32:].reshape(-1)
     return (
         output,
         input_grad,
-        summed[0],
+        gains[:2048],
         attn_grads[0],
         attn_grads[1],
         attn_grads[2],
         attn_grads[3],
-        summed[2],
-        summed[3],
-        summed[1],
-        summed[4],
+        gains[4096:4224],
+        gains[4224:4352],
+        gains[2048:4096],
+        router_grad,
         expert_in_grad,
         expert_out_grad,
     )

time: 997 us -> 899 us (0.902)
  waiting for transfers between devices: 171 us -> 0.09 us
  Pallas kernels: 453 us -> 610 us
  blocking collectives: 63.1 us -> 0 us
  matrix products: 151 us -> 141 us
    pallas_call x3 -> x7, Pallas kernels: 224 us -> 373 us  [the longest x2 135 us: rows_home(): remote_call(functools.partial(home_kernel, gated), 'rows_home', cid, HOME...]
    all_to_all x2 -> x1, waiting for transfers between devices: 121 us -> 0.01 us  [to_peers(): lax.all_to_all(rows, ('head', 'blk'), split_axis=1, concat_axis=1, tiled=...]
    psum x1 -> x0, blocking collectives: 63.1 us -> none  [on_device(): lax.psum((attn_gain_term, ffn_gain_term, query_gain_term, key_gain_term,...]
    psum x1 -> x0, waiting for transfers between devices: 49.2 us -> none  [on_device(): lax.psum((attn_gain_term, ffn_gain_term, query_gain_term, key_gain_term,...]
    dot_general x7 -> x4, matrix products: 48.8 us -> 33.8 us  [the longest x1 16.6 us: on_device(): jnp.einsum('erd,def->erf', arrived_cot, full_back, preferred_element_type...]
    unnamed x197 -> x194, local copies, waits for them, and re-layouts: 51.2 us -> 55.9 us
  transfers between devices with their start and end apart: 7 -> 5, of which waited for: 3 -> 0; matrix products, arithmetic and copies ran while one was open for 22% -> 25% of each run, Pallas kernels for 46% -> 68%
where the time goes in v2:
time: 899 us; the launch traced here: 895 us
  Pallas kernels  610 us (68%)
  matrix products  141 us (16%)
  local copies, waits for them, and re-layouts  94.3 us (10%)
  other arithmetic  28.5 us (3%)
  between operations  15.5 us (2%)
    pallas_call x2, Pallas kernels, rows_home(): remote_call(functools.partial(home_kernel, gated), 'rows_home', cid, HOME...  135 us
    pallas_call x2, Pallas kernels, spread(): remote_call(spread_kernel, 'spread', cid, 26, 1, [ANY], [ANY], (shaped((2...  123 us
    pallas_call x1, Pallas kernels, fold_grads(): remote_call(fold_kernel, 'fold_grads', 8, 52, 1, [VMEM] * 5, [VMEM] * 2,...  84.8 us
    pallas_call x1, Pallas kernels, gather_weights(): remote_call(weights_kernel, 'gather_weights', 1, 24, 3, [ANY] * 3, [ANY]...  66.4 us
    unnamed x194, local copies, waits for them, and re-layouts  55.9 us
    pallas_call x2, Pallas kernels, sum_rows(): remote_call(sum_kernel, 'sum_rows', cid, 3, 1, [VMEM], [VMEM], (shaped((1...  37.8 us
    pallas_call x1, Pallas kernels, heads_over_x(): remote_call(heads_kernel, 'heads_over_x', 3, 22, 4, [ANY] * 4, [ANY] * 4,...  37.4 us
    pallas_call x2, Pallas kernels, pick_rows(): pl.pallas_call(functools.partial(pick_kernel, gated), name='pick_rows', g...  29.5 us
  transfers between devices with their start and end apart: 5, of which 0 were waited for; matrix products, arithmetic and copies ran while one was open for 25% of the time, Pallas kernels for 68%

profile of v2, /device:TPU:0, one launch (start us, length us, event | category | flops | bytes accessed | tf_op | source)
XLA Modules:
  0.0 894.6 jit_solution(2090511726505006404)
XLA Ops:
  18.9 66.4 %gather_weights.1 = (bf16[3,4,2,4,64,512]{5,4,3,2,1,0:T(8,128)(2,1)}, bf16[4,64,512]{2,1,0:T(8,128)(2,1)}, bf16[4,128,2048]{2,1,0:T(8,128)(2,1)}) custom-call(bf16[3,64,512]{2,1,0:T(8,128)(2,1)} %pad_maximum_fusion.8.w, bf16[64,512]{1,0:T(8,128)(2,1)} %wo.1, bf16[128,2048]{1,0:T(8,128)(2,1)} %fusion.5.n), custom_call_target="tpu_custom_call" | custom-call | tf_op jit(solution)/shard_map/gather_weights/pallas_call | solution.py:181
  121.3 37.4 %heads_over_x.1 = (bf16[4,4,128,128]{3,2,1,0:T(8,128)(2,1)}, bf16[4,2,4,128,128]{4,3,2,1,0:T(8,128)(2,1)}, bf16[4,2,4,128,128]{4,3,2,1,0:T(8,128)(2,1)}, bf16[4,2,4,64,512]{4,3,2,1,0:T(8,128)(2,1)}) custom-call(bf16[4,4,128,128]{3,2,1,0:T(8,128)(2,1)} %pad_maximum_fusion.6.q, bf16[4,4,128,128]{3,2,1,0:T(8,128)(2,1)} %pad_maximum_fusion.7.k, ...), custom_call_target="tpu_custom_call" | custom-call | tf_op jit(solution)/shard_map/heads_over_x/pallas_call | solution.py:311
  162.7 14.4 %attend.1 = (bf16[2048,128]{1,0:T(8,128)(2,1)S(1)}, f32[2048,128]{1,0:T(8,128)S(1)}, f32[2048,128]{1,0:T(8,128)S(1)}) custom-call(s32[2,8]{1,0:T(2,128)S(1)} %pad_add_fusion.lim, bf16[2048,128]{1,0:T(8,128)(2,1)S(1)} %bitcast.189, bf16[4096,128]{1,0:T(8,128)(2,1)S(1)} %bitcast.182, bf16[4096,128]{1,0:T(8,128)(2,1)S(1)} %bitcast.184, ...), custom_call_target="tpu_custom_call" | custom-call | tf_op jit(solution)/shard_map/attend/pallas_call | solution.py:469
  179.9 8.3 back_over_x.1
  192.6 19.9 %sum_rows.2 = f32[128,2048]{1,0:T(8,128)S(1)} custom-call(bf16[2,2,128,2048]{3,2,1,0:T(8,128)(2,1)S(1)} %bitcast.188), custom_call_target="tpu_custom_call" | custom-call | tf_op jit(solution)/shard_map/sum_rows/pallas_call | solution.py:249
  216.7 63.4 %spread.2 = bf16[2,2,2,4,128,2176]{5,4,3,2,1,0:T(8,128)(2,1)} custom-call(bf16[128,2176]{1,0:T(8,128)(2,1)} %concatenate.54.src), custom_call_target="tpu_custom_call" | custom-call | tf_op jit(solution)/shard_map/spread/pallas_call | solution.py:617
  281.5 14.7 %pick_rows.2 = (bf16[2,16,48,2048]{3,2,1,0:T(8,128)(2,1)S(1)}, f32[2,16,48,128]{3,2,1,0:T(8,128)S(1)}) custom-call(bf16[8,128]{1,0:T(8,128)(2,1)S(1)} %fusion.25.sel, bf16[32,128,128]{2,1,0:T(8,128)(2,1)S(1)} %slice.136.info, bf16[32,128,2176]{2,1,0:T(8,128)(2,1)} %bitcast.209), custom_call_target="tpu_custom_call" | custom-call | tf_op jit(solution)/shard_map/pick_rows/pallas_call | solution.py:673
  299.1 59.6 %spread.3 = bf16[2,2,2,4,128,2048]{5,4,3,2,1,0:T(8,128)(2,1)} custom-call(bf16[128,2048]{1,0:T(8,128)(2,1)} %src.1), custom_call_target="tpu_custom_call" | custom-call | tf_op jit(solution)/shard_map/spread/pallas_call | solution.py:617
  358.8 14.8 %pick_rows.3 = bf16[2,16,48,2048]{3,2,1,0:T(8,128)(2,1)S(1)} custom-call(bf16[8,128]{1,0:T(8,128)(2,1)S(1)} %fusion.25.sel, bf16[32,128,128]{2,1,0:T(8,128)(2,1)S(1)} %slice.136.info, bf16[32,128,2048]{2,1,0:T(8,128)(2,1)} %bitcast.210), custom_call_target="tpu_custom_call" | custom-call | tf_op jit(solution)/shard_map/pick_rows/pallas_call | solution.py:673
  376.3 21.2 %fusion.49 = f32[2,768,2048]{2,1,0:T(8,128)} fusion(bf16[2,768,2048]{2,1,0:T(8,128)(2,1)} %bitcast.206, bf16[2048,2,2048]{2,0,1:T(8,128)(2,1)} %all-gather.3.cloned.1.call-done), kind=kOutput, calls=%fused_computation.184 | convolution fusion | flops 12884901888 | bytes 35651584 | tf_op jit(solution)/shard_map/erd,def->erf/dot_general | solution.py:1135
  397.4 14.4 %convolution_convert_fusion.1 = bf16[2,2048,1024]{2,1,0:T(8,128)(2,1)} fusion(bf16[2,768,2048]{2,1,0:T(8,128)(2,1)} %bitcast.177, f32[2,768]{1,0:T(2,128)S(1)} %bitcast.252, f32[2,768,2048]{2,1,0:T(8,128)} %fusion.49), kind=kOutput, calls=%fused_computation.10 | convolution fusion | flops 6457655296 | bytes 27269120 | tf_op jit(solution)/shard_map/erc,erf->ecf/dot_general | solution.py:1159
  412.0 16.6 %multiply_convert_fusion.2 = (bf16[2,768,1024]{2,1,0:T(8,128)(2,1)}, bf16[2,768,1024]{2,1,0:T(8,128)(2,1)}) fusion(f32[2,768,2048]{2,1,0:T(8,128)} %fusion.49, f32[2,768]{1,0:T(2,128)S(1)} %bitcast.253, bf16[2,768,2048]{2,1,0:T(8,128)(2,1)} %bitcast.178, bf16[2048,2,1024]{2,0,1:T(8,128)(2,1)} %all-gather.5.cloned.1.call-done), kind=kOutput, calls=%fused_computation.6 | convolution fusion | flops 6464471040 | bytes 33560576 | tf_op jit(solution)/shard_map/erd,def->erf/dot_general | solution.py:1147
  428.6 20.5 %convolution_convert_fusion = bf16[2,2048,2048]{2,1,0:T(8,128)(2,1)} fusion(bf16[2,768,2048]{2,1,0:T(8,128)(2,1)} %bitcast.207, bf16[2,768,1024]{2,1,0:T(8,128)(2,1)} %get-tuple-element.152, bf16[2,768,1024]{2,1,0:T(8,128)(2,1)} %get-tuple-element.151), kind=kOutput, calls=%fused_computation.1 | convolution fusion | flops 12905873408 | bytes 29360128 | tf_op jit(solution)/shard_map/erc,erf->ecf/dot_general | solution.py:1160
  451.6 15.9 %multiply_reduce_fusion = (f32[2,768]{1,0:T(2,128)S(1)}, bf16[2,768,2048]{2,1,0:T(8,128)(2,1)}) fusion(bf16[2,16,48,2048]{3,2,1,0:T(8,128)(2,1)} %copy-done, bf16[2048,2,1024]{2,0,1:T(8,128)(2,1)} %all-gather.5.cloned.1.call-done, f32[2,768,2048]{2,1,0:T(8,128)} %fusion.49), kind=kOutput, calls=%fused_computation | convolution fusion | flops 6467615232 | bytes 33560576 | tf_op jit(solution)/shard_map/erf,def->erd/dot_general | solution.py:1142
  473.3 19.5 %convolution_convert_fusion.3 = bf16[2,768,2048]{2,1,0:T(8,128)(2,1)} fusion(bf16[2048,2,2048]{2,0,1:T(8,128)(2,1)} %all-gather.3.cloned.1.call-done, bf16[2,768,1024]{2,1,0:T(8,128)(2,1)} %get-tuple-element.152, bf16[2,768,1024]{2,1,0:T(8,128)(2,1)} %get-tuple-element.151), kind=kOutput, calls=%fused_computation.12 | convolution fusion | flops 12900630528 | bytes 29360128 | tf_op jit(solution)/shard_map/erf,def->erd/dot_general | solution.py:1153
  492.8 68.3 %rows_home.3 = f32[128,2048]{1,0:T(8,128)S(1)} custom-call(bf16[8,128]{1,0:T(8,128)(2,1)S(1)} %fusion.23.sel, bf16[32,128,128]{2,1,0:T(8,128)(2,1)S(1)} %slice.136.info, bf16[2,2,2,4,48,2048]{5,4,3,2,1,0:T(8,128)(2,1)} %bitcast.218), custom_call_target="tpu_custom_call" | custom-call | tf_op jit(solution)/shard_map/rows_home/pallas_call | solution.py:822
  562.2 66.9 %rows_home.2 = f32[128,2048]{1,0:T(8,128)S(1)} custom-call(bf16[8,128]{1,0:T(8,128)(2,1)S(1)} %fusion.23.sel, bf16[32,128,128]{2,1,0:T(8,128)(2,1)S(1)} %slice.136.info, bf16[2,2,2,4,48,2048]{5,4,3,2,1,0:T(8,128)(2,1)} %bitcast.217), custom_call_target="tpu_custom_call" | custom-call | tf_op jit(solution)/shard_map/rows_home/pallas_call | solution.py:822
  635.7 17.6 %gather_rows.1 = bf16[4,128,2048]{2,1,0:T(8,128)(2,1)} custom-call(bf16[128,2048]{1,0:T(8,128)(2,1)} %fusion.37.n), custom_call_target="tpu_custom_call" | custom-call | tf_op jit(solution)/shard_map/gather_rows/pallas_call | solution.py:210
  659.7 10.5 %go_over_x.1 = bf16[4,4,128,128]{3,2,1,0:T(8,128)(2,1)} custom-call(bf16[4,4,128,128]{3,2,1,0:T(8,128)(2,1)} %bitcast.237), custom_call_target="tpu_custom_call" | custom-call | tf_op jit(solution)/shard_map/go_over_x/pallas_call | solution.py:361
  675.3 18.3 %attend_back.1 = (bf16[2048,128]{1,0:T(8,128)(2,1)S(1)}, bf16[4096,128]{1,0:T(8,128)(2,1)S(1)}, bf16[4096,128]{1,0:T(8,128)(2,1)S(1)}) custom-call(s32[2,8]{1,0:T(2,128)S(1)} %copy-done.19, bf16[2048,128]{1,0:T(8,128)(2,1)S(1)} %bitcast.190, bf16[4096,128]{1,0:T(8,128)(2,1)S(1)} %bitcast.183, bf16[4096,128]{1,0:T(8,128)(2,1)S(1)} %bitcast.185, ...), custom_call_target="tpu_custom_call" | custom-call | tf_op jit(solution)/shard_map/attend_back/pallas_call | solution.py:530
  693.6 27.1 %grads_over_x.1 = (bf16[4,4,128,128]{3,2,1,0:T(8,128)(2,1)S(1)}, bf16[4,4,128,128]{3,2,1,0:T(8,128)(2,1)S(1)}, bf16[4,4,128,128]{3,2,1,0:T(8,128)(2,1)S(1)}) custom-call(bf16[4,4,128,128]{3,2,1,0:T(8,128)(2,1)S(1)} %bitcast.197, bf16[4,2,4,128,128]{4,3,2,1,0:T(8,128)(2,1)S(1)} %bitcast.191, bf16[4,2,4,128,128]{4,3,2,1,0:T(8,128)(2,1)S(1)} %bitcast.192), custom_call_target="tpu_custom_call" | custom-call | tf_op jit(solution)/shard_map/grads_over_x/pallas_call | solution.py:405
  737.6 18.0 %sum_rows.3 = f32[128,2048]{1,0:T(8,128)S(1)} custom-call(bf16[2,2,128,2048]{3,2,1,0:T(8,128)(2,1)S(1)} %bitcast.176), custom_call_target="tpu_custom_call" | custom-call | tf_op jit(solution)/shard_map/sum_rows/pallas_call | solution.py:249
  770.4 84.8 %fold_grads.1 = (f32[4,64,512]{2,1,0:T(8,128)S(1)}, f32[4,2,4,40,128]{4,3,2,1,0:T(8,128)S(1)}) custom-call(bf16[4,2,4,64,512]{4,3,2,1,0:T(8,128)(2,1)S(1)} %bitcast.186, bf16[4,2,4,64,512]{4,3,2,1,0:T(8,128)(2,1)S(1)} %bitcast.187, bf16[4,2,4,64,512]{4,3,2,1,0:T(8,128)(2,1)} %bitcast.223, bf16[4,2,4,64,512]{4,3,2,1,0:T(8,128)(2,1)} %bitcast.224, ...), custom_call_target="tpu_custom_call" | custom-call | tf_op jit(solution)/shard_map/fold_grads/pallas_call | solution.py:986
  876.8 11.1 %copy.234 = f32[512,2,2048]{2,1,0:T(2,128)} copy(f32[512,2,2048]{2,0,1:T(8,128)S(1)} %convert_bitcast_fusion) | data formatting | bytes 16777216
  (317 shorter events, 149.6 us)
Async XLA Ops:
  7.2 369.1 %all-gather.3.cloned.1.call-start = ((), (), s32[]{:S(2)}) async-start(), calls=%async_computation.3 | async-start | bytes 20971520 | tf_op jit(solution)/shard_map/all_gather | solution.py:1041
  13.4 398.6 %all-gather.5.cloned.1.call-start = ((), (), s32[]{:S(2)}) async-start(), calls=%async_computation.4 | async-start | bytes 10485760 | tf_op jit(solution)/shard_map/all_gather | solution.py:1042
  16.9 849.3 %reduce-scatter.5.cloned.1.call-start = ((), (), s32[]{:S(2)}) async-start(), calls=%async_computation.6 | async-start | bytes 10485760 | tf_op jit(solution)/shard_map/reduce_scatter | solution.py:1163
  17.2 73.9 %copy-start.80 = (f32[128]{0:T(128)}, f32[128]{0:T(128)S(1)}, u32[]{:S(2)}) copy-start(f32[128]{0:T(128)S(1)} %add_rsqrt_fusion.3) | copy-start | bytes 1540
  116.3 60.8 %copy-start.14 = (s32[1,1,4,512]{3,1,2,0:T(1,128)}, s32[1,1,4,512]{3,1,2,0:T(1,128)S(1)}, u32[]{:S(2)}) copy-start(s32[1,1,4,512]{3,1,2,0:T(1,128)S(1)} %copy.247) | copy-start | bytes 24580
  159.2 33.3 %copy-start.18 = (s32[2,8]{1,0:T(2,128)}, s32[2,8]{1,0:T(2,128)S(1)}, u32[]{:S(2)}) copy-start(s32[2,8]{1,0:T(2,128)S(1)} %pad_add_fusion.lim) | copy-start | bytes 196
  189.4 23.0 %copy-start.86 = (s32[128,8]{0,1:T(8,128)S(1)}, s32[128,8]{0,1:T(8,128)}, u32[]{:S(2)}) copy-start(s32[128,8]{0,1:T(8,128)} %param.19) | copy-start | bytes 12292
  212.6 67.5 %copy-start.51 = (f32[128,64]{1,0:T(8,128)}, f32[128,64]{1,0:T(8,128)S(1)}, u32[]{:S(2)}) copy-start(f32[128,64]{1,0:T(8,128)S(1)} %copy.207) | copy-start | bytes 98308
  212.9 67.2 %copy-start.21 = (f32[128,2048]{1,0:T(8,128)}, f32[128,2048]{1,0:T(8,128)S(1)}, u32[]{:S(2)}) copy-start(f32[128,2048]{1,0:T(8,128)S(1)} %get-tuple-element.148) | copy-start | bytes 3145732
  213.6 66.5 %copy-start.33 = (bf16[128,2048]{1,0:T(8,128)(2,1)}, bf16[128,2048]{1,0:T(8,128)(2,1)S(1)}, u32[]{:S(2)}) copy-start(bf16[128,2048]{1,0:T(8,128)(2,1)S(1)} %multiply_convert_fusion.4) | copy-start | bytes 1572868
  214.1 66.1 %copy-start.47 = (f32[128,64]{1,0:T(8,128)}, f32[128,64]{1,0:T(8,128)S(1)}, u32[]{:S(2)}) copy-start(f32[128,64]{1,0:T(8,128)S(1)} %copy.209) | copy-start | bytes 98308
  214.5 65.7 %copy-start.54 = (f32[128,64]{1,0:T(8,128)}, f32[128,64]{1,0:T(8,128)S(1)}, u32[]{:S(2)}) copy-start(f32[128,64]{1,0:T(8,128)S(1)} %get-tuple-element.146) | copy-start | bytes 98308
  411.9 461.6 %reduce-scatter.3.cloned.1.call-start = ((), (), s32[]{:S(2)}) async-start(), calls=%async_computation.5 | async-start | bytes 20971520 | tf_op jit(solution)/shard_map/reduce_scatter | solution.py:1163
  468.3 161.8 %all-to-all-start = ((f32[2,32,24]{2,0,1:T(2,128)}), f32[2,32,24]{2,0,1:T(2,128)S(1)}, u32[]{:S(2)}, u32[]{:S(2)}) async-start(f32[2,32,24]{2,0,1:T(2,128)} %copy.217), calls=%async_computation | async-start | bytes 65536 | tf_op jit(solution)/shard_map/all_to_all | solution.py:1116
  562.1 68.4 %copy-start.55 = (f32[128,64]{1,0:T(8,128)S(1)}, f32[128,64]{1,0:T(8,128)}, u32[]{:S(2)}) copy-start(f32[128,64]{1,0:T(8,128)} %copy-done.54) | copy-start | bytes 98308
  562.1 68.4 %copy-start.79 = (f32[128]{0:T(128)S(1)}, f32[128]{0:T(128)}, u32[]{:S(2)}) copy-start(f32[128]{0:T(128)} %copy-done.78) | copy-start | bytes 1540
  562.1 68.6 %copy-start.48 = (f32[128,64]{1,0:T(8,128)S(1)}, f32[128,64]{1,0:T(8,128)}, u32[]{:S(2)}) copy-start(f32[128,64]{1,0:T(8,128)} %copy-done.47) | copy-start | bytes 98308
  562.1 68.6 %copy-start.52 = (f32[128,64]{1,0:T(8,128)S(1)}, f32[128,64]{1,0:T(8,128)}, u32[]{:S(2)}) copy-start(f32[128,64]{1,0:T(8,128)} %copy-done.51) | copy-start | bytes 98308
  562.1 68.6 %copy-start.73 = (f32[128]{0:T(128)S(1)}, f32[128]{0:T(128)}, u32[]{:S(2)}) copy-start(f32[128]{0:T(128)} %copy-done.72) | copy-start | bytes 1540
  562.1 68.6 %copy-start.77 = (f32[128]{0:T(128)S(1)}, f32[128]{0:T(128)}, u32[]{:S(2)}) copy-start(f32[128]{0:T(128)} %copy-done.76) | copy-start | bytes 1540
  562.1 69.0 %copy-start.60 = (f32[2048]{0:T(1024)S(1)}, f32[2048]{0:T(1024)}, u32[]{:S(2)}) copy-start(f32[2048]{0:T(1024)} %param.27) | copy-start | bytes 24580
  562.2 69.0 %copy-start.75 = (f32[128]{0:T(128)S(1)}, f32[128]{0:T(128)}, u32[]{:S(2)}) copy-start(f32[128]{0:T(128)} %copy-done.74) | copy-start | bytes 1540
  737.6 21.7 %copy-start.27 = (bf16[128,2048]{1,0:T(8,128)(2,1)S(1)}, bf16[128,2048]{1,0:T(8,128)(2,1)}, u32[]{:S(2)}) copy-start(bf16[128,2048]{1,0:T(8,128)(2,1)} %param.16) | copy-start | bytes 1572868
  737.6 21.7 %copy-start.66 = (f32[2048]{0:T(1024)S(1)}, f32[2048]{0:T(1024)}, u32[]{:S(2)}) copy-start(f32[2048]{0:T(1024)} %param.20) | copy-start | bytes 24580
  (70 other events, 351.2 us)
Sparse Core Ops, SparseCore 0:
  13.4 157.6 all-gather.2
  172.8 83.6 all-gather.4
  412.0 79.5 reduce-scatter.4
  494.0 147.7 reduce-scatter.2

commit v3 on v2

--- a/solution.py
+++ b/solution.py
@@ -73,33 +73,79 @@
     pl.semaphore_wait(barrier, len(devices))
 
 
+class View:
+    def __init__(self, ref, index=None):
+        self.ref, self.index = ref, index
+
+    @property
+    def at(self):
+        return self
+
+    def __getitem__(self, index):
+        return View(self, index)
+
+    def get(self):
+        base = self.ref.get() if isinstance(self.ref, View) else self.ref
+        return base if self.index is None else base.at[self.index]
+
+    def load(self):
+        return self.get()[...]
+
+    def store(self, value):
+        ref = self.get()
+        ref[...] = value.astype(ref.dtype)
+
+
+def plain(ref):
+    return ref.get() if isinstance(ref, View) else ref
+
+
+class Sent:
+    def __init__(self, make):
+        self.make = make
+
+    def wait_recv(self):
+        self.make().wait_recv()
+
+    def wait_send(self):
+        self.make().wait_send()
+
+    def wait(self):
+        self.make().wait()
+
+
 class Wire:
     def __init__(self, send_sem, recv_sem):
         self.send_sem, self.recv_sem, self.started = send_sem, recv_sem, []
 
     def send(self, src, dst, device):
         at = len(self.started)
-        copy = pltpu.make_async_remote_copy(
-            src_ref=src,
-            dst_ref=dst,
-            send_sem=self.send_sem.at[at],
-            recv_sem=self.recv_sem.at[at],
-            device_id=device,
-            device_id_type=MESH,
-        )
-        copy.start()
-        self.started.append(copy)
-        return copy
+
+        def make():
+            return pltpu.make_async_remote_copy(
+                src_ref=plain(src),
+                dst_ref=plain(dst),
+                send_sem=self.send_sem.at[at],
+                recv_sem=self.recv_sem.at[at],
+                device_id=device,
+                device_id_type=MESH,
+            )
+
+        make().start()
+        self.started.append(Sent(make))
+        return self.started[-1]
 
     def drain(self):
         for copy in self.started:
             copy.wait_send()
 
 
-def local(src, dst, sem):
-    copy = pltpu.make_async_copy(src, dst, sem)
-    copy.start()
-    return copy
+def local(src, dst, sems, at):
+    def make():
+        return pltpu.make_async_copy(plain(src), plain(dst), sems.at[at])
+
+    make().start()
+    return Sent(make)
 
 
 def remote_call(body, name, cid, sends, locals_, ins, outs, out_shape, scratch=(), vmem=None):
@@ -124,9 +170,9 @@
     p = Place()
     dp, yl, x = p.dp, p.yl, p.x
     own = [
-        local(w, g.at[:, dp, yl, x], ls.at[0]),
-        local(n, m.at[p.head], ls.at[1]),
-        local(wo, go.at[dp], ls.at[2]),
+        local(w, g.at[:, dp, yl, x], ls, 0),
+        local(n, m.at[p.head], ls, 1),
+        local(wo, go.at[dp], ls, 2),
     ]
     greet([p.ZR, p.ZL, p.XR, p.XL, p.Y, p.C, p.H])
     wire = Wire(ss, rs)
@@ -192,7 +238,7 @@
 
 def rows_kernel(n, m, ss, rs, ls):
     p = Place()
-    own = local(n, m.at[p.head], ls.at[0])
+    own = local(n, m.at[p.head], ls, 0)
     greet([p.C, p.H])
     wire = Wire(ss, rs)
     n_h = wire.send(n, m.at[p.head], p.H)
@@ -268,10 +314,10 @@
     p = Place()
     yl, x = p.yl, p.x
     own = [
-        local(q.at[x], qd.at[:, x], ls.at[0]),
-        local(k.at[x], kd.at[:, yl, x], ls.at[1]),
-        local(v.at[x], vd.at[:, yl, x], ls.at[2]),
-        local(go, gd.at[:, yl, x], ls.at[3]),
+        local(q.at[x], qd.at[:, x], ls, 0),
+        local(k.at[x], kd.at[:, yl, x], ls, 1),
+        local(v.at[x], vd.at[:, yl, x], ls, 2),
+        local(go, gd.at[:, yl, x], ls, 3),
     ]
     greet([p.Y, p.XR, p.XL, p.XO])
     wire = Wire(ss, rs)
@@ -327,7 +373,7 @@
 
 def back_x_kernel(o, att, ss, rs, ls):
     p = Place()
-    own = local(o.at[:, p.x], att.at[p.x], ls.at[0])
+    own = local(o.at[:, p.x], att.at[p.x], ls, 0)
     greet([p.XR, p.XL, p.XO])
     wire = Wire(ss, rs)
     for there, device in ((p.xo, p.XO), (p.xr, p.XR), (p.xl, p.XL)):
@@ -346,7 +392,7 @@
 
 def go_x_kernel(o, d, ss, rs, ls):
     p = Place()
-    own = local(o.at[p.x], d.at[:, p.x], ls.at[0])
+    own = local(o.at[p.x], d.at[:, p.x], ls, 0)
     greet([p.XR, p.XL, p.XO])
     wire = Wire(ss, rs)
     for there, device in ((p.xo, p.XO), (p.xr, p.XR), (p.xl, p.XL)):
@@ -366,7 +412,7 @@
 def grads_x_kernel(dq, dk, dv, qd, kd, vd, ss, rs, ls, gk, gv, sk, sv):
     p = Place()
     x, yl = p.x, p.yl
-    own = local(dq.at[:, x], qd.at[x], ls.at[0])
+    own = local(dq.at[:, x], qd.at[x], ls, 0)
     greet([p.Y, p.XR, p.XL, p.XO])
     wire = Wire(ss, rs)
     order = ((p.xo, p.XO), (p.xr, p.XR), (p.xl, p.XL), (x, None))
@@ -542,74 +588,81 @@
     )(lim, q, k, v, g, qseg[None], qpos[None], kseg[:, None], linv[None], delta[None])
 
 
-def spread_kernel(src, dst, ss, rs, ls):
-    p = Place()
+SPREAD_SENDS = 26
+
+
+def spread_steps(p, wire, sems, src, dst):
     yh, co, yl, x = p.yh, p.co, p.yl, p.x
-    own = local(src, dst.at[yh, co, yl, x], ls.at[0])
-    greet([p.XR, p.XL, p.YR, p.YL, p.C])
-    wire = Wire(ss, rs)
+    (rh, rl), (lh, ll), (oh, ol) = ((y // 2, lax.rem(y, 2)) for y in (p.yr, p.ylf, p.yo))
     A, A1, A2 = pl.ds(0, 64), pl.ds(0, 32), pl.ds(32, 32)
     B, B1, B2 = pl.ds(64, 64), pl.ds(64, 32), pl.ds(96, 32)
-
-    def at_y(y, rows):
-        return dst.at[y // 2, co, lax.rem(y, 2), :, rows]
-
-    def at_x(xx, rows):
-        return dst.at[:, co, :, xx, rows]
+    src, dst = View(src), View(dst)
+    own = local(src, dst.at[yh, co, yl, x], sems, 0)
 
     def both(ref, device):
         return wire.send(ref, ref, device)
 
-    y = yh * 2 + yl
     me = dst.at[yh, co, yl]
     a1 = wire.send(src.at[A], me.at[x, A], p.XR)
     b1 = wire.send(src.at[B], me.at[x, B], p.YR)
     a2 = wire.send(src.at[A], me.at[x, A], p.XL)
     b2 = wire.send(src.at[B], me.at[x, B], p.YL)
+    yield
     a1.wait_recv()
     a3 = both(me.at[p.xl, A1], p.XR)
     a2.wait_recv()
     a4 = both(me.at[p.xr, A2], p.XL)
-    yr, ylf, yo = p.yr, p.ylf, p.yo
-
-    def block(yy, rows):
-        return dst.at[yy // 2, co, lax.rem(yy, 2), x, rows]
-
     b1.wait_recv()
-    b3 = both(block(ylf, B1), p.YR)
+    b3 = both(dst.at[lh, co, ll, x, B1], p.YR)
     b2.wait_recv()
-    b4 = both(block(yr, B2), p.YL)
+    b4 = both(dst.at[rh, co, rl, x, B2], p.YL)
+    yield
     own.wait()
     a3.wait_recv()
     a4.wait_recv()
-    a5 = both(at_y(y, A), p.YR)
-    a6 = both(at_y(y, A), p.YL)
+    a5 = both(me.at[:, A], p.YR)
+    a6 = both(me.at[:, A], p.YL)
     b3.wait_recv()
     b4.wait_recv()
-    b5 = both(at_x(x, B), p.XR)
-    b6 = both(at_x(x, B), p.XL)
-    last = [both(at_y(y, A), p.C), both(at_x(x, B), p.C)]
+    b5 = both(dst.at[:, co, :, x, B], p.XR)
+    b6 = both(dst.at[:, co, :, x, B], p.XL)
+    last = [both(me.at[:, A], p.C), both(dst.at[:, co, :, x, B], p.C)]
+    yield
     a5.wait_recv()
-    a7 = both(at_y(ylf, A1), p.YR)
+    a7 = both(dst.at[lh, co, ll, :, A1], p.YR)
     b5.wait_recv()
-    b7 = both(at_x(p.xl, B1), p.XR)
+    b7 = both(dst.at[:, co, :, p.xl, B1], p.XR)
     a6.wait_recv()
-    a8 = both(at_y(yr, A2), p.YL)
+    a8 = both(dst.at[rh, co, rl, :, A2], p.YL)
     b6.wait_recv()
-    b8 = both(at_x(p.xr, B2), p.XL)
-    last += [both(at_y(ylf, A), p.C), both(at_x(p.xl, B), p.C)]
-    last += [both(at_y(yr, A), p.C), both(at_x(p.xr, B), p.C)]
+    b8 = both(dst.at[:, co, :, p.xr, B2], p.XL)
+    last += [both(dst.at[lh, co, ll, :, A], p.C), both(dst.at[:, co, :, p.xl, B], p.C)]
+    last += [both(dst.at[rh, co, rl, :, A], p.C), both(dst.at[:, co, :, p.xr, B], p.C)]
+    yield
     a7.wait_recv()
-    last.append(both(at_y(yo, A1), p.C))
+    last.append(both(dst.at[oh, co, ol, :, A1], p.C))
     b7.wait_recv()
-    last.append(both(at_x(p.xo, B1), p.C))
+    last.append(both(dst.at[:, co, :, p.xo, B1], p.C))
     a8.wait_recv()
-    last.append(both(at_y(yo, A2), p.C))
+    last.append(both(dst.at[oh, co, ol, :, A2], p.C))
     b8.wait_recv()
-    last.append(both(at_x(p.xo, B2), p.C))
+    last.append(both(dst.at[:, co, :, p.xo, B2], p.C))
+    yield
     for copy in last:
         copy.wait_recv()
     wire.drain()
+    yield
+
+
+def greet_plane(p):
+    greet([p.XR, p.XL, p.YR, p.YL, p.C])
+
+
+def spread_kernel(src, dst, ss, rs, ls):
+    p = Place()
+    greet_plane(p)
+    for _ in spread_steps(p, Wire(ss, rs), ls, src, dst):
+        pass
 
 
 def spread(src, cid):
@@ -618,12 +671,98 @@
         spread_kernel,
         "spread",
         cid,
-        26,
+        SPREAD_SENDS,
         1,
         [ANY],
         [ANY],
         (shaped((2, 2, 2, 4, 128, width)),),
     )(src)[0].reshape(32, 128, width)
+
+
+def at_step(number, *stages):
+    for step, stage in stages:
+
+        @pl.when(number == step)
+        def _():
+            next(stage)
+
+
+def block(shape, index):
+    return pl.BlockSpec(shape, index)
+
+
+def nt(a, b):
+    return lax.dot_general(a, b, (((1,), (1,)), ((), ())), preferred_element_type=f32)
+
+
+def tn(a, b):
+    return lax.dot_general(a, b, (((0,), (0,)), ((), ())), preferred_element_type=f32)
+
+
+PARTS = 4
+
+
+def forward_kernel(src, rows, w_in, w_out, dst, gate, up, hidden, y, ss, rs, ls):
+    p = Place()
+    greet_plane(p)
+    moving = spread_steps(p, Wire(ss, rs), ls, src, dst)
+    next(moving)
+    n = rows.shape[1]
+    cut = FF // PARTS
+
+    def first(rows, w_gate, w_up, gate, up, hidden):
+        at_step(pl.program_id(0) * PARTS + pl.program_id(1), (2, moving), (4, moving))
+        g = jnp.dot(rows[0], w_gate[0], preferred_element_type=f32)
+        u = jnp.dot(rows[0], w_up[0], preferred_element_type=f32)
+        gate[0] = g.astype(bf16)
+        up[0] = u.astype(bf16)
+        hidden[0] = (g * jax.nn.sigmoid(g) * u).astype(bf16)
+
+    out = block((1, n, cut), lambda e, j: (e, 0, j))
+    pltpu.emit_pipeline(
+        first,
+        grid=(EXP_DEV, PARTS),
+        in_specs=[
+            block((1, n, 2048), lambda e, j: (e, 0, 0)),
+            block((1, 2048, cut), lambda e, j: (e, 0, j)),
+            block((1, 2048, cut), lambda e, j: (e, 0, j + PARTS)),
+        ],
+        out_specs=[out, out, out],
+    )(rows, w_in, w_in, gate, up, hidden)
+
+    def second(hidden, w, y):
+        at_step(pl.program_id(0) * PARTS + pl.program_id(1), (3, moving))
+        y[0] = nt(hidden[0], w[0]).astype(bf16)
+
+    pltpu.emit_pipeline(
+        second,
+        grid=(EXP_DEV, PARTS),
+        in_specs=[
+            block((1, n, FF), lambda e, j: (e, 0, 0)),
+            block((1, 2048 // PARTS, FF), lambda e, j: (e, j, 0)),
+        ],
+        out_specs=[block((1, n, 2048 // PARTS), lambda e, j: (e, 0, j))],
+    )(hidden, w_out, y)
+    for _ in moving:
+        pass
+
+
+def expert_forward(src, rows, w_in, w_out, cid):
+    n, width = rows.shape[1:]
+    outs = remote_call(
+        forward_kernel,
+        "expert_forward",
+        cid,
+        SPREAD_SENDS,
+        1,
+        [ANY] * 4,
+        [ANY] * 5,
+        (shaped((2, 2, 2, 4, 128, width)),)
+        + (shaped((EXP_DEV, n, FF)),) * 3
+        + (shaped((EXP_DEV, n, width)),),
+        vmem=48 << 20,
+    )(src, rows, w_in, w_out)
+    return outs[0].reshape(32, 128, width), *outs[1:]
 
 
 def slot_hits(table, count, rows_down):
@@ -705,12 +844,14 @@
     yh, co, yl, x = p.yh, p.co, p.yl, p.x
     ys = [(yy // 2, lax.rem(yy, 2)) for yy in (p.yr, p.ylf, p.yo)]
     (rh, rl), (lh, ll), (oh, ol) = ys
+    rows, out, whole_q, whole_cat = View(rows), View(out), q, cat
+    q, cat, a1, b1, a2, b2, c1, c2 = (View(ref) for ref in (q, cat, a1, b1, a2, b2, c1, c2))
     own, first = [], []
     for e in range(EXP_DEV):
         lines = pl.ds(e * 2 * CAP, 2 * CAP)
         there = pl.ds((2 + e) * 2 * CAP, 2 * CAP)
         first.append(wire.send(rows.at[e, :, 1 - co], cat.at[:, :, there], p.C))
-        own.append(local(rows.at[e, :, co], cat.at[:, :, lines], sems.at[e]))
+        own.append(local(rows.at[e, :, co], cat.at[:, :, lines], sems, e))
     yield
     for copy in own:
         copy.wait()
@@ -728,11 +869,11 @@
         value = jnp.where(hit, gate if gated else 1.0, 0.0).astype(bf16)
         for c in range(0, 2048, 512):
             total = jnp.dot(
-                value, cat[h, pair, :, c : c + 512], preferred_element_type=f32
+                value, whole_cat[h, pair, :, c : c + 512], preferred_element_type=f32
             ).astype(bf16)
             at = lax.rem(pair, 2) * 2
-            q[h, pair // 2, at, :, c : c + 512] = total[:128]
-            q[h, pair // 2, at + 1, :, c : c + 512] = total[128:]
+            whole_q[h, pair // 2, at, :, c : c + 512] = total[:128]
+            whole_q[h, pair // 2, at + 1, :, c : c + 512] = total[128:]
         return carry
 
     lax.fori_loop(0, 8, place, 0)
@@ -746,10 +887,10 @@
     yield
 
     def add(dst, *srcs):
-        total = srcs[0][...].astype(f32)
+        total = srcs[0].load().astype(f32)
         for src in srcs[1:]:
-            total = total + src[...].astype(f32)
-        dst[...] = total.astype(dst.dtype)
+            total = total + src.load().astype(f32)
+        dst.store(total)
 
     def loop(count, body):
         def step(i, carry):
@@ -811,26 +952,146 @@
     yield
 
 
-def home_kernel(gated, sel, info, rows, out, ss, rs, ls, *scratch):
+def by_place(rows):
+    return rows.reshape(EXP_DEV, 2, 2, 4, 2 * CAP, 2048)
+
+
+def backward_kernel(
+    sel, info, y_places, y, cot, gate, up, hidden, row_gates, w_in, w_out,
+    mixture, dots, dgate, dup, drows, term, ss, rs, ls, *scratch,
+):
     p = Place()
-    greet([p.XR, p.XL, p.YR, p.YL, p.C])
-    for _ in home_steps(p, Wire(ss, rs), ls, gated, sel, info, rows, out, *scratch):
+    greet_plane(p)
+    moving = home_steps(p, Wire(ss, rs), ls, True, sel, info, y_places, mixture, *scratch)
+    next(moving)
+    n = cot.shape[1]
+    wide, cut = 2048 // PARTS, FF // PARTS
+    dots[...] = jnp.zeros_like(dots)
+
+    def number():
+        return pl.program_id(0) * PARTS + pl.program_id(1)
+
+    def first(y, cot, hidden, row_gates, term):
+        at_step(number(), (1, moving), (6, moving))
+        e = pl.program_id(0)
+        product = y[0].astype(f32) * cot[0].astype(f32)
+        partial = product[:, :128]
+        for c in range(128, wide, 128):
+            partial += product[:, c : c + 128]
+        dots[e] += partial
+        scaled = (hidden[0].astype(f32) * row_gates[0, :, :1]).astype(bf16)
+        term[0] = tn(cot[0], scaled).astype(bf16)
+
+    part = block((1, n, wide), lambda e, j: (e, 0, j))
+    whole = block((1, n, FF), lambda e, j: (e, 0, 0))
+    gates = block((1, n, 128), lambda e, j: (e, 0, 0))
+    pltpu.emit_pipeline(
+        first,
+        grid=(EXP_DEV, PARTS),
+        in_specs=[part, part, whole, gates],
+        out_specs=[block((1, wide, FF), lambda e, j: (e, j, 0))],
+    )(y, cot, hidden, row_gates, term)
+
+    def second(cot, w, row_gates, gate, up, dgate, dup):
+        at_step(number(), (5, moving))
+        dhidden = jnp.dot(cot[0], w[0], preferred_element_type=f32) * row_gates[0, :, :1]
+        g, u = gate[0].astype(f32), up[0].astype(f32)
+        sg = jax.nn.sigmoid(g)
+        dgate[0] = (dhidden * u * sg * (1.0 + g * (1.0 - sg))).astype(bf16)
+        dup[0] = (dhidden * g * sg).astype(bf16)
+
+    out = block((1, n, cut), lambda e, j: (e, 0, j))
+    pltpu.emit_pipeline(
+        second,
+        grid=(EXP_DEV, PARTS),
+        in_specs=[
+            block((1, n, 2048), lambda e, j: (e, 0, 0)),
+            block((1, 2048, cut), lambda e, j: (e, 0, j)),
+            gates,
+            out,
+            out,
+        ],
+        out_specs=[out, out],
+    )(cot, w_out, row_gates, gate, up, dgate, dup)
+
+    def third(dgate, dup, w, drows):
+        at_step(number(), (4, moving))
+        total = nt(dgate[0], w[0, :, :FF]) + nt(dup[0], w[0, :, FF:])
+        drows[0] = total.astype(bf16)
+
+    pltpu.emit_pipeline(
+        third,
+        grid=(EXP_DEV, PARTS),
+        in_specs=[whole, whole, block((1, wide, 2 * FF), lambda e, j: (e, j, 0))],
+        out_specs=[part],
+    )(dgate, dup, w_in, drows)
+    for _ in moving:
         pass
 
 
-def rows_home(sel, info, rows, gated, cid):
+def expert_backward(sel, info, y, cot, gate, up, hidden, row_gates, w_in, w_out, cid):
+    n = cot.shape[1]
+    half = shaped((EXP_DEV, n, FF))
     return remote_call(
-        functools.partial(home_kernel, gated),
-        "rows_home",
+        backward_kernel,
+        "expert_backward",
         cid,
         HOME_SENDS,
         2,
-        [VMEM, VMEM, ANY],
-        [VMEM],
-        (shaped((128, 2048), f32),),
+        [VMEM, VMEM] + [ANY] * 9,
+        [VMEM, VMEM] + [ANY] * 4,
+        (
+            shaped((128, 2048), f32),
+            shaped((EXP_DEV, n, 128), f32),
+            half,
+            half,
+            shaped((EXP_DEV, n, 2048)),
+            shaped((EXP_DEV, 2048, FF)),
+        ),
         scratch=home_scratch(),
-        vmem=48 << 20,
-    )(sel, info, rows.reshape(EXP_DEV, 2, 2, 4, 2 * CAP, 2048))[0]
+        vmem=58 << 20,
+    )(sel, info, by_place(y), y, cot, gate, up, hidden, row_gates, w_in, w_out)
+
+
+def finish_kernel(sel, info, places, rows, dgate, dup, home, term, ss, rs, ls, *scratch):
+    p = Place()
+    greet_plane(p)
+    moving = home_steps(p, Wire(ss, rs), ls, False, sel, info, places, home, *scratch)
+    next(moving)
+    n = rows.shape[1]
+    wide = 2048 // PARTS
+
+    def first(rows, dgate, dup, term):
+        at_step(
+            pl.program_id(0) * PARTS + pl.program_id(1), (1, moving), (4, moving), (7, moving)
+        )
+        term[0, :, :FF] = tn(rows[0], dgate[0]).astype(bf16)
+        term[0, :, FF:] = tn(rows[0], dup[0]).astype(bf16)
+
+    whole = block((1, n, FF), lambda e, j: (e, 0, 0))
+    pltpu.emit_pipeline(
+        first,
+        grid=(EXP_DEV, PARTS),
+        in_specs=[block((1, n, wide), lambda e, j: (e, 0, j)), whole, whole],
+        out_specs=[block((1, wide, 2 * FF), lambda e, j: (e, j, 0))],
+    )(rows, dgate, dup, term)
+    for _ in moving:
+        pass
+
+
+def expert_finish(sel, info, drows, rows, dgate, dup, cid):
+    return remote_call(
+        finish_kernel,
+        "expert_finish",
+        cid,
+        HOME_SENDS,
+        2,
+        [VMEM, VMEM] + [ANY] * 4,
+        [VMEM, ANY],
+        (shaped((128, 2048), f32), shaped((EXP_DEV, 2048, 2 * FF))),
+        scratch=home_scratch(),
+        vmem=58 << 20,
+    )(sel, info, by_place(drows), rows, dgate, dup)
 
 
 def fold_kernel(
@@ -1038,8 +1299,8 @@
     device = lax.axis_index("head") * 8 + blk
     yl = blk // 4
     tok, width = tokens.shape
-    full_in = lax.all_gather(expert_in, "dp", axis=0, tiled=True)
-    full_back = lax.all_gather(expert_out, "dp", axis=0, tiled=True)
+    full_in = lax.all_gather(jnp.transpose(expert_in, (1, 0, 2)), "dp", axis=1, tiled=True)
+    full_back = lax.all_gather(jnp.transpose(expert_out, (1, 0, 2)), "dp", axis=1, tiled=True)
 
     segment, valid = segment_ids[0], valid_mask[0]
     seq_len = segment.shape[0]
@@ -1117,7 +1378,6 @@
 
     sent = jnp.concatenate([normed_ffn, slot_code.astype(bf16), gates.astype(bf16)], axis=1)
     everyone = spread(sent, 7)
-    all_cot = spread(cotangent, 11)
     lane = jnp.arange(128)[None]
     sel_row = jnp.arange(8)[:, None]
     info = everyone[:, :, width:]
@@ -1128,36 +1388,20 @@
     sel_chip = (lane == column + (sel_row // 4) * EXPERTS).astype(bf16)
     expert_rows, row_gates = pick_rows(sel, info, everyone, width, True)
     expert_rows = expert_rows.reshape(EXP_DEV, -1, width)
-    row_gates = row_gates.reshape(EXP_DEV, -1, 128)[..., :1]
+    row_gates = row_gates.reshape(EXP_DEV, -1, 128)
+    all_cot, gate_part, up_part, hidden, expert_result = expert_forward(
+        cotangent, expert_rows, full_in, full_back, 11
+    )
     (arrived_cot,) = pick_rows(sel, info, all_cot, width, False)
     arrived_cot = arrived_cot.reshape(EXP_DEV, -1, width)
-
-    gate_up = jnp.einsum("erd,def->erf", expert_rows, full_in, preferred_element_type=f32)
-    gate_part, up_part = gate_up[..., :FF], gate_up[..., FF:]
-    sigmoid_gate = jax.nn.sigmoid(gate_part)
-    silu_gate = gate_part * sigmoid_gate
-    hidden_full = silu_gate * up_part
-    hidden = hidden_full.astype(bf16)
-    scaled_hidden = (hidden_full * row_gates).astype(bf16)
-    expert_result = jnp.einsum(
-        "erf,def->erd", hidden, full_back, preferred_element_type=f32
-    ).astype(bf16)
-    row_dots = jnp.sum(expert_result.astype(f32) * arrived_cot.astype(f32), axis=-1)
-
-    grad_hidden = row_gates * jnp.einsum(
-        "erd,def->erf", arrived_cot, full_back, preferred_element_type=f32
+    mixture, row_dots, grad_gate, grad_up, grad_rows, term_back = expert_backward(
+        sel_chip, info, expert_result, arrived_cot, gate_part, up_part, hidden, row_gates,
+        full_in, full_back, 12,
     )
-    grad_gate = grad_hidden * up_part * sigmoid_gate * (1.0 + gate_part * (1.0 - sigmoid_gate))
-    grad_up = grad_hidden * silu_gate
-    grad_gate_up = jnp.concatenate([grad_gate, grad_up], axis=-1).astype(bf16)
-    grad_rows = jnp.einsum(
-        "erf,def->erd", grad_gate_up, full_in, preferred_element_type=f32
-    ).astype(bf16)
-    mixture = rows_home(sel_chip, info, expert_result, True, 12)
-    grad_home = rows_home(sel_chip, info, grad_rows, False, 13)
-    back_dots = to_peers(row_dots.reshape(EXP_DEV, 32, CAP))
-    term_back = jnp.einsum("erc,erf->ecf", arrived_cot, scaled_hidden, preferred_element_type=f32)
-    term_in = jnp.einsum("erc,erf->ecf", expert_rows, grad_gate_up, preferred_element_type=f32)
+    grad_home, term_in = expert_finish(
+        sel_chip, info, grad_rows, expert_rows, grad_gate, grad_up, 13
+    )
+    back_dots = to_peers(jnp.sum(row_dots, axis=-1).reshape(EXP_DEV, 32, CAP))
 
     def fold_dp(term):
         return lax.psum_scatter(term.astype(bf16), "dp", scatter_dimension=1, tiled=True)

time: 899 us -> 825 us (0.918)
  matrix products: 141 us -> 29.9 us
  Pallas kernels: 610 us -> 628 us
    dot_general x6 -> x0, matrix products: 108 us -> none  [the longest x1 21.2 us: on_device(): jnp.einsum('erd,def->erf', expert_rows, full_in, preferred_element_type=f32)]
    pallas_call x4, Pallas kernels: 258 us -> 275 us  [the longest x1 81.3 us: expert_backward(): remote_call(backward_kernel, 'expert_backward', cid, HOME_SENDS, 2, [VMEM...]
    unnamed x194 -> x147, local copies, waits for them, and re-layouts: 55.9 us -> 58.6 us
  transfers between devices with their start and end apart: 5 -> 5, of which waited for: 0 -> 1; matrix products, arithmetic and copies ran while one was open for 25% -> 15% of each run, Pallas kernels for 68% -> 58%
where the time goes in v3:
time: 825 us; the launch traced here: 819 us
  Pallas kernels  628 us (76%)
  local copies, waits for them, and re-layouts  103 us (12%)
  other arithmetic  31.6 us (4%)
  matrix products  29.9 us (4%)
  between operations  15.2 us (2%)
    pallas_call x1, Pallas kernels, fold_grads(): remote_call(fold_kernel, 'fold_grads', 8, 52, 1, [VMEM] * 5, [VMEM] * 2,...  85.1 us
    pallas_call x1, Pallas kernels, expert_backward(): remote_call(backward_kernel, 'expert_backward', cid, HOME_SENDS, 2, [VMEM...  81.3 us
    pallas_call x1, Pallas kernels, gather_weights(): remote_call(weights_kernel, 'gather_weights', 1, 24, 3, [ANY] * 3, [ANY]...  72.2 us
    pallas_call x1, Pallas kernels, expert_finish(): remote_call(finish_kernel, 'expert_finish', cid, HOME_SENDS, 2, [VMEM, VM...  69.8 us
    pallas_call x1, Pallas kernels, spread(): remote_call(spread_kernel, 'spread', cid, SPREAD_SENDS, 1, [ANY], [ANY],...  67.1 us
    unnamed x147, local copies, waits for them, and re-layouts  58.6 us
    pallas_call x1, Pallas kernels, expert_forward(): remote_call(forward_kernel, 'expert_forward', cid, SPREAD_SENDS, 1, [ANY]...  56.6 us
    pallas_call x1, Pallas kernels, heads_over_x(): remote_call(heads_kernel, 'heads_over_x', 3, 22, 4, [ANY] * 4, [ANY] * 4,...  37.3 us
  transfers between devices with their start and end apart: 5, of which 1 were waited for; matrix products, arithmetic and copies ran while one was open for 15% of the time, Pallas kernels for 58%

profile of v3, /device:TPU:0, one launch (start us, length us, event | category | flops | bytes accessed | tf_op | source)
XLA Modules:
  0.0 818.6 jit_solution(11951216324163328708)
XLA Ops:
  10.9 6.1 copy.233
  19.7 72.2 %gather_weights.1 = (bf16[3,4,2,4,64,512]{5,4,3,2,1,0:T(8,128)(2,1)}, bf16[4,64,512]{2,1,0:T(8,128)(2,1)}, bf16[4,128,2048]{2,1,0:T(8,128)(2,1)}) custom-call(bf16[3,64,512]{2,1,0:T(8,128)(2,1)} %pad_maximum_fusion.5.w, bf16[64,512]{1,0:T(8,128)(2,1)} %wo.1, bf16[128,2048]{1,0:T(8,128)(2,1)} %fusion.2.n), custom_call_target="tpu_custom_call" | custom-call | tf_op jit(solution)/shard_map/gather_weights/pallas_call | solution.py:227
  92.0 5.6 fusion.36
  97.6 4.7 copy.186
  133.3 37.3 %heads_over_x.1 = (bf16[4,4,128,128]{3,2,1,0:T(8,128)(2,1)}, bf16[4,2,4,128,128]{4,3,2,1,0:T(8,128)(2,1)}, bf16[4,2,4,128,128]{4,3,2,1,0:T(8,128)(2,1)}, bf16[4,2,4,64,512]{4,3,2,1,0:T(8,128)(2,1)}) custom-call(bf16[4,4,128,128]{3,2,1,0:T(8,128)(2,1)} %pad_maximum_fusion.3.q, bf16[4,4,128,128]{3,2,1,0:T(8,128)(2,1)} %pad_maximum_fusion.4.k, ...), custom_call_target="tpu_custom_call" | custom-call | tf_op jit(solution)/shard_map/heads_over_x/pallas_call | solution.py:357
  174.7 14.1 %attend.1 = (bf16[2048,128]{1,0:T(8,128)(2,1)S(1)}, f32[2048,128]{1,0:T(8,128)S(1)}, f32[2048,128]{1,0:T(8,128)S(1)}) custom-call(s32[2,8]{1,0:T(2,128)S(1)} %pad_add_fusion.lim, bf16[2048,128]{1,0:T(8,128)(2,1)S(1)} %bitcast.185, bf16[4096,128]{1,0:T(8,128)(2,1)S(1)} %bitcast.178, bf16[4096,128]{1,0:T(8,128)(2,1)S(1)} %bitcast.180, ...), custom_call_target="tpu_custom_call" | custom-call | tf_op jit(solution)/shard_map/attend/pallas_call | solution.py:515
  191.5 8.9 %back_over_x.1 = bf16[4,4,128,128]{3,2,1,0:T(8,128)(2,1)} custom-call(bf16[4,4,128,128]{3,2,1,0:T(8,128)(2,1)} %bitcast.195), custom_call_target="tpu_custom_call" | custom-call | tf_op jit(solution)/shard_map/back_over_x/pallas_call | solution.py:388
  203.1 15.6 %sum_rows.2 = f32[128,2048]{1,0:T(8,128)S(1)} custom-call(bf16[2,2,128,2048]{3,2,1,0:T(8,128)(2,1)S(1)} %bitcast.184), custom_call_target="tpu_custom_call" | custom-call | tf_op jit(solution)/shard_map/sum_rows/pallas_call | solution.py:295
  223.0 67.1 %spread.1 = bf16[2,2,2,4,128,2176]{5,4,3,2,1,0:T(8,128)(2,1)} custom-call(bf16[128,2176]{1,0:T(8,128)(2,1)} %concatenate.50.src), custom_call_target="tpu_custom_call" | custom-call | tf_op jit(solution)/shard_map/spread/pallas_call | solution.py:670
  291.5 15.0 %pick_rows.2 = (bf16[2,16,48,2048]{3,2,1,0:T(8,128)(2,1)S(1)}, f32[2,16,48,128]{3,2,1,0:T(8,128)S(1)}) custom-call(bf16[8,128]{1,0:T(8,128)(2,1)S(1)} %fusion.22.sel, bf16[32,128,128]{2,1,0:T(8,128)(2,1)S(1)} %slice.124.info, bf16[32,128,2176]{2,1,0:T(8,128)(2,1)} %bitcast.203), custom_call_target="tpu_custom_call" | custom-call | tf_op jit(solution)/shard_map/pick_rows/pallas_call | solution.py:812
  310.8 56.6 %expert_forward.1 = (bf16[2,2,2,4,128,2048]{5,4,3,2,1,0:T(8,128)(2,1)}, bf16[2,768,1024]{2,1,0:T(8,128)(2,1)S(1)}, bf16[2,768,1024]{2,1,0:T(8,128)(2,1)}, bf16[2...) custom-call(bf16[128,2048]{1,0:T(8,128)(2,1)S(1)} %copy-done.3, bf16[2,768,2048]{2,1,0:T(8,128)(2,1)} %bitcast.171, ...), custom_call_target="tpu_custom_call" | custom-call | tf_op jit(solution)/shard_map/expert_forward/pallas_call | solution.py:752
  367.4 15.7 %pick_rows.3 = bf16[2,16,48,2048]{3,2,1,0:T(8,128)(2,1)S(1)} custom-call(bf16[8,128]{1,0:T(8,128)(2,1)S(1)} %fusion.22.sel, bf16[32,128,128]{2,1,0:T(8,128)(2,1)S(1)} %slice.124.info, bf16[32,128,2048]{2,1,0:T(8,128)(2,1)} %bitcast.209), custom_call_target="tpu_custom_call" | custom-call | tf_op jit(solution)/shard_map/pick_rows/pallas_call | solution.py:812
  385.8 81.3 %expert_backward.1 = (f32[128,2048]{1,0:T(8,128)}, f32[2,768,128]{2,1,0:T(8,128)}, bf16[2,768,1024]{2,1,0:T(8,128)(2,1)}, bf16[2,768,1024]{2,1,0:T(8,128)(2,1)},...) custom-call(bf16[8,128]{1,0:T(8,128)(2,1)} %fusion.20.sel, bf16[32,128,128]{2,1,0:T(8,128)(2,1)} %copy-done, ...), custom_call_target="tpu_custom_call" | custom-call | tf_op jit(solution)/shard_map/expert_backward/pallas_call | solution.py:1035
  467.2 69.8 %expert_finish.1 = (f32[128,2048]{1,0:T(8,128)}, bf16[2,2048,2048]{2,1,0:T(8,128)(2,1)}) custom-call(bf16[8,128]{1,0:T(8,128)(2,1)} %fusion.20.sel, bf16[32,128,128]{2,1,0:T(8,128)(2,1)} %copy-done, bf16[2,2,2,4,48,2048]{5,4,3,2,1,0:T(8,128)(2,1)} %bitcast.214, bf16[2,768,2048]{2,1,0:T(8,128)(2,1)} %bitcast.172, ...), custom_call_target="tpu_custom_call" | custom-call | tf_op jit(solution)/shard_map/expert_finish/pallas_call | solution.py:1083
  539.2 4.8 all-to-all-start
  545.7 5.5 all-to-all-done
  566.7 17.7 %gather_rows.1 = bf16[4,128,2048]{2,1,0:T(8,128)(2,1)} custom-call(bf16[128,2048]{1,0:T(8,128)(2,1)} %fusion.32.n), custom_call_target="tpu_custom_call" | custom-call | tf_op jit(solution)/shard_map/gather_rows/pallas_call | solution.py:256
  591.1 10.2 %go_over_x.1 = bf16[4,4,128,128]{3,2,1,0:T(8,128)(2,1)} custom-call(bf16[4,4,128,128]{3,2,1,0:T(8,128)(2,1)} %bitcast.233), custom_call_target="tpu_custom_call" | custom-call | tf_op jit(solution)/shard_map/go_over_x/pallas_call | solution.py:407
  605.4 17.8 %attend_back.1 = (bf16[2048,128]{1,0:T(8,128)(2,1)S(1)}, bf16[4096,128]{1,0:T(8,128)(2,1)S(1)}, bf16[4096,128]{1,0:T(8,128)(2,1)S(1)}) custom-call(s32[2,8]{1,0:T(2,128)S(1)} %pad_add_fusion.lim, bf16[2048,128]{1,0:T(8,128)(2,1)S(1)} %bitcast.186, bf16[4096,128]{1,0:T(8,128)(2,1)S(1)} %bitcast.179, bf16[4096,128]{1,0:T(8,128)(2,1)S(1)} %bitcast.181, ...), custom_call_target="tpu_custom_call" | custom-call | tf_op jit(solution)/shard_map/attend_back/pallas_call | solution.py:576
  623.2 27.8 %grads_over_x.1 = (bf16[4,4,128,128]{3,2,1,0:T(8,128)(2,1)S(1)}, bf16[4,4,128,128]{3,2,1,0:T(8,128)(2,1)S(1)}, bf16[4,4,128,128]{3,2,1,0:T(8,128)(2,1)S(1)}) custom-call(bf16[4,4,128,128]{3,2,1,0:T(8,128)(2,1)S(1)} %bitcast.193, bf16[4,2,4,128,128]{4,3,2,1,0:T(8,128)(2,1)S(1)} %bitcast.187, bf16[4,2,4,128,128]{4,3,2,1,0:T(8,128)(2,1)S(1)} %bitcast.188), custom_call_target="tpu_custom_call" | custom-call | tf_op jit(solution)/shard_map/grads_over_x/pallas_call | solution.py:451
  668.6 15.8 %sum_rows.3 = f32[128,2048]{1,0:T(8,128)S(1)} custom-call(bf16[2,2,128,2048]{3,2,1,0:T(8,128)(2,1)S(1)} %bitcast.174), custom_call_target="tpu_custom_call" | custom-call | tf_op jit(solution)/shard_map/sum_rows/pallas_call | solution.py:295
  694.1 85.1 %fold_grads.1 = (f32[4,64,512]{2,1,0:T(8,128)S(1)}, f32[4,2,4,40,128]{4,3,2,1,0:T(8,128)S(1)}) custom-call(bf16[4,2,4,64,512]{4,3,2,1,0:T(8,128)(2,1)S(1)} %bitcast.183, bf16[4,2,4,64,512]{4,3,2,1,0:T(8,128)(2,1)S(1)} %bitcast.182, bf16[4,2,4,64,512]{4,3,2,1,0:T(8,128)(2,1)} %bitcast.220, bf16[4,2,4,64,512]{4,3,2,1,0:T(8,128)(2,1)} %bitcast.219, ...), custom_call_target="tpu_custom_call" | custom-call | tf_op jit(solution)/shard_map/fold_grads/pallas_call | solution.py:1247
  792.2 5.3 copy.218
  800.8 11.1 %copy.217 = f32[512,2,2048]{2,1,0:T(2,128)} copy(f32[512,2,2048]{2,0,1:T(8,128)S(1)} %convert_bitcast_fusion) | data formatting | bytes 16777216
  (264 shorter events, 132.4 us)
Async XLA Ops:
  7.2 303.6 %all-gather.5.cloned.1.call-start = ((), (), s32[]{:S(2)}) async-start(), calls=%async_computation.4 | async-start | bytes 10485760 | tf_op jit(solution)/shard_map/all_gather | solution.py:1303
  10.8 300.0 %all-gather.3.cloned.1.call-start = ((), (), s32[]{:S(2)}) async-start(), calls=%async_computation.3 | async-start | bytes 20971520 | tf_op jit(solution)/shard_map/all_gather | solution.py:1302
  17.0 773.2 %reduce-scatter.5.cloned.1.call-start = ((), (), s32[]{:S(2)}) async-start(), calls=%async_computation.6 | async-start | bytes 10485760 | tf_op jit(solution)/shard_map/reduce_scatter | solution.py:1407
  18.8 78.8 %copy-start.54 = (f32[128]{0:T(128)}, f32[128]{0:T(128)S(1)}, u32[]{:S(2)}) copy-start(f32[128]{0:T(128)S(1)} %add_rsqrt_fusion.3) | copy-start | bytes 1540
  97.6 4.8 copy-start.19
  104.8 3.7 copy-start.63
  112.7 7.5 copy-start.29
  120.1 6.5 copy-start.45
  120.1 6.5 copy-start.49
  191.5 10.2 %copy-start.65 = (bf16[4,2,4,64,512]{4,3,2,1,0:T(8,128)(2,1)S(1)}, bf16[4,2,4,64,512]{4,3,2,1,0:T(8,128)(2,1)}, u32[]{:S(2)}) copy-start(bf16[4,2,4,64,512]{4,3,2,1,0:T(8,128)(2,1)} %get-tuple-element.53) | copy-start | bytes 6291460
  220.9 69.3 %copy-start.52 = (f32[128]{0:T(128)}, f32[128]{0:T(128)S(1)}, u32[]{:S(2)}) copy-start(f32[128]{0:T(128)S(1)} %fusion.15) | copy-start | bytes 1540
  291.4 76.0 %copy-start = (bf16[32,128,128]{2,1,0:T(8,128)(2,1)}, bf16[32,128,128]{2,1,0:T(8,128)(2,1)S(1)}, u32[]{:S(2)}) copy-start(bf16[32,128,128]{2,1,0:T(8,128)(2,1)S(1)} %slice.124.info) | copy-start | bytes 3145732
  291.5 19.3 %copy-start.3 = (bf16[128,2048]{1,0:T(8,128)(2,1)S(1)}, bf16[128,2048]{1,0:T(8,128)(2,1)}, u32[]{:S(2)}) copy-start(bf16[128,2048]{1,0:T(8,128)(2,1)} %src.1) | copy-start | bytes 1572868
  367.4 15.8 %copy-start.9 = (bf16[2,768,1024]{2,1,0:T(8,128)(2,1)}, bf16[2,768,1024]{2,1,0:T(8,128)(2,1)S(1)}, u32[]{:S(2)}) copy-start(bf16[2,768,1024]{2,1,0:T(8,128)(2,1)S(1)} %get-tuple-element.57.gate) | copy-start | bytes 9437188
  467.2 330.3 %reduce-scatter.3.cloned.1.call-start = ((), (), s32[]{:S(2)}) async-start(), calls=%async_computation.5 | async-start | bytes 20971520 | tf_op jit(solution)/shard_map/reduce_scatter | solution.py:1407
  537.0 7.0 copy-start.14
  539.2 12.0 %all-to-all-start = ((f32[2,32,24]{2,0,1:T(2,128)}), f32[2,32,24]{2,0,1:T(2,128)}, u32[]{:S(2)}, u32[]{:S(2)}) async-start(f32[2,32,24]{2,0,1:T(2,128)} %copy.202), calls=%async_computation | async-start | bytes 65536 | tf_op jit(solution)/shard_map/all_to_all | solution.py:1377
  564.6 19.9 %copy-start.61 = (f32[128]{0:T(128)}, f32[128]{0:T(128)S(1)}, u32[]{:S(2)}) copy-start(f32[128]{0:T(128)S(1)} %broadcast_multiply_fusion.4) | copy-start | bytes 1540
  589.0 14.1 %copy-start.11 = (bf16[4,4,128,128]{3,2,1,0:T(8,128)(2,1)S(1)}, bf16[4,4,128,128]{3,2,1,0:T(8,128)(2,1)}, u32[]{:S(2)}) copy-start(bf16[4,4,128,128]{3,2,1,0:T(8,128)(2,1)} %get-tuple-element.49) | copy-start | bytes 1572868
  658.9 8.0 copy-start.35
  668.6 15.8 %copy-start.23 = (bf16[128,2048]{1,0:T(8,128)(2,1)S(1)}, bf16[128,2048]{1,0:T(8,128)(2,1)}, u32[]{:S(2)}) copy-start(bf16[128,2048]{1,0:T(8,128)(2,1)} %param.16) | copy-start | bytes 1572868
  668.6 15.8 %copy-start.55 = (f32[128]{0:T(128)S(1)}, f32[128]{0:T(128)}, u32[]{:S(2)}) copy-start(f32[128]{0:T(128)} %copy-done.54) | copy-start | bytes 1540
  668.6 16.2 %copy-start.34 = (f32[4,2,4,32,128]{4,3,2,1,0:T(8,128)S(1)}, f32[4,2,4,32,128]{4,3,2,1,0:T(8,128)}, u32[]{:S(2)}) copy-start(f32[4,2,4,32,128]{4,3,2,1,0:T(8,128)} %concatenate.55) | copy-start | bytes 1572868
  780.0 6.5 copy-start.62
  (47 other events, 77.2 us)
Sparse Core Ops, SparseCore 0:
  10.9 93.5 all-gather.4
  106.8 151.3 all-gather.2
  467.3 77.6 reduce-scatter.4
  547.3 147.6 reduce-scatter.2

commit v4 on v3

--- a/solution.py
+++ b/solution.py
@@ -310,8 +310,9 @@
     )(part.reshape(2, 2, 128, 2048))[0]
 
 
-def heads_kernel(q, k, v, go, qd, kd, vd, gd, ss, rs, ls):
+def heads_kernel(three, go, qd, kd, vd, gd, ss, rs, ls):
     p = Place()
+    q, k, v = (three.at[i] for i in range(3))
     yl, x = p.yl, p.x
     own = [
         local(q.at[x], qd.at[:, x], ls, 0),
@@ -353,14 +354,14 @@
     wire.drain()
 
 
-def heads_over_x(q, k, v, go):
+def heads_over_x(three, go):
     return remote_call(
         heads_kernel,
         "heads_over_x",
         3,
         22,
         4,
-        [ANY] * 4,
+        [ANY] * 2,
         [ANY] * 4,
         (
             shaped((4, 4, 128, 128)),
@@ -368,7 +369,7 @@
             shaped((4, 2, 4, 128, 128)),
             shaped((4, 2, 4, 64, 512)),
         ),
-    )(q, k, v, go)
+    )(three, go)
 
 
 def back_x_kernel(o, att, ss, rs, ls):
@@ -409,9 +410,10 @@
     )(o)[0]
 
 
-def grads_x_kernel(dq, dk, dv, qd, kd, vd, ss, rs, ls, gk, gv, sk, sv):
+def grads_x_kernel(dq, dk, dv, three, ss, rs, ls, gk, gv, sk, sv):
     p = Place()
     x, yl = p.x, p.yl
+    qd, kd, vd = (three.at[i] for i in range(3))
     own = local(dq.at[:, x], qd.at[x], ls, 0)
     greet([p.Y, p.XR, p.XL, p.XO])
     wire = Wire(ss, rs)
@@ -455,8 +457,8 @@
         17,
         1,
         [ANY, VMEM, VMEM],
-        [ANY, VMEM, VMEM],
-        (shaped((4, 4, 128, 128)),) * 3,
+        [VMEM],
+        (shaped((3, 4, 4, 128, 128)),),
         scratch=[
             pltpu.VMEM((4, 4, 128, 128), bf16),
             pltpu.VMEM((4, 4, 128, 128), bf16),
@@ -464,7 +466,55 @@
             pltpu.VMEM((3, 4, 128, 128), bf16),
         ],
         vmem=16 << 20,
-    )(dq, dk, dv)
+    )(dq, dk, dv)[0]
+
+
+def turned(values, cosine, sine):
+    return values * cosine + pltpu.roll(values, 64, 1) * sine
+
+
+def project_kernel(rows, w, cosine, sine, gain, heads, kept):
+    flat = jnp.dot(rows[...], w[0], preferred_element_type=f32)
+    step = pl.program_id(0)
+    for h in range(4):
+        head = flat[:, h * HD : (h + 1) * HD]
+
+        @pl.when(step < 2)
+        def _():
+            kept[0, h] = head
+            scaled = head * rms_rows(head) * gain[0]
+            heads[0, h] = turned(scaled, cosine[...], sine[...]).astype(bf16)
+
+        @pl.when(step == 2)
+        def _():
+            heads[0, h] = head.astype(bf16)
+
+
+def project(rows, w, cosine, sine, gains):
+    def fixed(*shape):
+        return pl.BlockSpec(shape, lambda i: (0,) * len(shape))
+
+    def two(i):
+        return jnp.minimum(i, 1)
+
+    return pl.pallas_call(
+        project_kernel,
+        name="project",
+        grid=(3,),
+        out_shape=(shaped((3, 4, 512, HD)), shaped((2, 4, 512, HD), f32)),
+        in_specs=[
+            fixed(512, 2048),
+            pl.BlockSpec((1, 2048, 512), lambda i: (i, 0, 0)),
+            fixed(512, HD),
+            fixed(512, HD),
+            pl.BlockSpec((1, 1, HD), lambda i: (two(i), 0, 0)),
+        ],
+        out_specs=[
+            pl.BlockSpec((1, 4, 512, HD), lambda i: (i, 0, 0, 0)),
+            pl.BlockSpec((1, 4, 512, HD), lambda i: (two(i), 0, 0, 0)),
+        ],
+        compiler_params=pltpu.CompilerParams(vmem_limit_bytes=60 << 20),
+    )(rows, w, cosine, sine, gains)
 
 
 QB = 256
@@ -785,73 +835,75 @@
 
 
 def pick_kernel(gated, sel, info, src, rows_out, *gates_out):
-    tokens = jnp.concatenate([src[0], src[1]], axis=0)
-    both = jnp.concatenate([info[0], info[1]], axis=0)
-    table = lax.dot_general(
-        sel[...], both, (((1,), (1,)), ((), ())), preferred_element_type=f32
-    )
-    hit, gate = slot_hits(table, EXP_DEV, True)
-    rows = jnp.dot(hit.astype(bf16), tokens, preferred_element_type=f32).astype(bf16)
-    for e in range(EXP_DEV):
-        rows_out[e, 0] = rows[e * 2 * CAP : (e + 1) * 2 * CAP]
-    if gated:
-        total = jnp.sum(jnp.where(hit, gate, 0.0), axis=1, keepdims=True)
-        total = jnp.broadcast_to(total, (EXP_DEV * 2 * CAP, 128))
+    for pair in range(src.shape[0] // 256):
+        at = slice(pair * 256, (pair + 1) * 256)
+        hit, gate = slot_hits(nt(sel[...], info[at]), EXP_DEV, True)
+        rows = jnp.dot(hit.astype(bf16), src[at], preferred_element_type=f32).astype(bf16)
         for e in range(EXP_DEV):
-            gates_out[0][e, 0] = total[e * 2 * CAP : (e + 1) * 2 * CAP]
+            rows_out[e, pair] = rows[e * 2 * CAP : (e + 1) * 2 * CAP]
+        if gated:
+            total = jnp.sum(jnp.where(hit, gate, 0.0), axis=1, keepdims=True)
+            total = jnp.broadcast_to(total, (EXP_DEV * 2 * CAP, 128))
+            for e in range(EXP_DEV):
+                gates_out[0][e, pair] = total[e * 2 * CAP : (e + 1) * 2 * CAP]
 
 
 def pick_rows(sel, info, src, width, gated):
-    pairs = src.shape[0] // 2
+    pairs, step = src.shape[0] // 256, 2
 
     def spec(lanes):
-        return pl.BlockSpec((EXP_DEV, 1, 2 * CAP, lanes), lambda i: (0, i, 0, 0))
+        return pl.BlockSpec((EXP_DEV, step, 2 * CAP, lanes), lambda i: (0, i, 0, 0))
 
     shapes = [shaped((EXP_DEV, pairs, 2 * CAP, width)), shaped((EXP_DEV, pairs, 2 * CAP, 128), f32)]
     specs = [spec(width), spec(128)]
     return pl.pallas_call(
         functools.partial(pick_kernel, gated),
         name="pick_rows",
-        grid=(pairs,),
+        grid=(pairs // step,),
         out_shape=shapes[: 1 + gated],
         in_specs=[
             pl.BlockSpec((8, 128), lambda i: (0, 0)),
-            pl.BlockSpec((2, 128, 128), lambda i: (i, 0, 0)),
-            pl.BlockSpec((2, 128, width), lambda i: (i, 0, 0)),
+            pl.BlockSpec((256 * step, 128), lambda i: (i, 0)),
+            pl.BlockSpec((256 * step, width), lambda i: (i, 0)),
         ],
         out_specs=specs[: 1 + gated],
-        compiler_params=pltpu.CompilerParams(vmem_limit_bytes=40 << 20),
+        compiler_params=pltpu.CompilerParams(vmem_limit_bytes=60 << 20),
     )(sel, info, src)
 
 
-HOME_SENDS = 18
-
-
-def home_scratch():
+HOME_SENDS = 20
+
+
+def home_scratch(width):
     return [
-        pltpu.VMEM((2, 4, 8 * CAP, 2048), bf16),
-        pltpu.VMEM((2, 2, 4, 128, 2048), bf16),
-        pltpu.VMEM((2, 2, 64, 2048), bf16),
-        pltpu.VMEM((2, 2, 64, 2048), bf16),
-        pltpu.VMEM((2, 4, 64, 2048), bf16),
-        pltpu.VMEM((2, 2, 2, 64, 2048), bf16),
-        pltpu.VMEM((2, 2, 32, 2048), bf16),
-        pltpu.VMEM((2, 2, 64, 2048), bf16),
+        pltpu.VMEM((2, 4, 8 * CAP, width), bf16),
+        pltpu.VMEM((2, 2, 4, 128, width), bf16),
+        pltpu.VMEM((2, 2, 64, width), bf16),
+        pltpu.VMEM((2, 2, 64, width), bf16),
+        pltpu.VMEM((2, 4, 64, width), bf16),
+        pltpu.VMEM((2, 2, 2, 64, width), bf16),
+        pltpu.VMEM((2, 2, 32, width), bf16),
+        pltpu.VMEM((2, 2, 64, width), bf16),
     ]
 
 
-def home_steps(p, wire, sems, gated, sel, info, rows, out, cat, q, a1, b1, a2, b2, c1, c2):
+def home_steps(p, wire, sems, gated, sel, info, rows, more, out, cat, q, a1, b1, a2, b2, c1, c2):
     yh, co, yl, x = p.yh, p.co, p.yl, p.x
     ys = [(yy // 2, lax.rem(yy, 2)) for yy in (p.yr, p.ylf, p.yo)]
     (rh, rl), (lh, ll), (oh, ol) = ys
+    pieces = [(View(rows), slice(0, 2048))]
+    if more is not None:
+        pieces.append((View(more), slice(2048, 2048 + 128)))
     rows, out, whole_q, whole_cat = View(rows), View(out), q, cat
+    width = cat.shape[-1]
     q, cat, a1, b1, a2, b2, c1, c2 = (View(ref) for ref in (q, cat, a1, b1, a2, b2, c1, c2))
     own, first = [], []
     for e in range(EXP_DEV):
         lines = pl.ds(e * 2 * CAP, 2 * CAP)
         there = pl.ds((2 + e) * 2 * CAP, 2 * CAP)
-        first.append(wire.send(rows.at[e, :, 1 - co], cat.at[:, :, there], p.C))
-        own.append(local(rows.at[e, :, co], cat.at[:, :, lines], sems, e))
+        for piece, lanes in pieces:
+            first.append(wire.send(piece.at[e, :, 1 - co], cat.at[:, :, there, lanes], p.C))
+            own.append(local(piece.at[e, :, co], cat.at[:, :, lines, lanes], sems, len(own)))
     yield
     for copy in own:
         copy.wait()
@@ -867,13 +919,14 @@
         )
         hit, gate = slot_hits(table, 4, False)
         value = jnp.where(hit, gate if gated else 1.0, 0.0).astype(bf16)
-        for c in range(0, 2048, 512):
+        for c in range(0, width, 512):
+            lanes = slice(c, min(c + 512, width))
             total = jnp.dot(
-                value, whole_cat[h, pair, :, c : c + 512], preferred_element_type=f32
+                value, whole_cat[h, pair, :, lanes], preferred_element_type=f32
             ).astype(bf16)
             at = lax.rem(pair, 2) * 2
-            whole_q[h, pair // 2, at, :, c : c + 512] = total[:128]
-            whole_q[h, pair // 2, at + 1, :, c : c + 512] = total[128:]
+            whole_q[h, pair // 2, at, :, lanes] = total[:128]
+            whole_q[h, pair // 2, at + 1, :, lanes] = total[128:]
         return carry
 
     lax.fori_loop(0, 8, place, 0)
@@ -953,7 +1006,7 @@
 
 
 def by_place(rows):
-    return rows.reshape(EXP_DEV, 2, 2, 4, 2 * CAP, 2048)
+    return rows.reshape(EXP_DEV, 2, 2, 4, 2 * CAP, -1)
 
 
 def backward_kernel(
@@ -962,7 +1015,7 @@
 ):
     p = Place()
     greet_plane(p)
-    moving = home_steps(p, Wire(ss, rs), ls, True, sel, info, y_places, mixture, *scratch)
+    moving = home_steps(p, Wire(ss, rs), ls, True, sel, info, y_places, None, mixture, *scratch)
     next(moving)
     n = cot.shape[1]
     wide, cut = 2048 // PARTS, FF // PARTS
@@ -1048,15 +1101,15 @@
             shaped((EXP_DEV, n, 2048)),
             shaped((EXP_DEV, 2048, FF)),
         ),
-        scratch=home_scratch(),
+        scratch=home_scratch(2048),
         vmem=58 << 20,
     )(sel, info, by_place(y), y, cot, gate, up, hidden, row_gates, w_in, w_out)
 
 
-def finish_kernel(sel, info, places, rows, dgate, dup, home, term, ss, rs, ls, *scratch):
+def finish_kernel(sel, info, places, more, rows, dgate, dup, home, term, ss, rs, ls, *scratch):
     p = Place()
     greet_plane(p)
-    moving = home_steps(p, Wire(ss, rs), ls, False, sel, info, places, home, *scratch)
+    moving = home_steps(p, Wire(ss, rs), ls, False, sel, info, places, more, home, *scratch)
     next(moving)
     n = rows.shape[1]
     wide = 2048 // PARTS
@@ -1079,33 +1132,69 @@
         pass
 
 
-def expert_finish(sel, info, drows, rows, dgate, dup, cid):
+def expert_finish(sel, info, drows, more, rows, dgate, dup, cid):
     return remote_call(
         finish_kernel,
         "expert_finish",
         cid,
         HOME_SENDS,
-        2,
-        [VMEM, VMEM] + [ANY] * 4,
+        4,
+        [VMEM, VMEM] + [ANY] * 5,
         [VMEM, ANY],
-        (shaped((128, 2048), f32), shaped((EXP_DEV, 2048, 2 * FF))),
-        scratch=home_scratch(),
+        (shaped((128, 2048 + 128), f32), shaped((EXP_DEV, 2048, 2 * FF))),
+        scratch=home_scratch(2048 + 128),
         vmem=58 << 20,
-    )(sel, info, by_place(drows), rows, dgate, dup)
-
-
-def fold_kernel(
-    p0, p1, p2, p3, small, out, whole, ss, rs, ls,
+    )(sel, info, by_place(drows), by_place(more), rows, dgate, dup)
+
+
+def unstack_kernel(grads, out, held, sems):
+    e, j, steps = pl.program_id(0), pl.program_id(1), pl.num_programs(1)
+    step = e * steps + j
+    count = grads.shape[1]
+
+    def copy(at):
+        slot = lax.rem(at, 2)
+        rows = pl.ds(pl.multiple_of(lax.rem(at, steps) * count, count), count)
+        return pltpu.make_async_copy(held.at[slot], out.at[rows, at // steps], sems.at[slot])
+
+    @pl.when(step >= 2)
+    def _():
+        copy(step - 2).wait()
+
+    held[lax.rem(step, 2)] = grads[0].astype(f32)
+    copy(step).start()
+
+    @pl.when(step == EXP_DEV * steps - 1)
+    def _():
+        copy(step - 1).wait()
+        copy(step).wait()
+
+
+def unstack(grads):
+    experts, rows, cols = grads.shape
+    count = 128
+    return pl.pallas_call(
+        unstack_kernel,
+        name="unstack",
+        grid=(experts, rows // count),
+        out_shape=shaped((rows, experts, cols), f32),
+        in_specs=[pl.BlockSpec((1, count, cols), lambda e, j: (e, j, 0))],
+        out_specs=ANY,
+        scratch_shapes=[pltpu.VMEM((2, count, cols), f32), DMA((2,))],
+        compiler_params=pltpu.CompilerParams(vmem_limit_bytes=60 << 20),
+    )(grads)
+
+
+def last_kernel(
+    grads, kept, w, rows, cosine, sine, gain, p3, unit, small, out, normed, whole, ss, rs, ls,
+    flat, total, w_grads, part, got_c, got_h, half, mine,
     ra, rb, rc, rd, re, rf, rg, acc_x, acc_y, sz, az, sx, ax, sy, ay, sc, ac, sh,
 ):
     p = Place()
     dp, yl, x = p.dp, p.yl, p.x
     greet([p.ZR, p.ZL, p.ZO, p.XR, p.XL, p.XO, p.Y, p.C, p.H])
     wire = Wire(ss, rs)
-    zs_out = [
-        wire.send(small.at[there], sz.at[i], device)
-        for i, (there, device) in enumerate(((p.zo, p.ZO), (p.zr, p.ZR), (p.zl, p.ZL)))
-    ]
+    p0, p1, p2 = (w_grads.at[i] for i in range(3))
 
     def added(dst, *srcs):
         total = srcs[0][...].astype(f32)
@@ -1120,108 +1209,174 @@
 
         lax.fori_loop(0, count, step, 0)
 
-    firsts = []
-    for i, part in ((2, p2), (3, p3)):
-        firsts.append(wire.send(part.at[:, 1 - yl], rb.at[i - 2], p.Y))
+    def y_first(i, part):
+        return wire.send(part.at[:, 1 - yl], rb.at[i - 2], p.Y)
+
+    firsts = {3: y_first(3, p3)}
+    for d in range(4):
+        mine[d] = small[d]
     starts = []
-    for i, part in ((0, p0), (1, p1)):
-        starts.append(
-            (
-                wire.send(part.at[0:2, :, p.xo], ra.at[i, 0], p.XR),
-                wire.send(part.at[2:4, :, p.xo], ra.at[i, 1], p.XL),
+    for i in range(3):
+        if i < 2:
+            gained = jnp.zeros((1, HD), f32)
+            for h in range(4):
+                grad = turned(grads[i, h].astype(f32), cosine[...], -sine[...])
+                head = kept[i, h]
+                inverse = rms_rows(head)
+                gained += jnp.sum(grad * head * inverse, axis=0, keepdims=True)
+                back = rms_back(head, inverse, grad * gain[i])
+                flat[:, h * HD : (h + 1) * HD] = back.astype(bf16)
+            mine[0, 1, 0, 32 + i : 33 + i] = gained
+        else:
+            for h in range(4):
+                flat[:, h * HD : (h + 1) * HD] = grads[i, h]
+
+        def weight_rows(c, carry):
+            cols = pl.ds(pl.multiple_of(c * 512, 512), 512)
+            grad = tn(rows[:, cols], flat[...]).astype(bf16)
+            w_grads[i, c] = grad.reshape(2, 4, 64, 512)
+            return carry
+
+        lax.fori_loop(0, 4, weight_rows, 0)
+        if i < 2:
+            gradient = w_grads.at[i]
+            starts.append(
+                (
+                    wire.send(gradient.at[0:2, :, p.xo], ra.at[i, 0], p.XR),
+                    wire.send(gradient.at[2:4, :, p.xo], ra.at[i, 1], p.XL),
+                )
             )
-        )
+        else:
+            firsts[2] = y_first(2, p2)
+
+        def normed_cols(c, carry):
+            cols = pl.ds(pl.multiple_of(c * 512, 512), 512)
+            value = nt(flat[...], w[i, cols])
+            if i > 0:
+                value += total[:, cols]
+            if i < 2:
+                total[:, cols] = value
+            else:
+                part[:, :, cols] = value.astype(bf16).reshape(4, 128, 512)
+            return carry
+
+        lax.fori_loop(0, 4, normed_cols, 0)
+    mine_head, other = p.yh * 2 + (1 - p.co), (1 - p.yh) * 2 + (1 - p.co)
+    far = wire.send(part.at[other], got_c.at[0], p.C)
+    near = wire.send(part.at[mine_head], got_c.at[1], p.C)
+    far.wait_recv()
+
+    def by_16(body):
+        def step(i, carry):
+            body(pl.ds(pl.multiple_of(i * 16, 16), 16))
+            return carry
+
+        lax.fori_loop(0, 8, step, 0)
+
+    def add_far(at):
+        away = part[(1 - p.yh) * 2 + p.co, at].astype(f32)
+        half[at] = (away + got_c[0, at].astype(f32)).astype(bf16)
+
+    by_16(add_far)
+    over = wire.send(half, got_h, p.H)
     seconds = []
-    for i, part in ((0, p0), (1, p1)):
+    for i, gradient in ((0, p0), (1, p1)):
         one, two = starts[i]
         one.wait_recv()
-        loop(2, lambda d: added(part.at[d, :, p.xr], part.at[d, :, p.xr], ra.at[i, 0, d]))
-        s1 = wire.send(part.at[:, :, p.xr], rc.at[i, 0], p.XR)
+        loop(2, lambda d: added(gradient.at[d, :, p.xr], gradient.at[d, :, p.xr], ra.at[i, 0, d]))
+        s1 = wire.send(gradient.at[:, :, p.xr], rc.at[i, 0], p.XR)
         two.wait_recv()
-        loop(2, lambda d: added(part.at[d + 2, :, p.xl], part.at[d + 2, :, p.xl], ra.at[i, 1, d]))
-        s2 = wire.send(part.at[:, :, p.xl], rc.at[i, 1], p.XL)
+        loop(
+            2,
+            lambda d: added(gradient.at[d + 2, :, p.xl], gradient.at[d + 2, :, p.xl], ra.at[i, 1, d]),
+        )
+        s2 = wire.send(gradient.at[:, :, p.xl], rc.at[i, 1], p.XL)
         seconds.append((s1, s2))
+    mids = {}
+    for i, gradient in ((3, p3), (2, p2)):
+        firsts[i].wait_recv()
+        loop(4, lambda d: added(acc_y.at[i - 2, d], gradient.at[d, yl], rb.at[i - 2, d]))
+        acc = acc_y.at[i - 2]
+        mids[i] = (
+            wire.send(acc.at[0:2, p.xo], rd.at[i - 2, 0], p.XR),
+            wire.send(acc.at[2:4, p.xo], rd.at[i - 2, 1], p.XL),
+        )
+    near.wait_recv()
+    over.wait_recv()
+
+    def add_near(at):
+        close = part[p.yh * 2 + p.co, at].astype(f32) + got_c[1, at].astype(f32)
+        normed[at] = close + got_h[at].astype(f32)
+
+    by_16(add_near)
+    for c in range(16):
+        cols = slice(c * 128, (c + 1) * 128)
+        column = jnp.sum(normed[:, cols] * unit[:, cols], axis=0, keepdims=True)
+        mine[0, 0, c // 8, 32 + c % 8 : 33 + c % 8] = column
+    zs_out = [
+        wire.send(mine.at[there], sz.at[i], device)
+        for i, (there, device) in enumerate(((p.zo, p.ZO), (p.zr, p.ZR), (p.zl, p.ZL)))
+    ]
+    yends = []
+    for i, gradient in ((0, p0), (1, p1)):
+        for s in seconds[i]:
+            s.wait_recv()
+        acc = acc_x.at[i]
+        loop(4, lambda d: added(acc.at[d], gradient.at[d, :, x], rc.at[i, 0, d], rc.at[i, 1, d]))
+        yends.append(wire.send(acc.at[:, 1 - yl], re.at[i], p.Y))
     for copy in zs_out:
         copy.wait_recv()
-    for half in range(2):
-        az[half] = small[dp, half] + sz[0, half] + sz[1, half] + sz[2, half]
+    for y in range(2):
+        az[y] = mine[dp, y] + sz[0, y] + sz[1, y] + sz[2, y]
     xs_out = [
         wire.send(az.at[:, there], sx.at[i], device)
         for i, (there, device) in enumerate(((p.xo, p.XO), (p.xr, p.XR), (p.xl, p.XL)))
     ]
-    mids = []
-    for i, part in ((2, p2), (3, p3)):
-        firsts[i - 2].wait_recv()
-        loop(4, lambda d: added(acc_y.at[i - 2, d], part.at[d, yl], rb.at[i - 2, d]))
+    xends = {}
+    for i in (3, 2):
         acc = acc_y.at[i - 2]
-        mids.append(
-            (
-                wire.send(acc.at[0:2, p.xo], rd.at[i - 2, 0], p.XR),
-                wire.send(acc.at[2:4, p.xo], rd.at[i - 2, 1], p.XL),
-            )
-        )
-    for copy in xs_out:
-        copy.wait_recv()
-    ax[...] = az[:, x] + sx[0] + sx[1] + sx[2]
-    y_out = wire.send(ax.at[1 - yl], sy, p.Y)
-    yends = []
-    for i, part in ((0, p0), (1, p1)):
-        for s in seconds[i]:
-            s.wait_recv()
-        acc = acc_x.at[i]
-        loop(4, lambda d: added(acc.at[d], part.at[d, :, x], rc.at[i, 0, d], rc.at[i, 1, d]))
-        yends.append(wire.send(acc.at[:, 1 - yl], re.at[i], p.Y))
-    y_out.wait_recv()
-    ay[...] = ax[yl] + sy[...]
-    c_out = wire.send(ay, sc, p.C)
-    xends = []
-    for i in (2, 3):
-        acc = acc_y.at[i - 2]
-        one, two = mids[i - 2]
+        one, two = mids[i]
         one.wait_recv()
         loop(2, lambda d: added(acc.at[d, p.xr], acc.at[d, p.xr], rd.at[i - 2, 0, d]))
         s1 = wire.send(acc.at[:, p.xr], rf.at[i - 2, 0], p.XR)
         two.wait_recv()
         loop(2, lambda d: added(acc.at[d + 2, p.xl], acc.at[d + 2, p.xl], rd.at[i - 2, 1, d]))
         s2 = wire.send(acc.at[:, p.xl], rf.at[i - 2, 1], p.XL)
-        xends.append((s1, s2))
-    parts = []
-    zs = []
+        xends[i] = (s1, s2)
+    for copy in xs_out:
+        copy.wait_recv()
+    ax[...] = az[:, x] + sx[0] + sx[1] + sx[2]
+    y_out = wire.send(ax.at[1 - yl], sy, p.Y)
+    parts, zs = {}, {}
 
     def z_first(i, acc):
-        parts.append(acc)
-        zs.append(
-            (
-                wire.send(acc.at[p.zo, 0:32], rg.at[i, 0, 0:32], p.ZR),
-                wire.send(acc.at[p.zo, 32:64], rg.at[i, 1, 0:32], p.ZL),
-            )
+        parts[i] = acc
+        zs[i] = (
+            wire.send(acc.at[p.zo, 0:32], rg.at[i, 0, 0:32], p.ZR),
+            wire.send(acc.at[p.zo, 32:64], rg.at[i, 1, 0:32], p.ZL),
         )
 
-    c_out.wait_recv()
-    ac[...] = ay[...] + sc[...]
-    h_out = wire.send(ac, sh, p.H)
     for i in (0, 1):
         yends[i].wait_recv()
         acc = acc_x.at[i]
         loop(4, lambda d: added(acc.at[d, yl], acc.at[d, yl], re.at[i, d]))
         z_first(i, acc.at[:, yl])
-    h_out.wait_recv()
-    whole[dp, yl, x] = ac[...] + sh[...]
-    y_all = wire.send(whole.at[dp, yl, x], whole.at[dp, yl, x], p.Y)
-    for i in (2, 3):
-        for s in xends[i - 2]:
+    y_out.wait_recv()
+    ay[...] = ax[yl] + sy[...]
+    c_out = wire.send(ay, sc, p.C)
+    for i in (3, 2):
+        for s in xends[i]:
             s.wait_recv()
         acc = acc_y.at[i - 2]
         loop(
             4, lambda d: added(acc.at[d, x], acc.at[d, x], rf.at[i - 2, 0, d], rf.at[i - 2, 1, d])
         )
         z_first(i, acc.at[:, x])
-    y_all.wait_recv()
-    x_all = [
-        wire.send(whole.at[dp, :, x], whole.at[dp, :, x], device) for device in (p.XO, p.XR, p.XL)
-    ]
-    ends = []
-    for i in range(4):
+    c_out.wait_recv()
+    ac[...] = ay[...] + sc[...]
+    h_out = wire.send(ac, sh, p.H)
+    ends = {}
+    for i in (0, 1, 3, 2):
         one, two = zs[i]
         acc = parts[i]
         one.wait_recv()
@@ -1230,30 +1385,49 @@
         two.wait_recv()
         added(acc.at[p.zl, 32:64], acc.at[p.zl, 32:64], rg.at[i, 1, 0:32])
         s2 = wire.send(acc.at[p.zl], rg.at[i, 3], p.ZL)
-        ends.append((s1, s2))
-    for copy in x_all:
-        copy.wait_recv()
-    z_all = [wire.send(whole.at[dp], whole.at[dp], device) for device in (p.ZO, p.ZR, p.ZL)]
+        ends[i] = (s1, s2)
+    h_out.wait_recv()
+    whole[dp, yl, x] = ac[...] + sh[...]
+    y_all = wire.send(whole.at[dp, yl, x], whole.at[dp, yl, x], p.Y)
+    y_all.wait_recv()
+    x_all = [
+        wire.send(whole.at[dp, :, x], whole.at[dp, :, x], device) for device in (p.XO, p.XR, p.XL)
+    ]
     for i in range(4):
         for s in ends[i]:
             s.wait_recv()
         added(out.at[i], parts[i].at[dp], rg.at[i, 2], rg.at[i, 3])
+    for copy in x_all:
+        copy.wait_recv()
+    z_all = [wire.send(whole.at[dp], whole.at[dp], device) for device in (p.ZO, p.ZR, p.ZL)]
     for copy in z_all:
         copy.wait_recv()
     wire.drain()
 
 
-def fold_grads(grads, small):
+def last_sums(grads, kept, w, rows, cosine, sine, gains, fourth, unit, small):
     return remote_call(
-        fold_kernel,
-        "fold_grads",
+        last_kernel,
+        "last_sums",
         8,
-        52,
+        55,
         1,
-        [VMEM] * 5,
-        [VMEM] * 2,
-        (shaped((4, 64, 512), f32), shaped((4, 2, 4, 40, 128), f32)),
+        [VMEM] * 10,
+        [VMEM] * 3,
+        (
+            shaped((4, 64, 512), f32),
+            shaped((128, 2048), f32),
+            shaped((4, 2, 4, 40, 128), f32),
+        ),
         scratch=[
+            pltpu.VMEM((512, 512), bf16),
+            pltpu.VMEM((512, 2048), f32),
+            pltpu.VMEM((3, 4, 2, 4, 64, 512), bf16),
+            pltpu.VMEM((4, 128, 2048), bf16),
+            pltpu.VMEM((2, 128, 2048), bf16),
+            pltpu.VMEM((128, 2048), bf16),
+            pltpu.VMEM((128, 2048), bf16),
+            pltpu.VMEM((4, 2, 4, 40, 128), f32),
             pltpu.VMEM((2, 2, 2, 2, 64, 512), bf16),
             pltpu.VMEM((2, 4, 4, 64, 512), bf16),
             pltpu.VMEM((2, 2, 4, 2, 64, 512), bf16),
@@ -1273,8 +1447,11 @@
             pltpu.VMEM((40, 128), f32),
             pltpu.VMEM((40, 128), f32),
         ],
-        vmem=48 << 20,
-    )(*[g.reshape(4, 2, 4, 64, 512) for g in grads], small.reshape(4, 2, 4, 40, 128))
+        vmem=60 << 20,
+    )(
+        grads, kept, w, rows, cosine, sine, gains,
+        fourth.reshape(4, 2, 4, 64, 512), unit, small.reshape(4, 2, 4, 40, 128),
+    )
 
 
 def on_device(
@@ -1308,7 +1485,9 @@
     query_ids = (jnp.arange(4)[:, None] * 1024 + blk * 128 + jnp.arange(128)[None]).reshape(-1)
     frequency = rope_base ** (-jnp.arange(64, dtype=f32) / 64)
     angles = query_ids.astype(f32)[:, None] * frequency[None]
-    cosine, sine = jnp.cos(angles)[None], jnp.sin(angles)[None]
+    cosine, sine = jnp.cos(angles), jnp.sin(angles)
+    cosine = jnp.concatenate([cosine, cosine], axis=1)
+    sine = jnp.concatenate([-sine, sine], axis=1)
     half_ids = (jnp.arange(4)[:, None] * 1024 + yl * 512 + jnp.arange(512)[None]).reshape(-1)
     half_seg = lax.dynamic_index_in_dim(segment.reshape(4, 2, 512), yl, 1, keepdims=False).reshape(-1)
     key_seg = jnp.where(valid > 0, segment, -1)
@@ -1317,17 +1496,12 @@
     upper = (jnp.sum(segment[None] <= ends[:, -1:], axis=1, dtype=i32) + KB - 1) // KB
     limits = jnp.stack([lower, upper])
 
-    def rotary(values, turning):
-        a, b = values[..., :64], values[..., 64:]
-        turned = turning * sine
-        return jnp.concatenate([a * cosine - b * turned, b * cosine + a * turned], axis=-1)
-
     inputs = tokens.astype(f32)
     first_inv = rms_rows(inputs)
     normed = (inputs * first_inv * attn_gain).astype(bf16)
     w_three = jnp.stack([w_query, w_key, w_value])
     gathered, out_part, normed_all = gather_weights(w_three, w_out, normed)
-    full_query, full_key, full_value = (gathered[i].reshape(2048, 512) for i in range(3))
+    full_three = gathered.reshape(3, 2048, 512)
     normed_all = normed_all.reshape(512, width)
 
     def by_head(flat):
@@ -1336,20 +1510,10 @@
     def flat_of(heads):
         return jnp.transpose(heads.reshape(4, 512, HD), (1, 0, 2)).reshape(512, 512)
 
-    query_proj = by_head(jnp.dot(normed_all, full_query, preferred_element_type=f32))
-    key_proj = by_head(jnp.dot(normed_all, full_key, preferred_element_type=f32))
-    value_heads = by_head(jnp.dot(normed_all, full_value, preferred_element_type=f32).astype(bf16))
-    query_inv = rms_rows(query_proj)
-    query_unit = query_proj * query_inv
-    query_heads = rotary(query_unit * query_gain, 1.0).astype(bf16)
-    key_inv = rms_rows(key_proj)
-    key_unit = key_proj * key_inv
-    key_heads = rotary(key_unit * key_gain, 1.0).astype(bf16)
-
+    head_gains = jnp.stack([query_gain, key_gain])[:, None]
+    heads, projected = project(normed_all, full_three, cosine, sine, head_gains)
     runs = (4, 4, 128, HD)
-    q, k, v, full_out = heads_over_x(
-        query_heads.reshape(runs), key_heads.reshape(runs), value_heads.reshape(runs), out_part
-    )
+    q, k, v, full_out = heads_over_x(heads.reshape((3,) + runs), out_part)
     q, k, v = q.reshape(2048, HD), k.reshape(4096, HD), v.reshape(4096, HD)
     full_out = full_out.reshape(2048, 512)
     att_low, att, inverse = attend(limits, q, k, v, half_seg, half_ids, key_seg)
@@ -1371,11 +1535,6 @@
     gate_total = jnp.sum(chosen, axis=-1, keepdims=True)
     gates = chosen / gate_total
 
-    code = jnp.transpose(slot_code.reshape(tok, 32, EXP_DEV), (0, 2, 1))
-    home_hot = code[..., None] == jnp.arange(CAP, dtype=f32)
-    def to_peers(rows):
-        return lax.all_to_all(rows, ("head", "blk"), split_axis=1, concat_axis=1, tiled=True)
-
     sent = jnp.concatenate([normed_ffn, slot_code.astype(bf16), gates.astype(bf16)], axis=1)
     everyone = spread(sent, 7)
     lane = jnp.arange(128)[None]
@@ -1386,33 +1545,38 @@
     nearby = (device ^ 8) * EXP_DEV
     column = sel_row % 2 + jnp.where(sel_row // 2 % 2 == 0, device * EXP_DEV, nearby)
     sel_chip = (lane == column + (sel_row // 4) * EXPERTS).astype(bf16)
-    expert_rows, row_gates = pick_rows(sel, info, everyone, width, True)
+    flat_info, flat_everyone = info.reshape(32 * tok, -1), everyone.reshape(32 * tok, -1)
+    expert_rows, row_gates = pick_rows(sel, flat_info, flat_everyone, width, True)
     expert_rows = expert_rows.reshape(EXP_DEV, -1, width)
     row_gates = row_gates.reshape(EXP_DEV, -1, 128)
     all_cot, gate_part, up_part, hidden, expert_result = expert_forward(
         cotangent, expert_rows, full_in, full_back, 11
     )
-    (arrived_cot,) = pick_rows(sel, info, all_cot, width, False)
+    (arrived_cot,) = pick_rows(sel, flat_info, all_cot.reshape(32 * tok, width), width, False)
     arrived_cot = arrived_cot.reshape(EXP_DEV, -1, width)
     mixture, row_dots, grad_gate, grad_up, grad_rows, term_back = expert_backward(
         sel_chip, info, expert_result, arrived_cot, gate_part, up_part, hidden, row_gates,
         full_in, full_back, 12,
     )
+    row_dots = jnp.sum(row_dots, axis=-1, keepdims=True)
+    high = row_dots.astype(bf16)
+    column = (device * EXP_DEV + jnp.arange(EXP_DEV))[:, None, None]
+    low = jnp.where(lane == column + EXPERTS, (row_dots - high.astype(f32)).astype(bf16), 0)
+    row_dots = jnp.where(lane == column, high, low)
     grad_home, term_in = expert_finish(
-        sel_chip, info, grad_rows, expert_rows, grad_gate, grad_up, 13
+        sel_chip, info, grad_rows, row_dots, expert_rows, grad_gate, grad_up, 13
     )
-    back_dots = to_peers(jnp.sum(row_dots, axis=-1).reshape(EXP_DEV, 32, CAP))
+    grad_gates = grad_home[:, width : width + EXPERTS] + grad_home[:, width + EXPERTS :]
+    grad_home = grad_home[:, :width]
 
     def fold_dp(term):
         return lax.psum_scatter(term.astype(bf16), "dp", scatter_dimension=1, tiled=True)
 
-    expert_out_grad = jnp.transpose(fold_dp(term_back), (1, 0, 2)).astype(f32)
-    expert_in_grad = jnp.transpose(fold_dp(term_in), (1, 0, 2)).astype(f32)
+    expert_out_grad = unstack(fold_dp(term_back))
+    expert_in_grad = unstack(fold_dp(term_in))
 
     output = (middle + mixture).astype(bf16)
     grad_out = cotangent.astype(f32)
-    grad_gates = jnp.sum(jnp.where(home_hot, back_dots, 0.0), axis=-1)
-    grad_gates = jnp.transpose(grad_gates, (0, 2, 1)).reshape(tok, EXPERTS)
     mean_grad = jnp.sum(grad_gates * gates, axis=-1, keepdims=True)
     grad_probs = (grad_gates - mean_grad) / gate_total * hot
     grad_logits = probabilities * (
@@ -1438,41 +1602,17 @@
         limits, q, k, v, grad_att, half_seg, half_ids, key_seg, inverse[:, 0], delta
     )
     cut = (4, 2, 4, 128, HD)
-    grad_query, grad_key, grad_value = grads_over_x(
-        dq.reshape(runs), dk.reshape(cut), dv.reshape(cut)
+    grad_heads = grads_over_x(dq.reshape(runs), dk.reshape(cut), dv.reshape(cut))
+    out_grad = jnp.einsum(
+        "qc,qf->cf", branch_all, attended_flat, preferred_element_type=f32
+    ).astype(bf16)
+    gains = jnp.pad(ffn_gain_term, (width, 32 * 8 * 128 - 2 * width)).reshape(32, 8, 128)
+    small = jnp.concatenate([router_term.reshape(32, 32, 128), gains], axis=1)
+    attn_grads, grad_normed, summed = last_sums(
+        grad_heads.reshape(3, 4, 512, HD), projected, full_three, normed_all, cosine, sine,
+        head_gains, out_grad, inputs * first_inv, small,
     )
-    heads_shape = (4, 512, HD)
-    grad_query_unit = rotary(grad_query.reshape(heads_shape).astype(f32), -1.0)
-    query_gain_term = jnp.sum(grad_query_unit * query_unit, axis=(0, 1))
-    grad_query_flat = flat_of(
-        rms_back(query_proj, query_inv, grad_query_unit * query_gain).astype(bf16)
-    )
-    grad_key_unit = rotary(grad_key.reshape(heads_shape).astype(f32), -1.0)
-    key_gain_term = jnp.sum(grad_key_unit * key_unit, axis=(0, 1))
-    grad_key_flat = flat_of(rms_back(key_proj, key_inv, grad_key_unit * key_gain).astype(bf16))
-    grad_value_flat = flat_of(grad_value)
-    normed_part = jnp.einsum("qc,dc->qd", grad_query_flat, full_query, preferred_element_type=f32)
-    normed_part += jnp.einsum("qc,dc->qd", grad_key_flat, full_key, preferred_element_type=f32)
-    normed_part += jnp.einsum("qc,dc->qd", grad_value_flat, full_value, preferred_element_type=f32)
-    grad_normed = sum_rows(normed_part.astype(bf16), 10)
-    attn_gain_term = jnp.sum(grad_normed * inputs * first_inv, axis=0)
     input_grad = grad_middle + rms_back(inputs, first_inv, grad_normed * attn_gain)
-
-    def weight_grad(rows, grads):
-        return jnp.einsum("qc,qf->cf", rows, grads, preferred_element_type=f32).astype(bf16)
-
-    gains = jnp.concatenate([attn_gain_term, ffn_gain_term, query_gain_term, key_gain_term])
-    gains = jnp.pad(gains, (0, 32 * 8 * 128 - gains.shape[0])).reshape(32, 8, 128)
-    small = jnp.concatenate([router_term.reshape(32, 32, 128), gains], axis=1)
-    attn_grads, summed = fold_grads(
-        [
-            weight_grad(normed_all, grad_query_flat),
-            weight_grad(normed_all, grad_key_flat),
-            weight_grad(normed_all, grad_value_flat),
-            weight_grad(branch_all, attended_flat),
-        ],
-        small,
-    )
     summed = summed.reshape(32, 40, 128)
     router_grad = summed[:, :32].reshape(router.shape)
     gains = summed[:, 32:].reshape(-1)

time: 825 us -> 765 us (0.927)
  local copies, waits for them, and re-layouts: 103 us -> 48.3 us
  Pallas kernels: 628 us -> 658 us
  matrix products: 29.9 us -> 13.1 us
  other arithmetic: 31.6 us -> 19.6 us
    pallas_call x3 -> x6, Pallas kernels: 192 us -> 241 us  [the longest x1 107 us: last_sums(): remote_call(last_kernel, 'last_sums', 8, 55, 1, [VMEM] * 10, [VMEM] * 3,...]
    unnamed x147 -> x87, local copies, waits for them, and re-layouts: 58.6 us -> 27.8 us
    dot_general x10 -> x1, matrix products: 20.7 us -> 2.63 us  [on_device(): jnp.einsum('qc,qf->cf', branch_all, attended_flat, preferred_element_type...]
    pallas_call x2 -> x1, Pallas kernels: 31.4 us -> 15.6 us  [sum_rows(): remote_call(sum_kernel, 'sum_rows', cid, 3, 1, [VMEM], [VMEM], (shaped((1...]
  transfers between devices with their start and end apart: 5 -> 4, of which waited for: 1 -> 0; matrix products, arithmetic and copies ran while one was open for 15% -> 8% of each run, Pallas kernels for 58% -> 66%
where the time goes in v4:
time: 765 us; the launch traced here: 754 us
  Pallas kernels  658 us (86%)
  local copies, waits for them, and re-layouts  48.3 us (6%)
  other arithmetic  19.6 us (3%)
  between operations  15 us (2%)
  matrix products  13.1 us (2%)
    pallas_call x1, Pallas kernels, last_sums(): remote_call(last_kernel, 'last_sums', 8, 55, 1, [VMEM] * 10, [VMEM] * 3,...  107 us
    pallas_call x1, Pallas kernels, expert_backward(): remote_call(backward_kernel, 'expert_backward', cid, HOME_SENDS, 2, [VMEM...  81.6 us
    pallas_call x1, Pallas kernels, gather_weights(): remote_call(weights_kernel, 'gather_weights', 1, 24, 3, [ANY] * 3, [ANY]...  73.8 us
    pallas_call x1, Pallas kernels, expert_finish(): remote_call(finish_kernel, 'expert_finish', cid, HOME_SENDS, 4, [VMEM, VM...  71.5 us
    pallas_call x1, Pallas kernels, spread(): remote_call(spread_kernel, 'spread', cid, SPREAD_SENDS, 1, [ANY], [ANY],...  66.7 us
    pallas_call x1, Pallas kernels, expert_forward(): remote_call(forward_kernel, 'expert_forward', cid, SPREAD_SENDS, 1, [ANY]...  56.8 us
    pallas_call x1, Pallas kernels, heads_over_x(): remote_call(heads_kernel, 'heads_over_x', 3, 22, 4, [ANY] * 2, [ANY] * 4,...  39.9 us
    unnamed x87, local copies, waits for them, and re-layouts  27.8 us
  transfers between devices with their start and end apart: 4, of which 0 were waited for; matrix products, arithmetic and copies ran while one was open for 8% of the time, Pallas kernels for 66%

profile of v4, /device:TPU:0, one launch (start us, length us, event | category | flops | bytes accessed | tf_op | source)
XLA Modules:
  0.0 754.2 jit_solution(2075001840540595271)
XLA Ops:
  7.2 3.5 copy.105
  10.8 6.1 copy.104
  22.2 73.8 %gather_weights.1 = (bf16[3,4,2,4,64,512]{5,4,3,2,1,0:T(8,128)(2,1)}, bf16[4,64,512]{2,1,0:T(8,128)(2,1)}, bf16[4,128,2048]{2,1,0:T(8,128)(2,1)}) custom-call(bf16[3,64,512]{2,1,0:T(8,128)(2,1)} %pad_maximum_fusion.3.w, bf16[64,512]{1,0:T(8,128)(2,1)} %wo.1, bf16[128,2048]{1,0:T(8,128)(2,1)} %get-tuple-element.152.n), custom_call_target="tpu_custom_call" | custom-call | tf_op jit(solution)/shard_map/gather_weights/pallas_call | solution.py:227
  98.8 9.7 %project.1 = (bf16[3,4,512,128]{3,2,1,0:T(8,128)(2,1)}, f32[2,4,512,128]{3,2,1,0:T(8,128)}) custom-call(bf16[512,2048]{1,0:T(8,128)(2,1)} %bitcast.143, bf16[3,2048,512]{2,1,0:T(8,128)(2,1)} %bitcast.134, f32[512,128]{1,0:T(8,128)} %get-tuple-element.171.cosine, f32[512,128]{1,0:T(8,128)} %get-tuple-element.172.sine, f32[2,1,128]{2,1,0:T(1,128)} %bitcast.166), custom_call_target="tpu_custom_call" | custom-call | tf_op jit(solution)/shard_map/project/pallas_call | solution.py:500
  108.5 39.9 %heads_over_x.1 = (bf16[4,4,128,128]{3,2,1,0:T(8,128)(2,1)}, bf16[4,2,4,128,128]{4,3,2,1,0:T(8,128)(2,1)}, bf16[4,2,4,128,128]{4,3,2,1,0:T(8,128)(2,1)}, bf16[4,2,4,64,512]{4,3,2,1,0:T(8,128)(2,1)}) custom-call(bf16[3,4,4,128,128]{4,3,2,1,0:T(8,128)(2,1)} %bitcast.151, bf16[4,64,512]{2,1,0:T(8,128)(2,1)} %get-tuple-element.49.go), custom_call_target="tpu_custom_call" | custom-call | tf_op jit(solution)/shard_map/heads_over_x/pallas_call | solution.py:358
  152.4 14.4 %attend.1 = (bf16[2048,128]{1,0:T(8,128)(2,1)S(1)}, f32[2048,128]{1,0:T(8,128)S(1)}, f32[2048,128]{1,0:T(8,128)S(1)}) custom-call(s32[2,8]{1,0:T(2,128)S(1)} %pad_add_fusion.lim, bf16[2048,128]{1,0:T(8,128)(2,1)S(1)} %bitcast.118, bf16[4096,128]{1,0:T(8,128)(2,1)S(1)} %bitcast.113, bf16[4096,128]{1,0:T(8,128)(2,1)S(1)} %bitcast.115, ...), custom_call_target="tpu_custom_call" | custom-call | tf_op jit(solution)/shard_map/attend/pallas_call | solution.py:565
  169.6 8.0 %back_over_x.1 = bf16[4,4,128,128]{3,2,1,0:T(8,128)(2,1)} custom-call(bf16[4,4,128,128]{3,2,1,0:T(8,128)(2,1)} %bitcast.122), custom_call_target="tpu_custom_call" | custom-call | tf_op jit(solution)/shard_map/back_over_x/pallas_call | solution.py:389
  178.8 3.1 convolution_convert_fusion.1
  181.9 15.6 %sum_rows.1 = f32[128,2048]{1,0:T(8,128)S(1)} custom-call(bf16[2,2,128,2048]{3,2,1,0:T(8,128)(2,1)S(1)} %bitcast.117), custom_call_target="tpu_custom_call" | custom-call | tf_op jit(solution)/shard_map/sum_rows/pallas_call | solution.py:295
  201.2 66.7 %spread.1 = bf16[2,2,2,4,128,2176]{5,4,3,2,1,0:T(8,128)(2,1)} custom-call(bf16[128,2176]{1,0:T(8,128)(2,1)} %concatenate.25.src), custom_call_target="tpu_custom_call" | custom-call | tf_op jit(solution)/shard_map/spread/pallas_call | solution.py:720
  270.9 13.4 %pick_rows.2 = (bf16[2,16,48,2048]{3,2,1,0:T(8,128)(2,1)}, f32[2,16,48,128]{3,2,1,0:T(8,128)}) custom-call(bf16[8,128]{1,0:T(8,128)(2,1)} %fusion.15.sel, bf16[4096,128]{1,0:T(8,128)(2,1)} %bitcast.132, bf16[4096,2176]{1,0:T(8,128)(2,1)} %bitcast.131), custom_call_target="tpu_custom_call" | custom-call | tf_op jit(solution)/shard_map/pick_rows/pallas_call | solution.py:859
  284.9 56.8 %expert_forward.1 = (bf16[2,2,2,4,128,2048]{5,4,3,2,1,0:T(8,128)(2,1)}, bf16[2,768,1024]{2,1,0:T(8,128)(2,1)S(1)}, bf16[2,768,1024]{2,1,0:T(8,128)(2,1)}, bf16[2...) custom-call(bf16[128,2048]{1,0:T(8,128)(2,1)S(1)} %copy-done.1, bf16[2,768,2048]{2,1,0:T(8,128)(2,1)} %bitcast.136, ...), custom_call_target="tpu_custom_call" | custom-call | tf_op jit(solution)/shard_map/expert_forward/pallas_call | solution.py:802
  343.4 13.1 %pick_rows.3 = bf16[2,16,48,2048]{3,2,1,0:T(8,128)(2,1)} custom-call(bf16[8,128]{1,0:T(8,128)(2,1)} %fusion.15.sel, bf16[4096,128]{1,0:T(8,128)(2,1)} %bitcast.133, bf16[4096,2048]{1,0:T(8,128)(2,1)} %bitcast.140), custom_call_target="tpu_custom_call" | custom-call | tf_op jit(solution)/shard_map/pick_rows/pallas_call | solution.py:859
  356.5 81.6 %expert_backward.1 = (f32[128,2048]{1,0:T(8,128)}, f32[2,768,128]{2,1,0:T(8,128)}, bf16[2,768,1024]{2,1,0:T(8,128)(2,1)}, bf16[2,768,1024]{2,1,0:T(8,128)(2,1)},...) custom-call(bf16[8,128]{1,0:T(8,128)(2,1)} %fusion.13.sel, bf16[32,128,128]{2,1,0:T(8,128)(2,1)} %slice.88.info, ...), custom_call_target="tpu_custom_call" | custom-call | tf_op jit(solution)/shard_map/expert_backward/pallas_call | solution.py:1088
  440.9 71.5 %expert_finish.1 = (f32[128,2176]{1,0:T(8,128)}, bf16[2,2048,2048]{2,1,0:T(8,128)(2,1)}) custom-call(bf16[8,128]{1,0:T(8,128)(2,1)} %fusion.13.sel, bf16[32,128,128]{2,1,0:T(8,128)(2,1)} %slice.88.info, bf16[2,2,2,4,48,2048]{5,4,3,2,1,0:T(8,128)(2,1)} %bitcast.145, bf16[2,2,2,4,48,128]{5,4,3,2,1,0:T(8,128)(2,1)} %select_select_fusion.more, ...), custom_call_target="tpu_custom_call" | custom-call | tf_op jit(solution)/shard_map/expert_finish/pallas_call | solution.py:1136
  525.4 17.0 %gather_rows.1 = bf16[4,128,2048]{2,1,0:T(8,128)(2,1)} custom-call(bf16[128,2048]{1,0:T(8,128)(2,1)} %fusion.25.n), custom_call_target="tpu_custom_call" | custom-call | tf_op jit(solution)/shard_map/gather_rows/pallas_call | solution.py:256
  542.5 4.3 convolution_convert_fusion.2
  548.9 10.2 %go_over_x.1 = bf16[4,4,128,128]{3,2,1,0:T(8,128)(2,1)} custom-call(bf16[4,4,128,128]{3,2,1,0:T(8,128)(2,1)} %bitcast.149), custom_call_target="tpu_custom_call" | custom-call | tf_op jit(solution)/shard_map/go_over_x/pallas_call | solution.py:408
  563.3 18.3 %attend_back.1 = (bf16[2048,128]{1,0:T(8,128)(2,1)S(1)}, bf16[4096,128]{1,0:T(8,128)(2,1)S(1)}, bf16[4096,128]{1,0:T(8,128)(2,1)S(1)}) custom-call(s32[2,8]{1,0:T(2,128)S(1)} %pad_add_fusion.lim, bf16[2048,128]{1,0:T(8,128)(2,1)S(1)} %bitcast.119, bf16[4096,128]{1,0:T(8,128)(2,1)S(1)} %bitcast.114, bf16[4096,128]{1,0:T(8,128)(2,1)S(1)} %bitcast.116, ...), custom_call_target="tpu_custom_call" | custom-call | tf_op jit(solution)/shard_map/attend_back/pallas_call | solution.py:626
  581.6 27.8 %grads_over_x.1 = bf16[3,4,4,128,128]{4,3,2,1,0:T(8,128)(2,1)S(1)} custom-call(bf16[4,4,128,128]{3,2,1,0:T(8,128)(2,1)S(1)} %bitcast.123, bf16[4,2,4,128,128]{4,3,2,1,0:T(8,128)(2,1)S(1)} %bitcast.120, bf16[4,2,4,128,128]{4,3,2,1,0:T(8,128)(2,1)S(1)} %bitcast.121), custom_call_target="tpu_custom_call" | custom-call | tf_op jit(solution)/shard_map/grads_over_x/pallas_call | solution.py:453
  611.4 2.6 convolution_convert_fusion
  614.1 107.3 %last_sums.1 = (f32[4,64,512]{2,1,0:T(8,128)}, f32[128,2048]{1,0:T(8,128)}, f32[4,2,4,40,128]{4,3,2,1,0:T(8,128)}) custom-call(bf16[3,4,512,128]{3,2,1,0:T(8,128)(2,1)} %bitcast.109, f32[2,4,512,128]{3,2,1,0:T(8,128)} %get-tuple-element.73.kept, bf16[3,2048,512]{2,1,0:T(8,128)(2,1)} %bitcast.135, bf16[512,2048]{1,0:T(8,128)(2,1)} %bitcast.144, ...), custom_call_target="tpu_custom_call" | custom-call | tf_op jit(solution)/shard_map/last_sums/pallas_call | solution.py:1409
  734.3 5.7 unstack.3
  740.0 7.2 unstack.2
  (167 shorter events, 61.7 us)
Async XLA Ops:
  7.2 277.7 %all-gather.5.cloned.1.call-start = ((), (), s32[]{:S(2)}) async-start(), calls=%async_computation.3 | async-start | bytes 10485760 | tf_op jit(solution)/shard_map/all_gather | solution.py:1480
  10.8 274.1 %all-gather.3.cloned.1.call-start = ((), (), s32[]{:S(2)}) async-start(), calls=%async_computation.2 | async-start | bytes 20971520 | tf_op jit(solution)/shard_map/all_gather | solution.py:1479
  16.9 3.0 copy-start.32
  16.9 3.0 copy-start.33
  16.9 3.0 copy-start.34
  16.9 3.7 copy-start.16
  17.0 3.9 copy-start.30
  17.0 717.3 %reduce-scatter.5.cloned.1.call-start = ((), (), s32[]{:S(2)}) async-start(), calls=%async_computation.5 | async-start | bytes 10485760 | tf_op jit(solution)/shard_map/reduce_scatter | solution.py:1573
  19.9 76.2 %copy-start.37 = (f32[128]{0:T(128)S(1)}, f32[128]{0:T(128)}, u32[]{:S(2)}) copy-start(f32[128]{0:T(128)} %param.26) | copy-start | bytes 1540
  19.9 76.2 %copy-start.38 = (f32[128]{0:T(128)S(1)}, f32[128]{0:T(128)}, u32[]{:S(2)}) copy-start(f32[128]{0:T(128)} %param.25) | copy-start | bytes 1540
  178.8 3.1 copy-start.27
  270.9 14.0 %copy-start.1 = (bf16[128,2048]{1,0:T(8,128)(2,1)S(1)}, bf16[128,2048]{1,0:T(8,128)(2,1)}, u32[]{:S(2)}) copy-start(bf16[128,2048]{1,0:T(8,128)(2,1)} %src.1) | copy-start | bytes 1572868
  438.1 301.8 %reduce-scatter.3.cloned.1.call-start = ((), (), s32[]{:S(2)}) async-start(), calls=%async_computation.4 | async-start | bytes 20971520 | tf_op jit(solution)/shard_map/reduce_scatter | solution.py:1573
  517.4 3.6 copy-start.25
  521.1 3.2 copy-start.14
  546.8 14.1 %copy-start.9 = (bf16[4,4,128,128]{3,2,1,0:T(8,128)(2,1)S(1)}, bf16[4,4,128,128]{3,2,1,0:T(8,128)(2,1)}, u32[]{:S(2)}) copy-start(bf16[4,4,128,128]{3,2,1,0:T(8,128)(2,1)} %get-tuple-element.50) | copy-start | bytes 1572868
  581.6 28.9 %copy-start.22 = (f32[4,2,4,32,128]{4,3,2,1,0:T(8,128)S(1)}, f32[4,2,4,32,128]{4,3,2,1,0:T(8,128)}, u32[]{:S(2)}) copy-start(f32[4,2,4,32,128]{4,3,2,1,0:T(8,128)} %concatenate.28) | copy-start | bytes 1572868
  581.6 29.8 %copy-start.21 = (bf16[4,128,2048]{2,1,0:T(8,128)(2,1)S(1)}, bf16[4,128,2048]{2,1,0:T(8,128)(2,1)}, u32[]{:S(2)}) copy-start(bf16[4,128,2048]{2,1,0:T(8,128)(2,1)} %gather_rows.1) | copy-start | bytes 6291460
  581.6 29.8 %copy-start.28 = (bf16[4,512,128]{1,2,0:T(8,128)(2,1)S(1)}, bf16[4,512,128]{1,2,0:T(8,128)(2,1)}, u32[]{:S(2)}) copy-start(bf16[4,512,128]{1,2,0:T(8,128)(2,1)} %copy-done.27) | copy-start | bytes 1572868
  721.4 4.8 copy-start.17
  723.7 8.8 %copy-start.15 = (f32[128,2048]{1,0:T(8,128)S(1)}, f32[128,2048]{1,0:T(8,128)}, u32[]{:S(2)}) copy-start(f32[128,2048]{1,0:T(8,128)} %copy-done.13) | copy-start | bytes 3145732
  723.7 8.8 %copy-start.19 = (f32[128,2048]{1,0:T(8,128)S(1)}, f32[128,2048]{1,0:T(8,128)}, u32[]{:S(2)}) copy-start(f32[128,2048]{1,0:T(8,128)} %copy-done.18) | copy-start | bytes 3145732
  726.2 6.3 copy-start.20
  726.2 6.3 copy-start.23
  (19 other events, 22.5 us)
Sparse Core Ops, SparseCore 0:
  10.9 94.8 all-gather.4
  108.1 152.5 all-gather.2
  438.3 77.1 reduce-scatter.4
  517.8 147.6 reduce-scatter.2

commit v5 on v4

--- a/solution.py
+++ b/solution.py
@@ -910,8 +910,7 @@
     for copy in first:
         copy.wait_recv()
 
-    def place(i, carry):
-        h, pair = i // 4, lax.rem(i, 4)
+    def place(h, pair):
         block = h * 16 + co * 8 + pair * 2
         both = jnp.concatenate([info[block], info[block + 1]], axis=0)
         table = lax.dot_general(
@@ -927,16 +926,29 @@
             at = lax.rem(pair, 2) * 2
             whole_q[h, pair // 2, at, :, lanes] = total[:128]
             whole_q[h, pair // 2, at + 1, :, lanes] = total[128:]
+
+    def far_y(k, carry):
+        place(oh, ol * 2 + k)
         return carry
 
-    lax.fori_loop(0, 8, place, 0)
+    def nearer(half):
+        def one(k, carry):
+            y = lax.rem(yh * 2 + yl + k + k // 2, 4)
+            place(y // 2, lax.rem(y, 2) * 2 + half)
+            return carry
+
+        lax.fori_loop(0, 3, one, 0)
+
     A, B = pl.ds(0, 64), pl.ds(64, 64)
+    lax.fori_loop(0, 2, far_y, 0)
     s1 = [
         wire.send(q.at[oh, ol, 0:2, A], a1.at[0], p.YR),
-        wire.send(q.at[0, :, p.xo, B], b1.at[0], p.XR),
         wire.send(q.at[oh, ol, 2:4, A], a1.at[1], p.YL),
-        wire.send(q.at[1, :, p.xo, B], b1.at[1], p.XL),
     ]
+    nearer(p.xo // 2)
+    s1.insert(1, wire.send(q.at[0, :, p.xo, B], b1.at[0], p.XR))
+    s1.append(wire.send(q.at[1, :, p.xo, B], b1.at[1], p.XL))
+    nearer(1 - p.xo // 2)
     yield
 
     def add(dst, *srcs):
@@ -1025,7 +1037,7 @@
         return pl.program_id(0) * PARTS + pl.program_id(1)
 
     def first(y, cot, hidden, row_gates, term):
-        at_step(number(), (1, moving), (6, moving))
+        at_step(number(), (3, moving))
         e = pl.program_id(0)
         product = y[0].astype(f32) * cot[0].astype(f32)
         partial = product[:, :128]
@@ -1046,7 +1058,7 @@
     )(y, cot, hidden, row_gates, term)
 
     def second(cot, w, row_gates, gate, up, dgate, dup):
-        at_step(number(), (5, moving))
+        at_step(number(), (3, moving))
         dhidden = jnp.dot(cot[0], w[0], preferred_element_type=f32) * row_gates[0, :, :1]
         g, u = gate[0].astype(f32), up[0].astype(f32)
         sg = jax.nn.sigmoid(g)
@@ -1068,7 +1080,7 @@
     )(cot, w_out, row_gates, gate, up, dgate, dup)
 
     def third(dgate, dup, w, drows):
-        at_step(number(), (4, moving))
+        at_step(number(), (5, moving), (7, moving))
         total = nt(dgate[0], w[0, :, :FF]) + nt(dup[0], w[0, :, FF:])
         drows[0] = total.astype(bf16)
 
@@ -1116,7 +1128,7 @@
 
     def first(rows, dgate, dup, term):
         at_step(
-            pl.program_id(0) * PARTS + pl.program_id(1), (1, moving), (4, moving), (7, moving)
+            pl.program_id(0) * PARTS + pl.program_id(1), (2, moving), (7, moving)
         )
         term[0, :, :FF] = tn(rows[0], dgate[0]).astype(bf16)
         term[0, :, FF:] = tn(rows[0], dup[0]).astype(bf16)
@@ -1186,9 +1198,10 @@
 
 
 def last_kernel(
-    grads, kept, w, rows, cosine, sine, gain, p3, unit, small, out, normed, whole, ss, rs, ls,
+    grads, kept, w, rows, cosine, sine, gain, p3, unit, small, out, normed, whole, tiny, ss, rs, ls,
     flat, total, w_grads, part, got_c, got_h, half, mine,
     ra, rb, rc, rd, re, rf, rg, acc_x, acc_y, sz, az, sx, ax, sy, ay, sc, ac, sh,
+    tz, tx, ty, tc, th,
 ):
     p = Place()
     dp, yl, x = p.dp, p.yl, p.x
@@ -1213,8 +1226,10 @@
         return wire.send(part.at[:, 1 - yl], rb.at[i - 2], p.Y)
 
     firsts = {3: y_first(3, p3)}
-    for d in range(4):
-        mine[d] = small[d]
+    far_z = ((p.zo, p.ZO), (p.zr, p.ZR), (p.zl, p.ZL))
+    far_x = ((p.xo, p.XO), (p.xr, p.XR), (p.xl, p.XL))
+    zs_out = [wire.send(small.at[there], sz.at[i], dev) for i, (there, dev) in enumerate(far_z)]
+    mine[...] = jnp.zeros_like(mine)
     starts = []
     for i in range(3):
         if i < 2:
@@ -1226,7 +1241,7 @@
                 gained += jnp.sum(grad * head * inverse, axis=0, keepdims=True)
                 back = rms_back(head, inverse, grad * gain[i])
                 flat[:, h * HD : (h + 1) * HD] = back.astype(bf16)
-            mine[0, 1, 0, 32 + i : 33 + i] = gained
+            mine[0, 16 + i : 17 + i] = gained
         else:
             for h in range(4):
                 flat[:, h * HD : (h + 1) * HD] = grads[i, h]
@@ -1261,6 +1276,23 @@
             return carry
 
         lax.fori_loop(0, 4, normed_cols, 0)
+        if i == 0:
+            for copy in zs_out:
+                copy.wait_recv()
+            for y in range(2):
+                az[y] = small[dp, y] + sz[0, y] + sz[1, y] + sz[2, y]
+            xs_out = [
+                wire.send(az.at[:, there], sx.at[n], dev) for n, (there, dev) in enumerate(far_x)
+            ]
+        elif i == 1:
+            for copy in xs_out:
+                copy.wait_recv()
+            ax[...] = az[:, x] + sx[0] + sx[1] + sx[2]
+            y_out = wire.send(ax.at[1 - yl], sy, p.Y)
+        else:
+            y_out.wait_recv()
+            ay[...] = ax[yl] + sy[...]
+            c_out = wire.send(ay, sc, p.C)
     mine_head, other = p.yh * 2 + (1 - p.co), (1 - p.yh) * 2 + (1 - p.co)
     far = wire.send(part.at[other], got_c.at[0], p.C)
     near = wire.send(part.at[mine_head], got_c.at[1], p.C)
@@ -1279,6 +1311,9 @@
 
     by_16(add_far)
     over = wire.send(half, got_h, p.H)
+    c_out.wait_recv()
+    ac[...] = ay[...] + sc[...]
+    h_out = wire.send(ac, sh, p.H)
     seconds = []
     for i, gradient in ((0, p0), (1, p1)):
         one, two = starts[i]
@@ -1312,11 +1347,12 @@
     for c in range(16):
         cols = slice(c * 128, (c + 1) * 128)
         column = jnp.sum(normed[:, cols] * unit[:, cols], axis=0, keepdims=True)
-        mine[0, 0, c // 8, 32 + c % 8 : 33 + c % 8] = column
-    zs_out = [
-        wire.send(mine.at[there], sz.at[i], device)
-        for i, (there, device) in enumerate(((p.zo, p.ZO), (p.zr, p.ZR), (p.zl, p.ZL)))
-    ]
+        mine[0, c : c + 1] = column
+    h_out.wait_recv()
+    whole[dp, yl, x] = ac[...] + sh[...]
+    y_all = wire.send(whole.at[dp, yl, x], whole.at[dp, yl, x], p.Y)
+    tz_out = [wire.send(mine.at[0], tz.at[dp], dev) for _, dev in far_z]
+    tz[dp] = mine[0]
     yends = []
     for i, gradient in ((0, p0), (1, p1)):
         for s in seconds[i]:
@@ -1324,14 +1360,13 @@
         acc = acc_x.at[i]
         loop(4, lambda d: added(acc.at[d], gradient.at[d, :, x], rc.at[i, 0, d], rc.at[i, 1, d]))
         yends.append(wire.send(acc.at[:, 1 - yl], re.at[i], p.Y))
-    for copy in zs_out:
+    y_all.wait_recv()
+    x_all = [wire.send(whole.at[dp, :, x], whole.at[dp, :, x], dev) for _, dev in far_x]
+    for copy in tz_out:
         copy.wait_recv()
-    for y in range(2):
-        az[y] = mine[dp, y] + sz[0, y] + sz[1, y] + sz[2, y]
-    xs_out = [
-        wire.send(az.at[:, there], sx.at[i], device)
-        for i, (there, device) in enumerate(((p.xo, p.XO), (p.xr, p.XR), (p.xl, p.XL)))
-    ]
+    mine[1] = tz[0] + tz[1] + tz[2] + tz[3]
+    tx_out = [wire.send(mine.at[1], tx.at[x], dev) for _, dev in far_x]
+    tx[x] = mine[1]
     xends = {}
     for i in (3, 2):
         acc = acc_y.at[i - 2]
@@ -1343,10 +1378,13 @@
         loop(2, lambda d: added(acc.at[d + 2, p.xl], acc.at[d + 2, p.xl], rd.at[i - 2, 1, d]))
         s2 = wire.send(acc.at[:, p.xl], rf.at[i - 2, 1], p.XL)
         xends[i] = (s1, s2)
-    for copy in xs_out:
+    for copy in x_all:
         copy.wait_recv()
-    ax[...] = az[:, x] + sx[0] + sx[1] + sx[2]
-    y_out = wire.send(ax.at[1 - yl], sy, p.Y)
+    z_all = [wire.send(whole.at[dp], whole.at[dp], dev) for _, dev in far_z]
+    for copy in tx_out:
+        copy.wait_recv()
+    mine[2] = tx[0] + tx[1] + tx[2] + tx[3]
+    ty_out = wire.send(mine.at[2], ty, p.Y)
     parts, zs = {}, {}
 
     def z_first(i, acc):
@@ -1361,9 +1399,9 @@
         acc = acc_x.at[i]
         loop(4, lambda d: added(acc.at[d, yl], acc.at[d, yl], re.at[i, d]))
         z_first(i, acc.at[:, yl])
-    y_out.wait_recv()
-    ay[...] = ax[yl] + sy[...]
-    c_out = wire.send(ay, sc, p.C)
+    ty_out.wait_recv()
+    mine[3] = mine[2] + ty[...]
+    tc_out = wire.send(mine.at[3], tc, p.C)
     for i in (3, 2):
         for s in xends[i]:
             s.wait_recv()
@@ -1372,9 +1410,9 @@
             4, lambda d: added(acc.at[d, x], acc.at[d, x], rf.at[i - 2, 0, d], rf.at[i - 2, 1, d])
         )
         z_first(i, acc.at[:, x])
-    c_out.wait_recv()
-    ac[...] = ay[...] + sc[...]
-    h_out = wire.send(ac, sh, p.H)
+    tc_out.wait_recv()
+    mine[4] = mine[3] + tc[...]
+    th_out = wire.send(mine.at[4], th, p.H)
     ends = {}
     for i in (0, 1, 3, 2):
         one, two = zs[i]
@@ -1386,20 +1424,12 @@
         added(acc.at[p.zl, 32:64], acc.at[p.zl, 32:64], rg.at[i, 1, 0:32])
         s2 = wire.send(acc.at[p.zl], rg.at[i, 3], p.ZL)
         ends[i] = (s1, s2)
-    h_out.wait_recv()
-    whole[dp, yl, x] = ac[...] + sh[...]
-    y_all = wire.send(whole.at[dp, yl, x], whole.at[dp, yl, x], p.Y)
-    y_all.wait_recv()
-    x_all = [
-        wire.send(whole.at[dp, :, x], whole.at[dp, :, x], device) for device in (p.XO, p.XR, p.XL)
-    ]
+    th_out.wait_recv()
+    tiny[...] = mine[4] + th[...]
     for i in range(4):
         for s in ends[i]:
             s.wait_recv()
         added(out.at[i], parts[i].at[dp], rg.at[i, 2], rg.at[i, 3])
-    for copy in x_all:
-        copy.wait_recv()
-    z_all = [wire.send(whole.at[dp], whole.at[dp], device) for device in (p.ZO, p.ZR, p.ZL)]
     for copy in z_all:
         copy.wait_recv()
     wire.drain()
@@ -1410,14 +1440,15 @@
         last_kernel,
         "last_sums",
         8,
-        55,
+        64,
         1,
         [VMEM] * 10,
-        [VMEM] * 3,
+        [VMEM] * 4,
         (
             shaped((4, 64, 512), f32),
             shaped((128, 2048), f32),
             shaped((4, 2, 4, 40, 128), f32),
+            shaped((24, 128), f32),
         ),
         scratch=[
             pltpu.VMEM((512, 512), bf16),
@@ -1427,7 +1458,7 @@
             pltpu.VMEM((2, 128, 2048), bf16),
             pltpu.VMEM((128, 2048), bf16),
             pltpu.VMEM((128, 2048), bf16),
-            pltpu.VMEM((4, 2, 4, 40, 128), f32),
+            pltpu.VMEM((5, 24, 128), f32),
             pltpu.VMEM((2, 2, 2, 2, 64, 512), bf16),
             pltpu.VMEM((2, 4, 4, 64, 512), bf16),
             pltpu.VMEM((2, 2, 4, 2, 64, 512), bf16),
@@ -1446,6 +1477,11 @@
             pltpu.VMEM((40, 128), f32),
             pltpu.VMEM((40, 128), f32),
             pltpu.VMEM((40, 128), f32),
+            pltpu.VMEM((4, 24, 128), f32),
+            pltpu.VMEM((4, 24, 128), f32),
+            pltpu.VMEM((24, 128), f32),
+            pltpu.VMEM((24, 128), f32),
+            pltpu.VMEM((24, 128), f32),
         ],
         vmem=60 << 20,
     )(
@@ -1606,27 +1642,27 @@
     out_grad = jnp.einsum(
         "qc,qf->cf", branch_all, attended_flat, preferred_element_type=f32
     ).astype(bf16)
-    gains = jnp.pad(ffn_gain_term, (width, 32 * 8 * 128 - 2 * width)).reshape(32, 8, 128)
+    gains = jnp.pad(ffn_gain_term, (0, 32 * 8 * 128 - width)).reshape(32, 8, 128)
     small = jnp.concatenate([router_term.reshape(32, 32, 128), gains], axis=1)
-    attn_grads, grad_normed, summed = last_sums(
+    attn_grads, grad_normed, summed, tiny = last_sums(
         grad_heads.reshape(3, 4, 512, HD), projected, full_three, normed_all, cosine, sine,
         head_gains, out_grad, inputs * first_inv, small,
     )
     input_grad = grad_middle + rms_back(inputs, first_inv, grad_normed * attn_gain)
     summed = summed.reshape(32, 40, 128)
     router_grad = summed[:, :32].reshape(router.shape)
-    gains = summed[:, 32:].reshape(-1)
+    ffn_gain_grad = summed[:, 32:].reshape(-1)[:width]
     return (
         output,
         input_grad,
-        gains[:2048],
+        tiny[:16].reshape(-1),
         attn_grads[0],
         attn_grads[1],
         attn_grads[2],
         attn_grads[3],
-        gains[4096:4224],
-        gains[4224:4352],
-        gains[2048:4096],
+        tiny[16],
+        tiny[17],
+        ffn_gain_grad,
         router_grad,
         expert_in_grad,
         expert_out_grad,

time: 765 us -> 731 us (0.956)
  Pallas kernels: 658 us -> 629 us
    pallas_call x1, Pallas kernels: 107 us -> 92.6 us  [last_sums(): remote_call(last_kernel, 'last_sums', 8, 64, 1, [VMEM] * 10, [VMEM] * 4,...]
    pallas_call x1, Pallas kernels: 81.6 us -> 72.2 us  [expert_backward(): remote_call(backward_kernel, 'expert_backward', cid, HOME_SENDS, 2, [VMEM...]
    unnamed x87 -> x89, local copies, waits for them, and re-layouts: 27.8 us -> 27.8 us
  transfers between devices with their start and end apart: 4 -> 4, of which waited for: 0 -> 0; matrix products, arithmetic and copies ran while one was open for 8% -> 9% of each run, Pallas kernels for 66% -> 66%
where the time goes in v5:
time: 731 us; the launch traced here: 725 us
  Pallas kernels  629 us (86%)
  local copies, waits for them, and re-layouts  48 us (7%)
  other arithmetic  19.6 us (3%)
  between operations  14.8 us (2%)
  matrix products  13.1 us (2%)
    pallas_call x1, Pallas kernels, last_sums(): remote_call(last_kernel, 'last_sums', 8, 64, 1, [VMEM] * 10, [VMEM] * 4,...  92.6 us
    pallas_call x1, Pallas kernels, gather_weights(): remote_call(weights_kernel, 'gather_weights', 1, 24, 3, [ANY] * 3, [ANY]...  73.8 us
    pallas_call x1, Pallas kernels, expert_backward(): remote_call(backward_kernel, 'expert_backward', cid, HOME_SENDS, 2, [VMEM...  72.2 us
    pallas_call x1, Pallas kernels, expert_finish(): remote_call(finish_kernel, 'expert_finish', cid, HOME_SENDS, 4, [VMEM, VM...  68.3 us
    pallas_call x1, Pallas kernels, spread(): remote_call(spread_kernel, 'spread', cid, SPREAD_SENDS, 1, [ANY], [ANY],...  66.3 us
    pallas_call x1, Pallas kernels, expert_forward(): remote_call(forward_kernel, 'expert_forward', cid, SPREAD_SENDS, 1, [ANY]...  56.8 us
    pallas_call x1, Pallas kernels, heads_over_x(): remote_call(heads_kernel, 'heads_over_x', 3, 22, 4, [ANY] * 2, [ANY] * 4,...  39.9 us
    unnamed x89, local copies, waits for them, and re-layouts  27.8 us
  transfers between devices with their start and end apart: 4, of which 0 were waited for; matrix products, arithmetic and copies ran while one was open for 9% of the time, Pallas kernels for 66%

profile of v5, /device:TPU:0, one launch (start us, length us, event | category | flops | bytes accessed | tf_op | source)
XLA Modules:
  0.0 724.7 jit_solution(15128446372113925341)
XLA Ops:
  7.2 3.5 copy.105
  10.8 6.1 copy.104
  22.2 73.8 %gather_weights.1 = (bf16[3,4,2,4,64,512]{5,4,3,2,1,0:T(8,128)(2,1)}, bf16[4,64,512]{2,1,0:T(8,128)(2,1)}, bf16[4,128,2048]{2,1,0:T(8,128)(2,1)}) custom-call(bf16[3,64,512]{2,1,0:T(8,128)(2,1)} %pad_maximum_fusion.3.w, bf16[64,512]{1,0:T(8,128)(2,1)} %wo.1, bf16[128,2048]{1,0:T(8,128)(2,1)} %get-tuple-element.152.n), custom_call_target="tpu_custom_call" | custom-call | tf_op jit(solution)/shard_map/gather_weights/pallas_call | solution.py:227
  98.8 10.1 %project.1 = (bf16[3,4,512,128]{3,2,1,0:T(8,128)(2,1)}, f32[2,4,512,128]{3,2,1,0:T(8,128)}) custom-call(bf16[512,2048]{1,0:T(8,128)(2,1)} %bitcast.145, bf16[3,2048,512]{2,1,0:T(8,128)(2,1)} %bitcast.136, f32[512,128]{1,0:T(8,128)} %get-tuple-element.171.cosine, f32[512,128]{1,0:T(8,128)} %get-tuple-element.172.sine, f32[2,1,128]{2,1,0:T(1,128)} %bitcast.167), custom_call_target="tpu_custom_call" | custom-call | tf_op jit(solution)/shard_map/project/pallas_call | solution.py:500
  108.8 39.9 %heads_over_x.1 = (bf16[4,4,128,128]{3,2,1,0:T(8,128)(2,1)}, bf16[4,2,4,128,128]{4,3,2,1,0:T(8,128)(2,1)}, bf16[4,2,4,128,128]{4,3,2,1,0:T(8,128)(2,1)}, bf16[4,2,4,64,512]{4,3,2,1,0:T(8,128)(2,1)}) custom-call(bf16[3,4,4,128,128]{4,3,2,1,0:T(8,128)(2,1)} %bitcast.153, bf16[4,64,512]{2,1,0:T(8,128)(2,1)} %get-tuple-element.50.go), custom_call_target="tpu_custom_call" | custom-call | tf_op jit(solution)/shard_map/heads_over_x/pallas_call | solution.py:358
  152.8 14.0 %attend.1 = (bf16[2048,128]{1,0:T(8,128)(2,1)S(1)}, f32[2048,128]{1,0:T(8,128)S(1)}, f32[2048,128]{1,0:T(8,128)S(1)}) custom-call(s32[2,8]{1,0:T(2,128)S(1)} %pad_add_fusion.lim, bf16[2048,128]{1,0:T(8,128)(2,1)S(1)} %bitcast.120, bf16[4096,128]{1,0:T(8,128)(2,1)S(1)} %bitcast.115, bf16[4096,128]{1,0:T(8,128)(2,1)S(1)} %bitcast.117, ...), custom_call_target="tpu_custom_call" | custom-call | tf_op jit(solution)/shard_map/attend/pallas_call | solution.py:565
  169.5 8.0 %back_over_x.1 = bf16[4,4,128,128]{3,2,1,0:T(8,128)(2,1)} custom-call(bf16[4,4,128,128]{3,2,1,0:T(8,128)(2,1)} %bitcast.124), custom_call_target="tpu_custom_call" | custom-call | tf_op jit(solution)/shard_map/back_over_x/pallas_call | solution.py:389
  178.8 3.1 convolution_convert_fusion.1
  181.9 15.6 %sum_rows.1 = f32[128,2048]{1,0:T(8,128)S(1)} custom-call(bf16[2,2,128,2048]{3,2,1,0:T(8,128)(2,1)S(1)} %bitcast.119), custom_call_target="tpu_custom_call" | custom-call | tf_op jit(solution)/shard_map/sum_rows/pallas_call | solution.py:295
  201.1 66.3 %spread.1 = bf16[2,2,2,4,128,2176]{5,4,3,2,1,0:T(8,128)(2,1)} custom-call(bf16[128,2176]{1,0:T(8,128)(2,1)} %concatenate.25.src), custom_call_target="tpu_custom_call" | custom-call | tf_op jit(solution)/shard_map/spread/pallas_call | solution.py:720
  270.4 13.4 %pick_rows.2 = (bf16[2,16,48,2048]{3,2,1,0:T(8,128)(2,1)}, f32[2,16,48,128]{3,2,1,0:T(8,128)}) custom-call(bf16[8,128]{1,0:T(8,128)(2,1)} %fusion.15.sel, bf16[4096,128]{1,0:T(8,128)(2,1)} %bitcast.134, bf16[4096,2176]{1,0:T(8,128)(2,1)} %bitcast.133), custom_call_target="tpu_custom_call" | custom-call | tf_op jit(solution)/shard_map/pick_rows/pallas_call | solution.py:859
  284.4 56.8 %expert_forward.1 = (bf16[2,2,2,4,128,2048]{5,4,3,2,1,0:T(8,128)(2,1)}, bf16[2,768,1024]{2,1,0:T(8,128)(2,1)S(1)}, bf16[2,768,1024]{2,1,0:T(8,128)(2,1)}, bf16[2...) custom-call(bf16[128,2048]{1,0:T(8,128)(2,1)S(1)} %copy-done.1, bf16[2,768,2048]{2,1,0:T(8,128)(2,1)} %bitcast.138, ...), custom_call_target="tpu_custom_call" | custom-call | tf_op jit(solution)/shard_map/expert_forward/pallas_call | solution.py:802
  342.9 13.1 %pick_rows.3 = bf16[2,16,48,2048]{3,2,1,0:T(8,128)(2,1)} custom-call(bf16[8,128]{1,0:T(8,128)(2,1)} %fusion.15.sel, bf16[4096,128]{1,0:T(8,128)(2,1)} %bitcast.135, bf16[4096,2048]{1,0:T(8,128)(2,1)} %bitcast.142), custom_call_target="tpu_custom_call" | custom-call | tf_op jit(solution)/shard_map/pick_rows/pallas_call | solution.py:859
  356.0 72.2 %expert_backward.1 = (f32[128,2048]{1,0:T(8,128)}, f32[2,768,128]{2,1,0:T(8,128)}, bf16[2,768,1024]{2,1,0:T(8,128)(2,1)}, bf16[2,768,1024]{2,1,0:T(8,128)(2,1)},...) custom-call(bf16[8,128]{1,0:T(8,128)(2,1)} %fusion.13.sel, bf16[32,128,128]{2,1,0:T(8,128)(2,1)} %slice.80.info, ...), custom_call_target="tpu_custom_call" | custom-call | tf_op jit(solution)/shard_map/expert_backward/pallas_call | solution.py:1100
  430.9 68.3 %expert_finish.1 = (f32[128,2176]{1,0:T(8,128)}, bf16[2,2048,2048]{2,1,0:T(8,128)(2,1)}) custom-call(bf16[8,128]{1,0:T(8,128)(2,1)} %fusion.13.sel, bf16[32,128,128]{2,1,0:T(8,128)(2,1)} %slice.80.info, bf16[2,2,2,4,48,2048]{5,4,3,2,1,0:T(8,128)(2,1)} %bitcast.147, bf16[2,2,2,4,48,128]{5,4,3,2,1,0:T(8,128)(2,1)} %select_select_fusion.more, ...), custom_call_target="tpu_custom_call" | custom-call | tf_op jit(solution)/shard_map/expert_finish/pallas_call | solution.py:1148
  512.4 17.0 %gather_rows.1 = bf16[4,128,2048]{2,1,0:T(8,128)(2,1)} custom-call(bf16[128,2048]{1,0:T(8,128)(2,1)} %fusion.25.n), custom_call_target="tpu_custom_call" | custom-call | tf_op jit(solution)/shard_map/gather_rows/pallas_call | solution.py:256
  529.5 4.4 convolution_convert_fusion.2
  535.9 9.4 %go_over_x.1 = bf16[4,4,128,128]{3,2,1,0:T(8,128)(2,1)} custom-call(bf16[4,4,128,128]{3,2,1,0:T(8,128)(2,1)} %bitcast.151), custom_call_target="tpu_custom_call" | custom-call | tf_op jit(solution)/shard_map/go_over_x/pallas_call | solution.py:408
  549.6 17.7 %attend_back.1 = (bf16[2048,128]{1,0:T(8,128)(2,1)S(1)}, bf16[4096,128]{1,0:T(8,128)(2,1)S(1)}, bf16[4096,128]{1,0:T(8,128)(2,1)S(1)}) custom-call(s32[2,8]{1,0:T(2,128)S(1)} %pad_add_fusion.lim, bf16[2048,128]{1,0:T(8,128)(2,1)S(1)} %bitcast.121, bf16[4096,128]{1,0:T(8,128)(2,1)S(1)} %bitcast.116, bf16[4096,128]{1,0:T(8,128)(2,1)S(1)} %bitcast.118, ...), custom_call_target="tpu_custom_call" | custom-call | tf_op jit(solution)/shard_map/attend_back/pallas_call | solution.py:626
  567.3 27.7 %grads_over_x.1 = bf16[3,4,4,128,128]{4,3,2,1,0:T(8,128)(2,1)S(1)} custom-call(bf16[4,4,128,128]{3,2,1,0:T(8,128)(2,1)S(1)} %bitcast.125, bf16[4,2,4,128,128]{4,3,2,1,0:T(8,128)(2,1)S(1)} %bitcast.122, bf16[4,2,4,128,128]{4,3,2,1,0:T(8,128)(2,1)S(1)} %bitcast.123), custom_call_target="tpu_custom_call" | custom-call | tf_op jit(solution)/shard_map/grads_over_x/pallas_call | solution.py:453
  597.1 2.6 convolution_convert_fusion
  599.7 92.6 %last_sums.1 = (f32[4,64,512]{2,1,0:T(8,128)}, f32[128,2048]{1,0:T(8,128)}, f32[4,2,4,40,128]{4,3,2,1,0:T(8,128)}, f32[24,128]{1,0:T(8,128)}) custom-call(bf16[3,4,512,128]{3,2,1,0:T(8,128)(2,1)} %bitcast.111, f32[2,4,512,128]{3,2,1,0:T(8,128)} %get-tuple-element.74.kept, bf16[3,2048,512]{2,1,0:T(8,128)(2,1)} %bitcast.137, bf16[512,2048]{1,0:T(8,128)(2,1)} %bitcast.146, ...), custom_call_target="tpu_custom_call" | custom-call | tf_op jit(solution)/shard_map/last_sums/pallas_call | solution.py:1439
  704.9 5.7 unstack.3
  710.6 7.2 %unstack.2 = f32[512,2,2048]{2,1,0:T(2,128)} custom-call(bf16[2,512,2048]{2,1,0:T(8,128)(2,1)} %reduce-scatter.3.cloned.1.call-done.grads), custom_call_target="tpu_custom_call" | custom-call | tf_op jit(solution)/shard_map/unstack/pallas_call | solution.py:1188
  (169 shorter events, 61.3 us)
Async XLA Ops:
  7.2 277.2 %all-gather.5.cloned.1.call-start = ((), (), s32[]{:S(2)}) async-start(), calls=%async_computation.3 | async-start | bytes 10485760 | tf_op jit(solution)/shard_map/all_gather | solution.py:1516
  10.8 273.6 %all-gather.3.cloned.1.call-start = ((), (), s32[]{:S(2)}) async-start(), calls=%async_computation.2 | async-start | bytes 20971520 | tf_op jit(solution)/shard_map/all_gather | solution.py:1515
  16.9 3.0 copy-start.32
  16.9 3.0 copy-start.33
  16.9 3.7 copy-start.16
  17.0 3.9 copy-start.30
  17.0 687.9 %reduce-scatter.5.cloned.1.call-start = ((), (), s32[]{:S(2)}) async-start(), calls=%async_computation.5 | async-start | bytes 10485760 | tf_op jit(solution)/shard_map/reduce_scatter | solution.py:1609
  19.9 76.2 %copy-start.38 = (f32[128]{0:T(128)S(1)}, f32[128]{0:T(128)}, u32[]{:S(2)}) copy-start(f32[128]{0:T(128)} %param.26) | copy-start | bytes 1540
  19.9 76.2 %copy-start.39 = (f32[128]{0:T(128)S(1)}, f32[128]{0:T(128)}, u32[]{:S(2)}) copy-start(f32[128]{0:T(128)} %param.25) | copy-start | bytes 1540
  178.7 3.1 copy-start.27
  270.4 14.0 %copy-start.1 = (bf16[128,2048]{1,0:T(8,128)(2,1)S(1)}, bf16[128,2048]{1,0:T(8,128)(2,1)}, u32[]{:S(2)}) copy-start(bf16[128,2048]{1,0:T(8,128)(2,1)} %src.1) | copy-start | bytes 1572868
  428.2 282.4 %reduce-scatter.3.cloned.1.call-start = ((), (), s32[]{:S(2)}) async-start(), calls=%async_computation.4 | async-start | bytes 20971520 | tf_op jit(solution)/shard_map/reduce_scatter | solution.py:1609
  504.4 3.6 copy-start.25
  508.0 3.2 copy-start.14
  533.8 13.4 %copy-start.9 = (bf16[4,4,128,128]{3,2,1,0:T(8,128)(2,1)S(1)}, bf16[4,4,128,128]{3,2,1,0:T(8,128)(2,1)}, u32[]{:S(2)}) copy-start(bf16[4,4,128,128]{3,2,1,0:T(8,128)(2,1)} %get-tuple-element.51) | copy-start | bytes 1572868
  567.3 28.9 %copy-start.22 = (f32[4,2,4,32,128]{4,3,2,1,0:T(8,128)S(1)}, f32[4,2,4,32,128]{4,3,2,1,0:T(8,128)}, u32[]{:S(2)}) copy-start(f32[4,2,4,32,128]{4,3,2,1,0:T(8,128)} %concatenate.28) | copy-start | bytes 1572868
  567.3 29.8 %copy-start.21 = (bf16[4,128,2048]{2,1,0:T(8,128)(2,1)S(1)}, bf16[4,128,2048]{2,1,0:T(8,128)(2,1)}, u32[]{:S(2)}) copy-start(bf16[4,128,2048]{2,1,0:T(8,128)(2,1)} %gather_rows.1) | copy-start | bytes 6291460
  567.3 29.8 %copy-start.28 = (bf16[4,512,128]{1,2,0:T(8,128)(2,1)S(1)}, bf16[4,512,128]{1,2,0:T(8,128)(2,1)}, u32[]{:S(2)}) copy-start(bf16[4,512,128]{1,2,0:T(8,128)(2,1)} %copy-done.27) | copy-start | bytes 1572868
  692.3 4.8 copy-start.17
  693.5 5.3 copy-start.36
  694.7 8.4 %copy-start.15 = (f32[128,2048]{1,0:T(8,128)S(1)}, f32[128,2048]{1,0:T(8,128)}, u32[]{:S(2)}) copy-start(f32[128,2048]{1,0:T(8,128)} %copy-done.13) | copy-start | bytes 3145732
  694.7 8.4 %copy-start.19 = (f32[128,2048]{1,0:T(8,128)S(1)}, f32[128,2048]{1,0:T(8,128)}, u32[]{:S(2)}) copy-start(f32[128,2048]{1,0:T(8,128)} %copy-done.18) | copy-start | bytes 3145732
  697.2 5.9 copy-start.20
  697.2 5.9 copy-start.23
  (20 other events, 25.5 us)
Sparse Core Ops, SparseCore 0:
  10.9 94.8 all-gather.4
  108.1 152.5 all-gather.2
  428.3 77.6 reduce-scatter.4
  508.3 154.7 reduce-scatter.2

commit v6 on v5

--- a/solution.py
+++ b/solution.py
@@ -236,80 +236,6 @@
     )(w, wo, n)
 
 
-def rows_kernel(n, m, ss, rs, ls):
-    p = Place()
-    own = local(n, m.at[p.head], ls, 0)
-    greet([p.C, p.H])
-    wire = Wire(ss, rs)
-    n_h = wire.send(n, m.at[p.head], p.H)
-    n_c = wire.send(n, m.at[p.head], p.C)
-    n_h.wait_recv()
-    other = (1 - p.yh) * 2 + p.co
-    n_f = wire.send(m.at[other], m.at[other], p.C)
-    n_c.wait_recv()
-    n_f.wait_recv()
-    own.wait()
-    wire.drain()
-
-
-def gather_rows(n):
-    return remote_call(
-        rows_kernel, "gather_rows", 2, 3, 1, [ANY], [ANY], (shaped((4, 128, 2048)),)
-    )(n)[0]
-
-
-def sum_kernel(part, out, ss, rs, ls, got_c, got_h, half):
-    p = Place()
-    greet([p.C, p.H])
-    wire = Wire(ss, rs)
-    far = wire.send(part.at[1 - p.yh, 1 - p.co], got_c.at[0], p.C)
-    near = wire.send(part.at[p.yh, 1 - p.co], got_c.at[1], p.C)
-    far.wait_recv()
-
-    def add_far(i, carry):
-        rows = pl.ds(pl.multiple_of(i * 16, 16), 16)
-        half[rows] = (
-            part[1 - p.yh, p.co, rows].astype(f32) + got_c[0, rows].astype(f32)
-        ).astype(bf16)
-        return carry
-
-    lax.fori_loop(0, 8, add_far, 0)
-    over = wire.send(half, got_h, p.H)
-    near.wait_recv()
-    over.wait_recv()
-
-    def add_near(i, carry):
-        rows = pl.ds(pl.multiple_of(i * 16, 16), 16)
-        out[rows] = (
-            part[p.yh, p.co, rows].astype(f32)
-            + got_c[1, rows].astype(f32)
-            + got_h[rows].astype(f32)
-        )
-        return carry
-
-    lax.fori_loop(0, 8, add_near, 0)
-    wire.drain()
-
-
-def sum_rows(part, cid):
-    return remote_call(
-        sum_kernel,
-        "sum_rows",
-        cid,
-        3,
-        1,
-        [VMEM],
-        [VMEM],
-        (shaped((128, 2048), f32),),
-        scratch=[
-            pltpu.VMEM((2, 128, 2048), bf16),
-            pltpu.VMEM((128, 2048), bf16),
-            pltpu.VMEM((128, 2048), bf16),
-        ],
-        vmem=16 << 20,
-    )(part.reshape(2, 2, 128, 2048))[0]
-
-
 def heads_kernel(three, go, qd, kd, vd, gd, ss, rs, ls):
     p = Place()
     q, k, v = (three.at[i] for i in range(3))
@@ -372,42 +298,131 @@
     )(three, go)
 
 
-def back_x_kernel(o, att, ss, rs, ls):
+def attended_kernel(o, w, att, out, ss, rs, ls, flat, part, got_c, got_h, half):
     p = Place()
-    own = local(o.at[:, p.x], att.at[p.x], ls, 0)
-    greet([p.XR, p.XL, p.XO])
+    greet([p.C, p.H, p.XR, p.XL, p.XO])
     wire = Wire(ss, rs)
-    for there, device in ((p.xo, p.XO), (p.xr, p.XR), (p.xl, p.XL)):
-        wire.send(o.at[:, there], att.at[p.x], device)
-    for copy in wire.started:
+    near_c, far_c = p.yh * 2 + (1 - p.co), (1 - p.yh) * 2 + (1 - p.co)
+    far = (1 - p.yh) * 2 + p.co
+    order = (far_c, near_c, far, p.head)
+    came = []
+    for run in order:
+        came.append(
+            [
+                wire.send(o.at[run, there], att.at[p.x, run], device)
+                for there, device in ((p.xo, p.XO), (p.xr, p.XR), (p.xl, p.XL))
+            ]
+        )
+        att[p.x, run] = o[run, p.x]
+
+    def times(i, store):
+        for copy in came[i]:
+            copy.wait_recv()
+        for h in range(4):
+            flat[:, h * HD : (h + 1) * HD] = att[h, order[i]]
+        for c in range(0, 2048, 512):
+            cols = slice(c, c + 512)
+            store(cols, nt(flat[...], w[cols]))
+
+    sums = []
+    for i in range(2):
+
+        def keep(cols, value):
+            part[i, :, cols] = value.astype(bf16)
+
+        times(i, keep)
+        sums.append(wire.send(part.at[i], got_c.at[i], p.C))
+    sums[0].wait_recv()
+
+    def add_far(cols, value):
+        half[:, cols] = (value + got_c[0, :, cols].astype(f32)).astype(bf16)
+
+    times(2, add_far)
+    over = wire.send(half, got_h, p.H)
+
+    def first(cols, value):
+        out[:, cols] = value
+
+    times(3, first)
+    sums[1].wait_recv()
+    over.wait_recv()
+
+    def add(i, carry):
+        at = pl.ds(pl.multiple_of(i * 16, 16), 16)
+        out[at] += got_c[1, at].astype(f32) + got_h[at].astype(f32)
+        return carry
+
+    lax.fori_loop(0, 8, add, 0)
+    wire.drain()
+
+
+def attended_home(o, w):
+    return remote_call(
+        attended_kernel,
+        "attended_home",
+        4,
+        15,
+        1,
+        [VMEM, VMEM],
+        [VMEM, VMEM],
+        (shaped((4, 4, 128, 128)), shaped((128, 2048), f32)),
+        scratch=[
+            pltpu.VMEM((128, 512), bf16),
+            pltpu.VMEM((2, 128, 2048), bf16),
+            pltpu.VMEM((2, 128, 2048), bf16),
+            pltpu.VMEM((128, 2048), bf16),
+            pltpu.VMEM((128, 2048), bf16),
+        ],
+        vmem=32 << 20,
+    )(o, w)
+
+
+def branch_kernel(n, w, m, d, ss, rs, ls, heads):
+    p = Place()
+    own = local(n, m.at[p.head], ls, 0)
+    greet([p.C, p.H, p.XR, p.XL, p.XO])
+    wire = Wire(ss, rs)
+    n_h = wire.send(n, m.at[p.head], p.H)
+    n_c = wire.send(n, m.at[p.head], p.C)
+    sibling = p.yh * 2 + (1 - p.co)
+    other, last = (1 - p.yh) * 2 + p.co, (1 - p.yh) * 2 + (1 - p.co)
+    moved = []
+
+    def out(run, at):
+        value = jnp.dot(m[run], w[...], preferred_element_type=f32).astype(bf16)
+        for h in range(4):
+            heads[at, h] = value[:, h * HD : (h + 1) * HD]
+        for there, device in ((p.xo, p.XO), (p.xr, p.XR), (p.xl, p.XL)):
+            moved.append(wire.send(heads.at[at, there], d.at[run, p.x], device))
+        d[run, p.x] = heads[at, p.x]
+
+    own.wait()
+    out(p.head, 0)
+    n_c.wait_recv()
+    out(sibling, 1)
+    n_h.wait_recv()
+    n_f = wire.send(m.at[other], m.at[other], p.C)
+    out(other, 2)
+    n_f.wait_recv()
+    out(last, 3)
+    for copy in moved:
         copy.wait_recv()
-    own.wait()
     wire.drain()
 
 
-def back_over_x(o):
+def branch_to_heads(n, w):
     return remote_call(
-        back_x_kernel, "back_over_x", 4, 3, 1, [ANY], [ANY], (shaped((4, 4, 128, 128)),)
-    )(o)[0]
-
-
-def go_x_kernel(o, d, ss, rs, ls):
-    p = Place()
-    own = local(o.at[p.x], d.at[:, p.x], ls, 0)
-    greet([p.XR, p.XL, p.XO])
-    wire = Wire(ss, rs)
-    for there, device in ((p.xo, p.XO), (p.xr, p.XR), (p.xl, p.XL)):
-        wire.send(o.at[there], d.at[:, p.x], device)
-    for copy in wire.started:
-        copy.wait_recv()
-    own.wait()
-    wire.drain()
-
-
-def go_over_x(o):
-    return remote_call(
-        go_x_kernel, "go_over_x", 5, 3, 1, [ANY], [ANY], (shaped((4, 4, 128, 128)),)
-    )(o)[0]
+        branch_kernel,
+        "branch_to_heads",
+        2,
+        15,
+        1,
+        [VMEM, VMEM],
+        [VMEM, VMEM],
+        (shaped((4, 128, 2048)), shaped((4, 4, 128, 128))),
+        scratch=[pltpu.VMEM((4, 4, 128, 128), bf16)],
+        vmem=32 << 20,
+    )(n, w)
 
 
 def grads_x_kernel(dq, dk, dv, three, ss, rs, ls, gk, gv, sk, sv):
@@ -1540,9 +1555,6 @@
     full_three = gathered.reshape(3, 2048, 512)
     normed_all = normed_all.reshape(512, width)
 
-    def by_head(flat):
-        return jnp.transpose(flat.reshape(512, 4, HD), (1, 0, 2))
-
     def flat_of(heads):
         return jnp.transpose(heads.reshape(4, 512, HD), (1, 0, 2)).reshape(512, 512)
 
@@ -1553,10 +1565,9 @@
     q, k, v = q.reshape(2048, HD), k.reshape(4096, HD), v.reshape(4096, HD)
     full_out = full_out.reshape(2048, 512)
     att_low, att, inverse = attend(limits, q, k, v, half_seg, half_ids, key_seg)
-    attended = back_over_x(att_low.reshape(runs))
+    attended, branch = attended_home(att_low.reshape(runs), full_out)
     attended_flat = flat_of(attended)
-    branch_part = jnp.einsum("qc,mc->qm", attended_flat, full_out, preferred_element_type=f32)
-    middle = inputs + sum_rows(branch_part.astype(bf16), 9)
+    middle = inputs + branch
     second_inv = rms_rows(middle)
     normed_ffn = (middle * second_inv * ffn_gain).astype(bf16)
     logits = jnp.dot(normed_ffn, router, preferred_element_type=f32)
@@ -1628,11 +1639,8 @@
     ffn_gain_term = jnp.sum(grad_ffn * middle * second_inv, axis=0)
     grad_middle = grad_out + rms_back(middle, second_inv, grad_ffn * ffn_gain)
     grad_branch = grad_middle.astype(bf16)
-    branch_all = gather_rows(grad_branch).reshape(512, width)
-    grad_att = by_head(
-        jnp.dot(branch_all, full_out, preferred_element_type=f32).astype(bf16)
-    )
-    grad_att = go_over_x(grad_att.reshape(runs)).reshape(2048, HD)
+    branch_all, grad_att = branch_to_heads(grad_branch, full_out)
+    branch_all, grad_att = branch_all.reshape(512, width), grad_att.reshape(2048, HD)
     delta = jnp.sum(grad_att.astype(f32) * att, axis=-1)
     dq, dk, dv = attend_back(
         limits, q, k, v, grad_att, half_seg, half_ids, key_seg, inverse[:, 0], delta

time: 731 us -> 714 us (0.977)
  matrix products: 13.1 us -> 5.68 us
    dot_general x2 -> x0, matrix products: 7.46 us -> none  [the longest x1 4.36 us: on_device(): jnp.dot(branch_all, full_out, preferred_element_type=f32).astype(bf16)]
    pallas_call x4 -> x2, Pallas kernels: 50 us -> 45.6 us  [the longest x1 25.2 us: attended_home(): remote_call(attended_kernel, 'attended_home', 4, 15, 1, [VMEM, VMEM], [VM...]
  transfers between devices with their start and end apart: 4 -> 4, of which waited for: 0 -> 0; matrix products, arithmetic and copies ran while one was open for 9% -> 8% of each run, Pallas kernels for 66% -> 67%
where the time goes in v6:
time: 714 us; the launch traced here: 709 us
  Pallas kernels  627 us (88%)
  local copies, waits for them, and re-layouts  40.8 us (6%)
  other arithmetic  20 us (3%)
  between operations  14.8 us (2%)
    pallas_call x1, Pallas kernels, last_sums(): remote_call(last_kernel, 'last_sums', 8, 64, 1, [VMEM] * 10, [VMEM] * 4,...  95.8 us
    pallas_call x1, Pallas kernels, gather_weights(): remote_call(weights_kernel, 'gather_weights', 1, 24, 3, [ANY] * 3, [ANY]...  73.7 us
    pallas_call x1, Pallas kernels, expert_backward(): remote_call(backward_kernel, 'expert_backward', cid, HOME_SENDS, 2, [VMEM...  72.1 us
    pallas_call x1, Pallas kernels, spread(): remote_call(spread_kernel, 'spread', cid, SPREAD_SENDS, 1, [ANY], [ANY],...  67.1 us
    pallas_call x1, Pallas kernels, expert_finish(): remote_call(finish_kernel, 'expert_finish', cid, HOME_SENDS, 4, [VMEM, VM...  67 us
    pallas_call x1, Pallas kernels, expert_forward(): remote_call(forward_kernel, 'expert_forward', cid, SPREAD_SENDS, 1, [ANY]...  56.4 us
    pallas_call x1, Pallas kernels, heads_over_x(): remote_call(heads_kernel, 'heads_over_x', 3, 22, 4, [ANY] * 2, [ANY] * 4,...  38.4 us
    pallas_call x1, Pallas kernels, grads_over_x(): remote_call(grads_x_kernel, 'grads_over_x', 6, 17, 1, [ANY, VMEM, VMEM],...  29.5 us
  transfers between devices with their start and end apart: 4, of which 0 were waited for; matrix products, arithmetic and copies ran while one was open for 8% of the time, Pallas kernels for 67%

profile of v6, /device:TPU:0, one launch (start us, length us, event | category | flops | bytes accessed | tf_op | source)
XLA Modules:
  0.0 708.6 jit_solution(11387677627764974614)
XLA Ops:
  7.2 3.5 copy.100
  10.8 6.1 copy.99
  23.1 73.7 %gather_weights.1 = (bf16[3,4,2,4,64,512]{5,4,3,2,1,0:T(8,128)(2,1)}, bf16[4,64,512]{2,1,0:T(8,128)(2,1)}, bf16[4,128,2048]{2,1,0:T(8,128)(2,1)}) custom-call(bf16[3,64,512]{2,1,0:T(8,128)(2,1)} %pad_maximum_fusion.3.w, bf16[64,512]{1,0:T(8,128)(2,1)} %wo.1, bf16[128,2048]{1,0:T(8,128)(2,1)} %get-tuple-element.160.n), custom_call_target="tpu_custom_call" | custom-call | tf_op jit(solution)/shard_map/gather_weights/pallas_call | solution.py:227
  99.6 10.0 %project.1 = (bf16[3,4,512,128]{3,2,1,0:T(8,128)(2,1)}, f32[2,4,512,128]{3,2,1,0:T(8,128)}) custom-call(bf16[512,2048]{1,0:T(8,128)(2,1)} %bitcast.139, bf16[3,2048,512]{2,1,0:T(8,128)(2,1)} %bitcast.130, f32[512,128]{1,0:T(8,128)} %get-tuple-element.179.cosine, f32[512,128]{1,0:T(8,128)} %get-tuple-element.180.sine, f32[2,1,128]{2,1,0:T(1,128)} %bitcast.155), custom_call_target="tpu_custom_call" | custom-call | tf_op jit(solution)/shard_map/project/pallas_call | solution.py:515
  109.6 38.4 %heads_over_x.1 = (bf16[4,4,128,128]{3,2,1,0:T(8,128)(2,1)}, bf16[4,2,4,128,128]{4,3,2,1,0:T(8,128)(2,1)}, bf16[4,2,4,128,128]{4,3,2,1,0:T(8,128)(2,1)}, bf16[4,2,4,64,512]{4,3,2,1,0:T(8,128)(2,1)}) custom-call(bf16[3,4,4,128,128]{4,3,2,1,0:T(8,128)(2,1)} %bitcast.143, bf16[4,64,512]{2,1,0:T(8,128)(2,1)} %get-tuple-element.54.go), custom_call_target="tpu_custom_call" | custom-call | tf_op jit(solution)/shard_map/heads_over_x/pallas_call | solution.py:284
  153.5 14.0 %attend.1 = (bf16[2048,128]{1,0:T(8,128)(2,1)S(1)}, f32[2048,128]{1,0:T(8,128)S(1)}, f32[2048,128]{1,0:T(8,128)S(1)}) custom-call(s32[2,8]{1,0:T(2,128)S(1)} %pad_add_fusion.lim, bf16[2048,128]{1,0:T(8,128)(2,1)S(1)} %bitcast.112, bf16[4096,128]{1,0:T(8,128)(2,1)S(1)} %bitcast.107, bf16[4096,128]{1,0:T(8,128)(2,1)S(1)} %bitcast.109, ...), custom_call_target="tpu_custom_call" | custom-call | tf_op jit(solution)/shard_map/attend/pallas_call | solution.py:580
  168.5 25.2 %attended_home.1 = (bf16[4,4,128,128]{3,2,1,0:T(8,128)(2,1)S(1)}, f32[128,2048]{1,0:T(8,128)S(1)}) custom-call(bf16[4,4,128,128]{3,2,1,0:T(8,128)(2,1)S(1)} %bitcast.116, bf16[2048,512]{1,0:T(8,128)(2,1)S(1)} %bitcast.102), custom_call_target="tpu_custom_call" | custom-call | tf_op jit(solution)/shard_map/attended_home/pallas_call | solution.py:360
  196.8 67.1 %spread.1 = bf16[2,2,2,4,128,2176]{5,4,3,2,1,0:T(8,128)(2,1)} custom-call(bf16[128,2176]{1,0:T(8,128)(2,1)} %concatenate.25.src), custom_call_target="tpu_custom_call" | custom-call | tf_op jit(solution)/shard_map/spread/pallas_call | solution.py:735
  263.9 2.3 slice.80.info
  266.9 13.4 %pick_rows.2 = (bf16[2,16,48,2048]{3,2,1,0:T(8,128)(2,1)}, f32[2,16,48,128]{3,2,1,0:T(8,128)}) custom-call(bf16[8,128]{1,0:T(8,128)(2,1)} %fusion.15.sel, bf16[4096,128]{1,0:T(8,128)(2,1)} %bitcast.128, bf16[4096,2176]{1,0:T(8,128)(2,1)} %bitcast.127), custom_call_target="tpu_custom_call" | custom-call | tf_op jit(solution)/shard_map/pick_rows/pallas_call | solution.py:874
  280.9 56.4 %expert_forward.1 = (bf16[2,2,2,4,128,2048]{5,4,3,2,1,0:T(8,128)(2,1)}, bf16[2,768,1024]{2,1,0:T(8,128)(2,1)S(1)}, bf16[2,768,1024]{2,1,0:T(8,128)(2,1)}, bf16[2...) custom-call(bf16[128,2048]{1,0:T(8,128)(2,1)S(1)} %copy-done.3, bf16[2,768,2048]{2,1,0:T(8,128)(2,1)} %bitcast.132, ...), custom_call_target="tpu_custom_call" | custom-call | tf_op jit(solution)/shard_map/expert_forward/pallas_call | solution.py:817
  339.0 13.1 %pick_rows.3 = bf16[2,16,48,2048]{3,2,1,0:T(8,128)(2,1)} custom-call(bf16[8,128]{1,0:T(8,128)(2,1)} %fusion.15.sel, bf16[4096,128]{1,0:T(8,128)(2,1)} %bitcast.129, bf16[4096,2048]{1,0:T(8,128)(2,1)} %bitcast.136), custom_call_target="tpu_custom_call" | custom-call | tf_op jit(solution)/shard_map/pick_rows/pallas_call | solution.py:874
  352.1 72.1 %expert_backward.1 = (f32[128,2048]{1,0:T(8,128)}, f32[2,768,128]{2,1,0:T(8,128)}, bf16[2,768,1024]{2,1,0:T(8,128)(2,1)}, bf16[2,768,1024]{2,1,0:T(8,128)(2,1)},...) custom-call(bf16[8,128]{1,0:T(8,128)(2,1)} %fusion.13.sel, bf16[32,128,128]{2,1,0:T(8,128)(2,1)} %slice.80.info, ...), custom_call_target="tpu_custom_call" | custom-call | tf_op jit(solution)/shard_map/expert_backward/pallas_call | solution.py:1115
  427.2 67.0 %expert_finish.1 = (f32[128,2176]{1,0:T(8,128)}, bf16[2,2048,2048]{2,1,0:T(8,128)(2,1)}) custom-call(bf16[8,128]{1,0:T(8,128)(2,1)} %fusion.13.sel, bf16[32,128,128]{2,1,0:T(8,128)(2,1)} %slice.80.info, bf16[2,2,2,4,48,2048]{5,4,3,2,1,0:T(8,128)(2,1)} %bitcast.141, bf16[2,2,2,4,48,128]{5,4,3,2,1,0:T(8,128)(2,1)} %select_select_fusion.more, ...), custom_call_target="tpu_custom_call" | custom-call | tf_op jit(solution)/shard_map/expert_finish/pallas_call | solution.py:1163
  504.4 2.2 multiply_reduce_fusion
  507.1 20.4 %branch_to_heads.1 = (bf16[4,128,2048]{2,1,0:T(8,128)(2,1)S(1)}, bf16[4,4,128,128]{3,2,1,0:T(8,128)(2,1)S(1)}) custom-call(bf16[128,2048]{1,0:T(8,128)(2,1)S(1)} %fusion.25.n, bf16[2048,512]{1,0:T(8,128)(2,1)S(1)} %bitcast.103), custom_call_target="tpu_custom_call" | custom-call | tf_op jit(solution)/shard_map/branch_to_heads/pallas_call | solution.py:414
  528.0 17.8 %attend_back.1 = (bf16[2048,128]{1,0:T(8,128)(2,1)S(1)}, bf16[4096,128]{1,0:T(8,128)(2,1)S(1)}, bf16[4096,128]{1,0:T(8,128)(2,1)S(1)}) custom-call(s32[2,8]{1,0:T(2,128)S(1)} %pad_add_fusion.lim, bf16[2048,128]{1,0:T(8,128)(2,1)S(1)} %bitcast.113, bf16[4096,128]{1,0:T(8,128)(2,1)S(1)} %bitcast.108, bf16[4096,128]{1,0:T(8,128)(2,1)S(1)} %bitcast.110, ...), custom_call_target="tpu_custom_call" | custom-call | tf_op jit(solution)/shard_map/attend_back/pallas_call | solution.py:641
  545.8 29.5 %grads_over_x.1 = bf16[3,4,4,128,128]{4,3,2,1,0:T(8,128)(2,1)S(1)} custom-call(bf16[4,4,128,128]{3,2,1,0:T(8,128)(2,1)S(1)} %bitcast.118, bf16[4,2,4,128,128]{4,3,2,1,0:T(8,128)(2,1)S(1)} %bitcast.114, bf16[4,2,4,128,128]{4,3,2,1,0:T(8,128)(2,1)S(1)} %bitcast.115), custom_call_target="tpu_custom_call" | custom-call | tf_op jit(solution)/shard_map/grads_over_x/pallas_call | solution.py:468
  577.5 2.6 convolution_convert_fusion
  580.1 95.8 %last_sums.1 = (f32[4,64,512]{2,1,0:T(8,128)}, f32[128,2048]{1,0:T(8,128)}, f32[4,2,4,40,128]{4,3,2,1,0:T(8,128)}, f32[24,128]{1,0:T(8,128)}) custom-call(bf16[3,4,512,128]{3,2,1,0:T(8,128)(2,1)} %bitcast.104, f32[2,4,512,128]{3,2,1,0:T(8,128)} %get-tuple-element.80.kept, bf16[3,2048,512]{2,1,0:T(8,128)(2,1)} %bitcast.131, bf16[512,2048]{1,0:T(8,128)(2,1)} %bitcast.140, ...), custom_call_target="tpu_custom_call" | custom-call | tf_op jit(solution)/shard_map/last_sums/pallas_call | solution.py:1454
  678.3 2.3 copy.88
  685.4 3.4 subtract_add_fusion
  688.8 5.7 unstack.3
  694.5 7.2 %unstack.2 = f32[512,2,2048]{2,1,0:T(2,128)} custom-call(bf16[2,512,2048]{2,1,0:T(8,128)(2,1)} %reduce-scatter.3.cloned.1.call-done.grads), custom_call_target="tpu_custom_call" | custom-call | tf_op jit(solution)/shard_map/unstack/pallas_call | solution.py:1203
  (164 shorter events, 44.4 us)
Async XLA Ops:
  7.2 273.7 %all-gather.5.cloned.1.call-start = ((), (), s32[]{:S(2)}) async-start(), calls=%async_computation.3 | async-start | bytes 10485760 | tf_op jit(solution)/shard_map/all_gather | solution.py:1531
  10.8 270.1 %all-gather.3.cloned.1.call-start = ((), (), s32[]{:S(2)}) async-start(), calls=%async_computation.2 | async-start | bytes 20971520 | tf_op jit(solution)/shard_map/all_gather | solution.py:1530
  16.9 80.0 %copy-start.38 = (f32[128]{0:T(128)S(1)}, f32[128]{0:T(128)}, u32[]{:S(2)}) copy-start(f32[128]{0:T(128)} %param.26) | copy-start | bytes 1540
  17.0 80.0 %copy-start.39 = (f32[128]{0:T(128)S(1)}, f32[128]{0:T(128)}, u32[]{:S(2)}) copy-start(f32[128]{0:T(128)} %param.25) | copy-start | bytes 1540
  17.0 671.8 %reduce-scatter.5.cloned.1.call-start = ((), (), s32[]{:S(2)}) async-start(), calls=%async_computation.5 | async-start | bytes 10485760 | tf_op jit(solution)/shard_map/reduce_scatter | solution.py:1620
  148.1 20.5 %copy-start = (bf16[4,2,4,64,512]{4,3,2,1,0:T(8,128)(2,1)S(1)}, bf16[4,2,4,64,512]{4,3,2,1,0:T(8,128)(2,1)}, u32[]{:S(2)}) copy-start(bf16[4,2,4,64,512]{4,3,2,1,0:T(8,128)(2,1)} %get-tuple-element.59) | copy-start | bytes 6291460
  153.5 40.3 %copy-start.19 = (bf16[128,2048]{1,0:T(8,128)(2,1)S(1)}, bf16[128,2048]{1,0:T(8,128)(2,1)}, u32[]{:S(2)}) copy-start(bf16[128,2048]{1,0:T(8,128)(2,1)} %param.16) | copy-start | bytes 1572868
  168.5 25.6 %copy-start.14 = (f32[2048,128]{1,0:T(8,128)}, f32[2048,128]{1,0:T(8,128)S(1)}, u32[]{:S(2)}) copy-start(f32[2048,128]{1,0:T(8,128)S(1)} %get-tuple-element.75) | copy-start | bytes 3145732
  168.5 25.5 %copy-start.29 = (f32[2048]{0:T(1024)S(1)}, f32[2048]{0:T(1024)}, u32[]{:S(2)}) copy-start(f32[2048]{0:T(1024)} %param.27) | copy-start | bytes 24580
  168.5 25.6 %copy-start.25 = (bf16[2048,64]{0,1:T(8,128)(2,1)S(1)}, bf16[2048,64]{0,1:T(8,128)(2,1)}, u32[]{:S(2)}) copy-start(bf16[2048,64]{0,1:T(8,128)(2,1)} %param.28) | copy-start | bytes 786436
  194.2 69.7 %copy-start.22 = (bf16[128,2048]{1,0:T(8,128)(2,1)}, bf16[128,2048]{1,0:T(8,128)(2,1)S(1)}, u32[]{:S(2)}) copy-start(bf16[128,2048]{1,0:T(8,128)(2,1)S(1)} %multiply_convert_fusion) | copy-start | bytes 1572868
  266.9 14.0 %copy-start.3 = (bf16[128,2048]{1,0:T(8,128)(2,1)S(1)}, bf16[128,2048]{1,0:T(8,128)(2,1)}, u32[]{:S(2)}) copy-start(bf16[128,2048]{1,0:T(8,128)(2,1)} %src.1) | copy-start | bytes 1572868
  424.3 270.2 %reduce-scatter.3.cloned.1.call-start = ((), (), s32[]{:S(2)}) async-start(), calls=%async_computation.4 | async-start | bytes 20971520 | tf_op jit(solution)/shard_map/reduce_scatter | solution.py:1620
  495.2 5.9 copy-start.23
  506.6 21.3 %copy-start.21 = (f32[128,2048]{1,0:T(8,128)}, f32[128,2048]{1,0:T(8,128)S(1)}, u32[]{:S(2)}) copy-start(f32[128,2048]{1,0:T(8,128)S(1)} %get-tuple-element.176) | copy-start | bytes 3145732
  506.6 21.0 %copy-start.13 = (f32[2048,128]{1,0:T(8,128)S(1)}, f32[2048,128]{1,0:T(8,128)}, u32[]{:S(2)}) copy-start(f32[2048,128]{1,0:T(8,128)} %copy-done.12) | copy-start | bytes 3145732
  506.7 21.3 %copy-start.1 = (s32[4096,1]{1,0:T(8,128)S(1)}, s32[4096,1]{1,0:T(8,128)}, u32[]{:S(2)}) copy-start(s32[4096,1]{1,0:T(8,128)} %copy.85.kseg) | copy-start | bytes 49156
  506.7 21.3 %copy-start.6 = (bf16[4,2,4,128,128]{4,3,2,1,0:T(8,128)(2,1)S(1)}, bf16[4,2,4,128,128]{4,3,2,1,0:T(8,128)(2,1)}, u32[]{:S(2)}) copy-start(bf16[4,2,4,128,128]{4,3,2,1,0:T(8,128)(2,1)} %get-tuple-element.56) | copy-start | bytes 3145732
  506.7 21.3 %copy-start.8 = (bf16[4,2,4,128,128]{4,3,2,1,0:T(8,128)(2,1)S(1)}, bf16[4,2,4,128,128]{4,3,2,1,0:T(8,128)(2,1)}, u32[]{:S(2)}) copy-start(bf16[4,2,4,128,128]{4,3,2,1,0:T(8,128)(2,1)} %get-tuple-element.57) | copy-start | bytes 3145732
  506.7 21.3 %copy-start.11 = (bf16[4,4,128,128]{3,2,1,0:T(8,128)(2,1)S(1)}, bf16[4,4,128,128]{3,2,1,0:T(8,128)(2,1)}, u32[]{:S(2)}) copy-start(bf16[4,4,128,128]{3,2,1,0:T(8,128)(2,1)} %get-tuple-element.55) | copy-start | bytes 1572868
  545.8 31.7 %copy-start.27 = (bf16[4,512,128]{1,2,0:T(8,128)(2,1)S(1)}, bf16[4,512,128]{1,2,0:T(8,128)(2,1)}, u32[]{:S(2)}) copy-start(bf16[4,512,128]{1,2,0:T(8,128)(2,1)} %copy.86) | copy-start | bytes 1572868
  675.9 6.3 copy-start.36
  675.9 8.7 %copy-start.28 = (f32[4,64,512]{2,1,0:T(8,128)S(1)}, f32[4,64,512]{2,1,0:T(8,128)}, u32[]{:S(2)}) copy-start(f32[4,64,512]{2,1,0:T(8,128)} %get-tuple-element.85) | copy-start | bytes 1572868
  677.1 8.3 %copy-start.17 = (f32[128,2048]{1,0:T(8,128)S(1)}, f32[128,2048]{1,0:T(8,128)}, u32[]{:S(2)}) copy-start(f32[128,2048]{1,0:T(8,128)} %copy-done.15) | copy-start | bytes 3145732
  (20 other events, 49.1 us)
Sparse Core Ops, SparseCore 0:
  10.9 94.8 all-gather.4
  108.0 153.0 all-gather.2
  424.4 77.0 reduce-scatter.4
  503.8 162.1 reduce-scatter.2

commit v7 on v6

--- a/solution.py
+++ b/solution.py
@@ -1174,42 +1174,52 @@
     )(sel, info, by_place(drows), by_place(more), rows, dgate, dup)
 
 
-def unstack_kernel(grads, out, held, sems):
+def unstack_kernel(first, second, first_out, second_out, held, held_two, sems):
     e, j, steps = pl.program_id(0), pl.program_id(1), pl.num_programs(1)
     step = e * steps + j
-    count = grads.shape[1]
-
-    def copy(at):
+    count = first.shape[1]
+
+    def copies(at):
         slot = lax.rem(at, 2)
         rows = pl.ds(pl.multiple_of(lax.rem(at, steps) * count, count), count)
-        return pltpu.make_async_copy(held.at[slot], out.at[rows, at // steps], sems.at[slot])
+        return [
+            pltpu.make_async_copy(buffer.at[slot], out.at[rows, at // steps], sems.at[i, slot])
+            for i, (buffer, out) in enumerate(((held, first_out), (held_two, second_out)))
+        ]
+
+    def wait(at):
+        for copy in copies(at):
+            copy.wait()
 
     @pl.when(step >= 2)
     def _():
-        copy(step - 2).wait()
-
-    held[lax.rem(step, 2)] = grads[0].astype(f32)
-    copy(step).start()
+        wait(step - 2)
+
+    held[lax.rem(step, 2)] = first[0].astype(f32)
+    held_two[lax.rem(step, 2)] = second[0].astype(f32)
+    for copy in copies(step):
+        copy.start()
 
     @pl.when(step == EXP_DEV * steps - 1)
     def _():
-        copy(step - 1).wait()
-        copy(step).wait()
-
-
-def unstack(grads):
-    experts, rows, cols = grads.shape
+        wait(step - 1)
+        wait(step)
+
+
+def unstack(first, second):
+    experts, rows = first.shape[:2]
     count = 128
+    wide = (first.shape[2], second.shape[2])
     return pl.pallas_call(
         unstack_kernel,
         name="unstack",
         grid=(experts, rows // count),
-        out_shape=shaped((rows, experts, cols), f32),
-        in_specs=[pl.BlockSpec((1, count, cols), lambda e, j: (e, j, 0))],
-        out_specs=ANY,
-        scratch_shapes=[pltpu.VMEM((2, count, cols), f32), DMA((2,))],
+        out_shape=tuple(shaped((rows, experts, cols), f32) for cols in wide),
+        in_specs=[pl.BlockSpec((1, count, cols), lambda e, j: (e, j, 0)) for cols in wide],
+        out_specs=[ANY, ANY],
+        scratch_shapes=[pltpu.VMEM((2, count, cols), f32) for cols in wide] + [DMA((2, 2))],
         compiler_params=pltpu.CompilerParams(vmem_limit_bytes=60 << 20),
-    )(grads)
+    )(first, second)
 
 
 def last_kernel(
@@ -1619,8 +1629,7 @@
     def fold_dp(term):
         return lax.psum_scatter(term.astype(bf16), "dp", scatter_dimension=1, tiled=True)
 
-    expert_out_grad = unstack(fold_dp(term_back))
-    expert_in_grad = unstack(fold_dp(term_in))
+    expert_in_grad, expert_out_grad = unstack(fold_dp(term_in), fold_dp(term_back))
 
     output = (middle + mixture).astype(bf16)
     grad_out = cotangent.astype(f32)

time: 714 us -> 709 us (level)
  no operation moved by 1% of the time
where the time goes in v7:
time: 709 us; the launch traced here: 703 us
  Pallas kernels  622 us (88%)
  local copies, waits for them, and re-layouts  40.9 us (6%)
  other arithmetic  20 us (3%)
  between operations  14.8 us (2%)
    pallas_call x1, Pallas kernels, last_sums(): remote_call(last_kernel, 'last_sums', 8, 64, 1, [VMEM] * 10, [VMEM] * 4,...  96.7 us
    pallas_call x1, Pallas kernels, gather_weights(): remote_call(weights_kernel, 'gather_weights', 1, 24, 3, [ANY] * 3, [ANY]...  73.7 us
    pallas_call x1, Pallas kernels, expert_backward(): remote_call(backward_kernel, 'expert_backward', cid, HOME_SENDS, 2, [VMEM...  72.1 us
    pallas_call x1, Pallas kernels, expert_finish(): remote_call(finish_kernel, 'expert_finish', cid, HOME_SENDS, 4, [VMEM, VM...  68.1 us
    pallas_call x1, Pallas kernels, spread(): remote_call(spread_kernel, 'spread', cid, SPREAD_SENDS, 1, [ANY], [ANY],...  64.7 us
    pallas_call x1, Pallas kernels, expert_forward(): remote_call(forward_kernel, 'expert_forward', cid, SPREAD_SENDS, 1, [ANY]...  56.2 us
    pallas_call x1, Pallas kernels, heads_over_x(): remote_call(heads_kernel, 'heads_over_x', 3, 22, 4, [ANY] * 2, [ANY] * 4,...  38.4 us
    pallas_call x1, Pallas kernels, grads_over_x(): remote_call(grads_x_kernel, 'grads_over_x', 6, 17, 1, [ANY, VMEM, VMEM],...  26.6 us
  transfers between devices with their start and end apart: 4, of which 0 were waited for; matrix products, arithmetic and copies ran while one was open for 8% of the time, Pallas kernels for 67%

profile of v7, /device:TPU:0, one launch (start us, length us, event | category | flops | bytes accessed | tf_op | source)
XLA Modules:
  0.0 703.5 jit_solution(13730395669481158803)
XLA Ops:
  7.2 3.5 copy.100
  10.8 6.1 copy.99
  23.1 73.7 %gather_weights.1 = (bf16[3,4,2,4,64,512]{5,4,3,2,1,0:T(8,128)(2,1)}, bf16[4,64,512]{2,1,0:T(8,128)(2,1)}, bf16[4,128,2048]{2,1,0:T(8,128)(2,1)}) custom-call(bf16[3,64,512]{2,1,0:T(8,128)(2,1)} %pad_maximum_fusion.3.w, bf16[64,512]{1,0:T(8,128)(2,1)} %wo.1, bf16[128,2048]{1,0:T(8,128)(2,1)} %get-tuple-element.164.n), custom_call_target="tpu_custom_call" | custom-call | tf_op jit(solution)/shard_map/gather_weights/pallas_call | solution.py:227
  99.6 10.0 %project.1 = (bf16[3,4,512,128]{3,2,1,0:T(8,128)(2,1)}, f32[2,4,512,128]{3,2,1,0:T(8,128)}) custom-call(bf16[512,2048]{1,0:T(8,128)(2,1)} %bitcast.139, bf16[3,2048,512]{2,1,0:T(8,128)(2,1)} %bitcast.130, f32[512,128]{1,0:T(8,128)} %get-tuple-element.183.cosine, f32[512,128]{1,0:T(8,128)} %get-tuple-element.184.sine, f32[2,1,128]{2,1,0:T(1,128)} %bitcast.155), custom_call_target="tpu_custom_call" | custom-call | tf_op jit(solution)/shard_map/project/pallas_call | solution.py:515
  109.6 38.4 %heads_over_x.1 = (bf16[4,4,128,128]{3,2,1,0:T(8,128)(2,1)}, bf16[4,2,4,128,128]{4,3,2,1,0:T(8,128)(2,1)}, bf16[4,2,4,128,128]{4,3,2,1,0:T(8,128)(2,1)}, bf16[4,2,4,64,512]{4,3,2,1,0:T(8,128)(2,1)}) custom-call(bf16[3,4,4,128,128]{4,3,2,1,0:T(8,128)(2,1)} %bitcast.143, bf16[4,64,512]{2,1,0:T(8,128)(2,1)} %get-tuple-element.56.go), custom_call_target="tpu_custom_call" | custom-call | tf_op jit(solution)/shard_map/heads_over_x/pallas_call | solution.py:284
  153.5 15.7 %attend.1 = (bf16[2048,128]{1,0:T(8,128)(2,1)S(1)}, f32[2048,128]{1,0:T(8,128)S(1)}, f32[2048,128]{1,0:T(8,128)S(1)}) custom-call(s32[2,8]{1,0:T(2,128)S(1)} %pad_add_fusion.lim, bf16[2048,128]{1,0:T(8,128)(2,1)S(1)} %bitcast.112, bf16[4096,128]{1,0:T(8,128)(2,1)S(1)} %bitcast.107, bf16[4096,128]{1,0:T(8,128)(2,1)S(1)} %bitcast.109, ...), custom_call_target="tpu_custom_call" | custom-call | tf_op jit(solution)/shard_map/attend/pallas_call | solution.py:580
  170.2 25.2 %attended_home.1 = (bf16[4,4,128,128]{3,2,1,0:T(8,128)(2,1)S(1)}, f32[128,2048]{1,0:T(8,128)S(1)}) custom-call(bf16[4,4,128,128]{3,2,1,0:T(8,128)(2,1)S(1)} %bitcast.116, bf16[2048,512]{1,0:T(8,128)(2,1)S(1)} %bitcast.102), custom_call_target="tpu_custom_call" | custom-call | tf_op jit(solution)/shard_map/attended_home/pallas_call | solution.py:360
  198.4 64.7 %spread.1 = bf16[2,2,2,4,128,2176]{5,4,3,2,1,0:T(8,128)(2,1)} custom-call(bf16[128,2176]{1,0:T(8,128)(2,1)} %concatenate.25.src), custom_call_target="tpu_custom_call" | custom-call | tf_op jit(solution)/shard_map/spread/pallas_call | solution.py:735
  263.1 2.3 slice.80.info
  266.1 13.4 %pick_rows.2 = (bf16[2,16,48,2048]{3,2,1,0:T(8,128)(2,1)}, f32[2,16,48,128]{3,2,1,0:T(8,128)}) custom-call(bf16[8,128]{1,0:T(8,128)(2,1)} %fusion.15.sel, bf16[4096,128]{1,0:T(8,128)(2,1)} %bitcast.128, bf16[4096,2176]{1,0:T(8,128)(2,1)} %bitcast.127), custom_call_target="tpu_custom_call" | custom-call | tf_op jit(solution)/shard_map/pick_rows/pallas_call | solution.py:874
  280.1 56.2 %expert_forward.1 = (bf16[2,2,2,4,128,2048]{5,4,3,2,1,0:T(8,128)(2,1)}, bf16[2,768,1024]{2,1,0:T(8,128)(2,1)S(1)}, bf16[2,768,1024]{2,1,0:T(8,128)(2,1)}, bf16[2...) custom-call(bf16[128,2048]{1,0:T(8,128)(2,1)S(1)} %copy-done.3, bf16[2,768,2048]{2,1,0:T(8,128)(2,1)} %bitcast.132, ...), custom_call_target="tpu_custom_call" | custom-call | tf_op jit(solution)/shard_map/expert_forward/pallas_call | solution.py:817
  338.0 13.1 %pick_rows.3 = bf16[2,16,48,2048]{3,2,1,0:T(8,128)(2,1)} custom-call(bf16[8,128]{1,0:T(8,128)(2,1)} %fusion.15.sel, bf16[4096,128]{1,0:T(8,128)(2,1)} %bitcast.129, bf16[4096,2048]{1,0:T(8,128)(2,1)} %bitcast.136), custom_call_target="tpu_custom_call" | custom-call | tf_op jit(solution)/shard_map/pick_rows/pallas_call | solution.py:874
  351.1 72.1 %expert_backward.1 = (f32[128,2048]{1,0:T(8,128)}, f32[2,768,128]{2,1,0:T(8,128)}, bf16[2,768,1024]{2,1,0:T(8,128)(2,1)}, bf16[2,768,1024]{2,1,0:T(8,128)(2,1)},...) custom-call(bf16[8,128]{1,0:T(8,128)(2,1)} %fusion.13.sel, bf16[32,128,128]{2,1,0:T(8,128)(2,1)} %slice.80.info, ...), custom_call_target="tpu_custom_call" | custom-call | tf_op jit(solution)/shard_map/expert_backward/pallas_call | solution.py:1115
  426.3 68.1 %expert_finish.1 = (f32[128,2176]{1,0:T(8,128)}, bf16[2,2048,2048]{2,1,0:T(8,128)(2,1)}) custom-call(bf16[8,128]{1,0:T(8,128)(2,1)} %fusion.13.sel, bf16[32,128,128]{2,1,0:T(8,128)(2,1)} %slice.80.info, bf16[2,2,2,4,48,2048]{5,4,3,2,1,0:T(8,128)(2,1)} %bitcast.141, bf16[2,2,2,4,48,128]{5,4,3,2,1,0:T(8,128)(2,1)} %select_select_fusion.more, ...), custom_call_target="tpu_custom_call" | custom-call | tf_op jit(solution)/shard_map/expert_finish/pallas_call | solution.py:1163
  495.5 2.0 copy.85.kseg
  504.7 2.2 multiply_reduce_fusion
  507.4 19.3 %branch_to_heads.1 = (bf16[4,128,2048]{2,1,0:T(8,128)(2,1)S(1)}, bf16[4,4,128,128]{3,2,1,0:T(8,128)(2,1)S(1)}) custom-call(bf16[128,2048]{1,0:T(8,128)(2,1)S(1)} %fusion.25.n, bf16[2048,512]{1,0:T(8,128)(2,1)S(1)} %bitcast.103), custom_call_target="tpu_custom_call" | custom-call | tf_op jit(solution)/shard_map/branch_to_heads/pallas_call | solution.py:414
  527.1 19.9 %attend_back.1 = (bf16[2048,128]{1,0:T(8,128)(2,1)S(1)}, bf16[4096,128]{1,0:T(8,128)(2,1)S(1)}, bf16[4096,128]{1,0:T(8,128)(2,1)S(1)}) custom-call(s32[2,8]{1,0:T(2,128)S(1)} %pad_add_fusion.lim, bf16[2048,128]{1,0:T(8,128)(2,1)S(1)} %bitcast.113, bf16[4096,128]{1,0:T(8,128)(2,1)S(1)} %bitcast.108, bf16[4096,128]{1,0:T(8,128)(2,1)S(1)} %bitcast.110, ...), custom_call_target="tpu_custom_call" | custom-call | tf_op jit(solution)/shard_map/attend_back/pallas_call | solution.py:641
  547.0 26.6 %grads_over_x.1 = bf16[3,4,4,128,128]{4,3,2,1,0:T(8,128)(2,1)S(1)} custom-call(bf16[4,4,128,128]{3,2,1,0:T(8,128)(2,1)S(1)} %bitcast.118, bf16[4,2,4,128,128]{4,3,2,1,0:T(8,128)(2,1)S(1)} %bitcast.114, bf16[4,2,4,128,128]{4,3,2,1,0:T(8,128)(2,1)S(1)} %bitcast.115), custom_call_target="tpu_custom_call" | custom-call | tf_op jit(solution)/shard_map/grads_over_x/pallas_call | solution.py:468
  575.7 2.6 convolution_convert_fusion
  578.3 96.7 %last_sums.1 = (f32[4,64,512]{2,1,0:T(8,128)}, f32[128,2048]{1,0:T(8,128)}, f32[4,2,4,40,128]{4,3,2,1,0:T(8,128)}, f32[24,128]{1,0:T(8,128)}) custom-call(bf16[3,4,512,128]{3,2,1,0:T(8,128)(2,1)} %bitcast.104, f32[2,4,512,128]{3,2,1,0:T(8,128)} %get-tuple-element.82.kept, bf16[3,2048,512]{2,1,0:T(8,128)(2,1)} %bitcast.131, bf16[512,2048]{1,0:T(8,128)(2,1)} %bitcast.140, ...), custom_call_target="tpu_custom_call" | custom-call | tf_op jit(solution)/shard_map/last_sums/pallas_call | solution.py:1464
  677.4 2.3 copy.88
  684.5 3.4 subtract_add_fusion
  687.9 8.8 %unstack.1 = (f32[512,2,2048]{2,1,0:T(2,128)}, f32[512,2,1024]{2,1,0:T(2,128)}) custom-call(bf16[2,512,2048]{2,1,0:T(8,128)(2,1)} %reduce-scatter.3.cloned.1.call-done.first, bf16[2,512,1024]{2,1,0:T(8,128)(2,1)} %reduce-scatter.5.cloned.1.call-done.second), custom_call_target="tpu_custom_call" | custom-call | tf_op jit(solution)/shard_map/unstack/pallas_call | solution.py:1213
  (163 shorter events, 42.4 us)
Async XLA Ops:
  7.2 272.9 %all-gather.5.cloned.1.call-start = ((), (), s32[]{:S(2)}) async-start(), calls=%async_computation.3 | async-start | bytes 10485760 | tf_op jit(solution)/shard_map/all_gather | solution.py:1541
  10.7 269.4 %all-gather.3.cloned.1.call-start = ((), (), s32[]{:S(2)}) async-start(), calls=%async_computation.2 | async-start | bytes 20971520 | tf_op jit(solution)/shard_map/all_gather | solution.py:1540
  16.9 80.0 %copy-start.38 = (f32[128]{0:T(128)S(1)}, f32[128]{0:T(128)}, u32[]{:S(2)}) copy-start(f32[128]{0:T(128)} %param.26) | copy-start | bytes 1540
  17.0 80.0 %copy-start.39 = (f32[128]{0:T(128)S(1)}, f32[128]{0:T(128)}, u32[]{:S(2)}) copy-start(f32[128]{0:T(128)} %param.25) | copy-start | bytes 1540
  17.0 670.9 %reduce-scatter.5.cloned.1.call-start = ((), (), s32[]{:S(2)}) async-start(), calls=%async_computation.5 | async-start | bytes 10485760 | tf_op jit(solution)/shard_map/reduce_scatter | solution.py:1630
  148.0 22.2 %copy-start = (bf16[4,2,4,64,512]{4,3,2,1,0:T(8,128)(2,1)S(1)}, bf16[4,2,4,64,512]{4,3,2,1,0:T(8,128)(2,1)}, u32[]{:S(2)}) copy-start(bf16[4,2,4,64,512]{4,3,2,1,0:T(8,128)(2,1)} %get-tuple-element.61) | copy-start | bytes 6291460
  153.5 42.0 %copy-start.19 = (bf16[128,2048]{1,0:T(8,128)(2,1)S(1)}, bf16[128,2048]{1,0:T(8,128)(2,1)}, u32[]{:S(2)}) copy-start(bf16[128,2048]{1,0:T(8,128)(2,1)} %param.16) | copy-start | bytes 1572868
  170.2 25.6 %copy-start.14 = (f32[2048,128]{1,0:T(8,128)}, f32[2048,128]{1,0:T(8,128)S(1)}, u32[]{:S(2)}) copy-start(f32[2048,128]{1,0:T(8,128)S(1)} %get-tuple-element.77) | copy-start | bytes 3145732
  170.2 25.5 %copy-start.29 = (f32[2048]{0:T(1024)S(1)}, f32[2048]{0:T(1024)}, u32[]{:S(2)}) copy-start(f32[2048]{0:T(1024)} %param.27) | copy-start | bytes 24580
  170.2 25.6 %copy-start.25 = (bf16[2048,64]{0,1:T(8,128)(2,1)S(1)}, bf16[2048,64]{0,1:T(8,128)(2,1)}, u32[]{:S(2)}) copy-start(bf16[2048,64]{0,1:T(8,128)(2,1)} %param.28) | copy-start | bytes 786436
  195.9 67.2 %copy-start.22 = (bf16[128,2048]{1,0:T(8,128)(2,1)}, bf16[128,2048]{1,0:T(8,128)(2,1)S(1)}, u32[]{:S(2)}) copy-start(bf16[128,2048]{1,0:T(8,128)(2,1)S(1)} %multiply_convert_fusion) | copy-start | bytes 1572868
  266.1 14.0 %copy-start.3 = (bf16[128,2048]{1,0:T(8,128)(2,1)S(1)}, bf16[128,2048]{1,0:T(8,128)(2,1)}, u32[]{:S(2)}) copy-start(bf16[128,2048]{1,0:T(8,128)(2,1)} %src.1) | copy-start | bytes 1572868
  423.3 264.6 %reduce-scatter.3.cloned.1.call-start = ((), (), s32[]{:S(2)}) async-start(), calls=%async_computation.4 | async-start | bytes 20971520 | tf_op jit(solution)/shard_map/reduce_scatter | solution.py:1630
  495.4 6.0 copy-start.23
  506.9 20.2 %copy-start.21 = (f32[128,2048]{1,0:T(8,128)}, f32[128,2048]{1,0:T(8,128)S(1)}, u32[]{:S(2)}) copy-start(f32[128,2048]{1,0:T(8,128)S(1)} %get-tuple-element.180) | copy-start | bytes 3145732
  506.9 19.8 %copy-start.13 = (f32[2048,128]{1,0:T(8,128)S(1)}, f32[2048,128]{1,0:T(8,128)}, u32[]{:S(2)}) copy-start(f32[2048,128]{1,0:T(8,128)} %copy-done.12) | copy-start | bytes 3145732
  506.9 20.2 %copy-start.1 = (s32[4096,1]{1,0:T(8,128)S(1)}, s32[4096,1]{1,0:T(8,128)}, u32[]{:S(2)}) copy-start(s32[4096,1]{1,0:T(8,128)} %copy.85.kseg) | copy-start | bytes 49156
  507.0 20.1 %copy-start.6 = (bf16[4,2,4,128,128]{4,3,2,1,0:T(8,128)(2,1)S(1)}, bf16[4,2,4,128,128]{4,3,2,1,0:T(8,128)(2,1)}, u32[]{:S(2)}) copy-start(bf16[4,2,4,128,128]{4,3,2,1,0:T(8,128)(2,1)} %get-tuple-element.58) | copy-start | bytes 3145732
  507.0 20.1 %copy-start.8 = (bf16[4,2,4,128,128]{4,3,2,1,0:T(8,128)(2,1)S(1)}, bf16[4,2,4,128,128]{4,3,2,1,0:T(8,128)(2,1)}, u32[]{:S(2)}) copy-start(bf16[4,2,4,128,128]{4,3,2,1,0:T(8,128)(2,1)} %get-tuple-element.59) | copy-start | bytes 3145732
  507.0 20.1 %copy-start.11 = (bf16[4,4,128,128]{3,2,1,0:T(8,128)(2,1)S(1)}, bf16[4,4,128,128]{3,2,1,0:T(8,128)(2,1)}, u32[]{:S(2)}) copy-start(bf16[4,4,128,128]{3,2,1,0:T(8,128)(2,1)} %get-tuple-element.57) | copy-start | bytes 1572868
  547.0 28.7 %copy-start.27 = (bf16[4,512,128]{1,2,0:T(8,128)(2,1)S(1)}, bf16[4,512,128]{1,2,0:T(8,128)(2,1)}, u32[]{:S(2)}) copy-start(bf16[4,512,128]{1,2,0:T(8,128)(2,1)} %copy.86) | copy-start | bytes 1572868
  675.0 6.3 copy-start.36
  675.0 8.7 %copy-start.28 = (f32[4,64,512]{2,1,0:T(8,128)S(1)}, f32[4,64,512]{2,1,0:T(8,128)}, u32[]{:S(2)}) copy-start(f32[4,64,512]{2,1,0:T(8,128)} %get-tuple-element.87) | copy-start | bytes 1572868
  676.2 8.3 %copy-start.17 = (f32[128,2048]{1,0:T(8,128)S(1)}, f32[128,2048]{1,0:T(8,128)}, u32[]{:S(2)}) copy-start(f32[128,2048]{1,0:T(8,128)} %copy-done.15) | copy-start | bytes 3145732
  (20 other events, 49.1 us)
Sparse Core Ops, SparseCore 0:
  10.9 94.8 all-gather.4
  108.0 153.0 all-gather.2
  423.4 77.0 reduce-scatter.4
  502.9 162.1 reduce-scatter.2
